TPU v7x, 32 devices: a whole 2x2x4 slice. The times are simulated.
32 devices in a mesh: dp: 4 (over z), seq: 8 (over y, x, core).
Axes of the slice: x: 2, y: 2, z: 4, core: 2. Of those that a mesh axis runs over, the one named last changes fastest.
Arguments:
- inputs: bfloat16 [1024, 8, 1024], P('seq', 'dp'), may hold values from -6 to 6
- memory: bfloat16 [512, 8, 1024], P('seq', 'dp'), may hold values from -6 to 6
- target_length: int32 [8], P('dp'), may hold values from 768 to 1024, as said below
- memory_length: int32 [8], P('dp'), may hold values from 256 to 512, as said below
- distance_bucket: int32 [1024], replicated, may hold values from 0 to 31, as said below
- bias_table: float32 [32, 16], replicated, may hold values from -3 to 3
- self_gain: float32 [1024], replicated, may hold values from 0.5 to 1.5
- self_query: bfloat16 [1024, 1024], replicated, may hold values from -0.1875 to 0.1875
- self_key: bfloat16 [1024, 512], replicated, may hold values from -0.1875 to 0.1875
- self_value: bfloat16 [1024, 512], replicated, may hold values from -0.1875 to 0.1875
- self_out: bfloat16 [1024, 1024], replicated, may hold values from -4 to 4
- cross_gain: float32 [1024], replicated, may hold values from 0.5 to 1.5
- cross_query: bfloat16 [1024, 1024], replicated, may hold values from -0.1875 to 0.1875
- cross_key: bfloat16 [1024, 512], replicated, may hold values from -0.1875 to 0.1875
- cross_value: bfloat16 [1024, 512], replicated, may hold values from -0.1875 to 0.1875
- cross_out: bfloat16 [1024, 1024], replicated, may hold values from -3 to 3
- feed_gain: float32 [1024], replicated, may hold values from 0.5 to 1.5
- gate_weight: bfloat16 [1024, 2816], replicated, may hold values from -0.1875 to 0.1875
- up_weight: bfloat16 [1024, 2816], replicated, may hold values from -0.1875 to 0.1875
- down_weight: bfloat16 [2816, 1024], replicated, may hold values from -0.109375 to 0.109375
- upstream: bfloat16 [1024, 8, 1024], P('seq', 'dp'), may hold values from -6 to 6
Outputs:
- outputs: bfloat16 [1024, 8, 1024], P('seq', 'dp')
- input_grad: float32 [1024, 8, 1024], P('seq', 'dp')
- memory_grad: float32 [512, 8, 1024], P('seq', 'dp')
- self_gain_grad: float32 [1024], replicated
- self_query_grad: float32 [1024, 1024], P(('dp', 'seq'))
- self_key_grad: float32 [1024, 512], P(('dp', 'seq'))
- self_value_grad: float32 [1024, 512], P(('dp', 'seq'))
- self_out_grad: float32 [1024, 1024], P(('dp', 'seq'))
- bias_table_grad: float32 [32, 16], replicated
- cross_gain_grad: float32 [1024], replicated
- cross_query_grad: float32 [1024, 1024], P(('dp', 'seq'))
- cross_key_grad: float32 [1024, 512], P(('dp', 'seq'))
- cross_value_grad: float32 [1024, 512], P(('dp', 'seq'))
- cross_out_grad: float32 [1024, 1024], P(('dp', 'seq'))
- feed_gain_grad: float32 [1024], replicated
- gate_weight_grad: float32 [1024, 2816], P(('dp', 'seq'))
- up_weight_grad: float32 [1024, 2816], P(('dp', 'seq'))
- down_weight_grad: float32 [2816, 1024], P(('dp', 'seq'))
Inputs may be any that keep to these rules, and one draw needn't show every extreme that they name: `target_length`: in every aligned block of 2 sequences (one index of dp) one sequence has the full length 1024 and another exactly 768. `memory_length`: in every aligned block of 2 sequences one has all 512 encoder rows and another exactly 256. `distance_bucket`: never falls with the distance; 0 at distance 0 and 31 at distance 1024 - 1.
All inputs are finite; a program needn't handle non-finite values.
Results may differ from a plain program's by a relative error of at most 0.02.
Values may be sent and summed in bfloat16 or wider, within the bound.
No kernel may reach another device: no remote copies, remote signals or barrier semaphores. Data moves between devices by JAX's collectives and lax.ppermute only.
A program may use at most 320 MiB of HBM per device.

v0:
```python
import jax
import jax.numpy as jnp
from jax import lax
from jax.sharding import PartitionSpec as P

GROUPS = 8


epsilon = 1e-06
scale = 0.125
negative = -1e30
highest = lax.Precision.HIGHEST


def rms_norm(value, gain):
    return value * lax.rsqrt(jnp.mean(value * value, axis=-1, keepdims=True) + epsilon) * gain


def gating(gate, upper):
    return jax.nn.gelu(gate, approximate=True) * upper


def project(left, right):
    return jnp.einsum("tsd,de->tse", left, right, preferred_element_type=jnp.float32)


def weight_grad(left, right):
    return jnp.einsum("tsd,tse->de", left, right, preferred_element_type=jnp.float32)


def back_project(grad, right):
    return jnp.einsum("tse,de->tsd", grad, right, preferred_element_type=jnp.float32)


def pick(array, index):
    return lax.dynamic_index_in_dim(array, index, 1, keepdims=False)


def place(array, piece, index):
    return lax.dynamic_update_index_in_dim(array, piece, index, 1)


def split_heads(query, keys):
    width = keys.shape[1] // GROUPS
    heads = query.reshape(query.shape[0], GROUPS, -1, width)
    return (heads, keys.reshape(keys.shape[0], GROUPS, width))


def raw_scores(heads, keyset, extra, allowed):
    scores = scale * jnp.einsum("tgrd,lgd->grtl", heads, keyset, preferred_element_type=jnp.float32)
    if extra is not None:
        scores = scores + extra
    return jnp.where(allowed, scores, negative)


def attend(query, keys, values, extra, allowed):
    heads, keyset = split_heads(query, keys)
    valset = values.reshape(keyset.shape)
    scores = raw_scores(heads, keyset, extra, allowed)
    peak = jnp.max(scores, axis=-1, keepdims=True)
    raised = jnp.exp(scores - peak)
    total = jnp.sum(raised, axis=-1, keepdims=True)
    shares = (raised / total).astype(jnp.bfloat16)
    mixed = jnp.einsum("grtl,lgd->tgrd", shares, valset, preferred_element_type=jnp.float32)
    return (mixed.reshape(query.shape).astype(jnp.bfloat16), (peak + jnp.log(total))[..., 0])


def attend_back(query, keys, values, extra, allowed, logsum, upstream):
    heads, keyset = split_heads(query, keys)
    valset = values.reshape(keyset.shape)
    scores = raw_scores(heads, keyset, extra, allowed)
    shares = jnp.exp(scores - logsum[..., None])
    incoming = upstream.reshape(heads.shape)
    share_grad = jnp.einsum("tgrd,lgd->grtl", incoming, valset, preferred_element_type=jnp.float32)
    inner = jnp.sum(shares * share_grad, axis=-1, keepdims=True)
    score_grad = (shares * (share_grad - inner)).astype(jnp.bfloat16)
    query_grad = scale * jnp.einsum(
        "grtl,lgd->tgrd", score_grad, keyset, preferred_element_type=jnp.float32
    )
    key_grad = scale * jnp.einsum(
        "grtl,tgrd->lgd", score_grad, heads, preferred_element_type=jnp.float32
    )
    value_grad = jnp.einsum(
        "grtl,tgrd->lgd", shares.astype(jnp.bfloat16), incoming, preferred_element_type=jnp.float32
    )
    return (
        query_grad.reshape(query.shape).astype(jnp.bfloat16),
        key_grad.reshape(keys.shape),
        value_grad.reshape(keys.shape),
        score_grad,
    )


def per_device(
    inputs,
    memory,
    target_length,
    memory_length,
    distance_bucket,
    bias_table,
    self_gain,
    self_query,
    self_key,
    self_value,
    self_out,
    cross_gain,
    cross_query,
    cross_key,
    cross_value,
    cross_out,
    feed_gain,
    gate_weight,
    up_weight,
    down_weight,
    upstream,
):
    tokens, seqs, width = inputs.shape
    length = tokens * lax.axis_size("seq")
    buckets = bias_table.shape[0]
    head_cols = self_query.shape[1]
    group_cols = self_key.shape[1]
    hidden_cols = gate_weight.shape[1]
    positions = lax.axis_index("seq") * tokens + jnp.arange(tokens, dtype=jnp.int32)
    columns = jnp.arange(length, dtype=jnp.int32)
    live = positions[:, None] < target_length[None, :]
    causal = columns[None, :] <= positions[:, None]
    offset = jnp.clip(positions[:, None] - columns[None, :], 0, length - 1)
    bucket_ids = jnp.arange(buckets, dtype=jnp.int32)
    thresholds = jnp.sum((distance_bucket[None, :] < bucket_ids[:, None]).astype(jnp.int32), axis=1)
    pair_bucket = jnp.sum(
        (offset[None, :, :] >= thresholds[1:, None, None]).astype(jnp.int32), axis=0
    )
    bucket_match = bucket_ids[:, None, None] == pair_bucket[None, :, :]
    extra = jnp.einsum(
        "btl,bh->htl", bucket_match.astype(jnp.float32), bias_table, precision=highest
    ).reshape(GROUPS, -1, tokens, length)
    bucket_onehot = bucket_match.astype(jnp.bfloat16)
    inputs_float = inputs.astype(jnp.float32)
    normed_self = rms_norm(inputs_float, self_gain).astype(jnp.bfloat16)
    query = project(normed_self, self_query).astype(jnp.bfloat16)
    keys = project(normed_self, self_key).astype(jnp.bfloat16)
    values = project(normed_self, self_value).astype(jnp.bfloat16)
    all_keys, all_values = (
        lax.all_gather(keys, "seq", axis=0, tiled=True),
        lax.all_gather(values, "seq", axis=0, tiled=True),
    )
    memory_keys = project(memory, cross_key).astype(jnp.bfloat16)
    memory_values = project(memory, cross_value).astype(jnp.bfloat16)
    recall_keys, recall_values = (
        lax.all_gather(memory_keys, "seq", axis=0, tiled=True),
        lax.all_gather(memory_values, "seq", axis=0, tiled=True),
    )
    mem_rows = recall_keys.shape[0]
    reach = jnp.arange(mem_rows, dtype=jnp.int32)

    def self_allowed(index):
        return causal & (columns[None, :] < target_length[index])

    def cross_allowed(index):
        return jnp.broadcast_to(reach[None, :] < memory_length[index], (tokens, mem_rows))

    def self_forward(index, carry):
        mixed_all, logsum_all = carry
        mixed, logsum = attend(
            pick(query, index),
            pick(all_keys, index),
            pick(all_values, index),
            extra,
            self_allowed(index),
        )
        return (
            place(mixed_all, mixed, index),
            lax.dynamic_update_index_in_dim(logsum_all, logsum, index, 0),
        )

    self_mixed, self_logsum = lax.fori_loop(
        0,
        seqs,
        self_forward,
        (jnp.zeros(query.shape, jnp.bfloat16), jnp.zeros((seqs,) + extra.shape[:3], jnp.float32)),
    )
    first = inputs_float + project(self_mixed, self_out)
    normed_cross = rms_norm(first, cross_gain).astype(jnp.bfloat16)
    recall_query = project(normed_cross, cross_query).astype(jnp.bfloat16)

    def cross_forward(index, carry):
        mixed_all, logsum_all = carry
        mixed, logsum = attend(
            pick(recall_query, index),
            pick(recall_keys, index),
            pick(recall_values, index),
            None,
            cross_allowed(index),
        )
        return (
            place(mixed_all, mixed, index),
            lax.dynamic_update_index_in_dim(logsum_all, logsum, index, 0),
        )

    cross_mixed, cross_logsum = lax.fori_loop(
        0,
        seqs,
        cross_forward,
        (
            jnp.zeros(recall_query.shape, jnp.bfloat16),
            jnp.zeros((seqs,) + extra.shape[:3], jnp.float32),
        ),
    )
    second = first + project(cross_mixed, cross_out)
    normed_feed = rms_norm(second, feed_gain).astype(jnp.bfloat16)
    gate = project(normed_feed, gate_weight)
    upper = project(normed_feed, up_weight)
    hidden = gating(gate, upper).astype(jnp.bfloat16)
    result = second + project(hidden, down_weight)
    outputs = jnp.where(live[..., None], result, 0.0).astype(jnp.bfloat16)
    grad = jnp.where(live[..., None], upstream.astype(jnp.float32), 0.0)
    grad_low = grad.astype(jnp.bfloat16)
    down_grad = weight_grad(hidden, grad_low)
    hidden_grad = back_project(grad_low, down_weight)
    unused, gate_back = jax.vjp(gating, gate, upper)
    gate_grad, upper_grad = gate_back(hidden_grad)
    gate_grad = gate_grad.astype(jnp.bfloat16)
    upper_grad = upper_grad.astype(jnp.bfloat16)
    feed_weights_grad = weight_grad(normed_feed, jnp.concatenate([gate_grad, upper_grad], axis=-1))
    feed_in = back_project(gate_grad, gate_weight) + back_project(upper_grad, up_weight)
    unused, norm_back = jax.vjp(rms_norm, second, feed_gain)
    second_part, feed_gain_grad = norm_back(feed_in)
    second_grad = grad + second_part
    second_low = second_grad.astype(jnp.bfloat16)
    cross_out_grad = weight_grad(cross_mixed, second_low)
    cross_mixed_grad = back_project(second_low, cross_out).astype(jnp.bfloat16)

    def cross_backward(index, carry):
        query_all, key_all, value_all = carry
        query_grad, key_grad, value_grad, score_grad = attend_back(
            pick(recall_query, index),
            pick(recall_keys, index),
            pick(recall_values, index),
            None,
            cross_allowed(index),
            cross_logsum[index],
            pick(cross_mixed_grad, index),
        )
        return (
            place(query_all, query_grad, index),
            place(key_all, key_grad, index),
            place(value_all, value_grad, index),
        )

    recall_query_grad, recall_key_part, recall_value_part = lax.fori_loop(
        0,
        seqs,
        cross_backward,
        (
            jnp.zeros(recall_query.shape, jnp.bfloat16),
            jnp.zeros(recall_keys.shape, jnp.float32),
            jnp.zeros(recall_keys.shape, jnp.float32),
        ),
    )
    memory_key_grad, memory_value_grad = (
        lax.psum_scatter(
            recall_key_part.astype(jnp.bfloat16), "seq", scatter_dimension=0, tiled=True
        ).astype(jnp.float32),
        lax.psum_scatter(
            recall_value_part.astype(jnp.bfloat16), "seq", scatter_dimension=0, tiled=True
        ).astype(jnp.float32),
    )
    memory_key_low = memory_key_grad.astype(jnp.bfloat16)
    memory_value_low = memory_value_grad.astype(jnp.bfloat16)
    cross_kv_weights_grad = weight_grad(
        memory, jnp.concatenate([memory_key_low, memory_value_low], axis=-1)
    )
    memory_grad = back_project(memory_key_low, cross_key) + back_project(
        memory_value_low, cross_value
    )
    cross_query_grad = weight_grad(normed_cross, recall_query_grad)
    cross_in = back_project(recall_query_grad, cross_query)
    unused, norm_back = jax.vjp(rms_norm, first, cross_gain)
    first_part, cross_gain_grad = norm_back(cross_in)
    first_grad = second_grad + first_part
    first_low = first_grad.astype(jnp.bfloat16)
    self_out_grad = weight_grad(self_mixed, first_low)
    self_mixed_grad = back_project(first_low, self_out).astype(jnp.bfloat16)
    used_keys, used_values = (all_keys, all_values)

    def self_backward(index, carry):
        query_all, key_all, value_all, table_all = carry
        query_grad, key_grad, value_grad, score_grad = attend_back(
            pick(query, index),
            pick(used_keys, index),
            pick(used_values, index),
            extra,
            self_allowed(index),
            self_logsum[index],
            pick(self_mixed_grad, index),
        )
        table_all = table_all + jnp.einsum(
            "grtl,btl->grb", score_grad, bucket_onehot, preferred_element_type=jnp.float32
        )
        return (
            place(query_all, query_grad, index),
            place(key_all, key_grad, index),
            place(value_all, value_grad, index),
            table_all,
        )

    query_grad_all, key_part, value_part, table_all = lax.fori_loop(
        0,
        seqs,
        self_backward,
        (
            jnp.zeros(query.shape, jnp.bfloat16),
            jnp.zeros(used_keys.shape, jnp.float32),
            jnp.zeros(used_keys.shape, jnp.float32),
            jnp.zeros(extra.shape[:2] + (buckets,), jnp.float32),
        ),
    )
    key_local, value_local = (
        lax.psum_scatter(
            key_part.astype(jnp.bfloat16), "seq", scatter_dimension=0, tiled=True
        ).astype(jnp.float32),
        lax.psum_scatter(
            value_part.astype(jnp.bfloat16), "seq", scatter_dimension=0, tiled=True
        ).astype(jnp.float32),
    )
    key_low = key_local.astype(jnp.bfloat16)
    value_low = value_local.astype(jnp.bfloat16)
    self_weights_grad = weight_grad(
        normed_self, jnp.concatenate([query_grad_all, key_low, value_low], axis=-1)
    )
    self_in = (
        back_project(query_grad_all, self_query)
        + back_project(key_low, self_key)
        + back_project(value_low, self_value)
    )
    unused, norm_back = jax.vjp(rms_norm, inputs_float, self_gain)
    input_part, self_gain_grad = norm_back(self_in)
    input_grad = first_grad + input_part
    table_grad = table_all.reshape(-1, buckets).T
    gains = jnp.concatenate([self_gain_grad, cross_gain_grad, feed_gain_grad])
    gain_sum, table_sum = lax.psum((gains, table_grad), ("dp", "seq"))
    rows_block = jnp.concatenate(
        [self_weights_grad, cross_query_grad, cross_kv_weights_grad, feed_weights_grad], axis=1
    )
    out_block = jnp.concatenate([self_out_grad, cross_out_grad], axis=1)
    rows_part, out_part, down_part = (
        lax.psum_scatter(rows_block, ("dp", "seq"), scatter_dimension=0, tiled=True),
        lax.psum_scatter(out_block, ("dp", "seq"), scatter_dimension=0, tiled=True),
        lax.psum_scatter(down_grad, ("dp", "seq"), scatter_dimension=0, tiled=True),
    )
    cuts = [
        head_cols,
        group_cols,
        group_cols,
        head_cols,
        group_cols,
        group_cols,
        hidden_cols,
        hidden_cols,
    ]
    pieces = []
    start = 0
    for cut in cuts:
        pieces.append(rows_part[:, start : start + cut])
        start = start + cut
    return (
        outputs,
        input_grad,
        memory_grad,
        gain_sum[:width],
        pieces[0],
        pieces[1],
        pieces[2],
        out_part[:, :width],
        table_sum,
        gain_sum[width : 2 * width],
        pieces[3],
        pieces[4],
        pieces[5],
        out_part[:, width:],
        gain_sum[2 * width :],
        pieces[6],
        pieces[7],
        down_part,
    )


def solution(mesh):
    placed = (
        P("seq", "dp", None),
        P("seq", "dp", None),
        P("dp"),
        P("dp"),
        P(),
        P(),
        P(),
        P(),
        P(),
        P(),
        P(),
        P(),
        P(),
        P(),
        P(),
        P(),
        P(),
        P(),
        P(),
        P(),
        P("seq", "dp", None),
    )
    return jax.shard_map(
        per_device,
        mesh=mesh,
        in_specs=placed,
        out_specs=(
            P("seq", "dp", None),
            P("seq", "dp", None),
            P("seq", "dp", None),
            P(),
            P(("dp", "seq"), None),
            P(("dp", "seq"), None),
            P(("dp", "seq"), None),
            P(("dp", "seq"), None),
            P(),
            P(),
            P(("dp", "seq"), None),
            P(("dp", "seq"), None),
            P(("dp", "seq"), None),
            P(("dp", "seq"), None),
            P(),
            P(("dp", "seq"), None),
            P(("dp", "seq"), None),
            P(("dp", "seq"), None),
        ),
        check_vma=False,
    )
```

profile of v0, /device:TPU:0, one launch (start us, length us, event | category | flops | bytes accessed | tf_op | source)
XLA Modules:
  0.0 1171.7 jit_solution(12976857163496981924)
XLA Ops:
  7.3 2.4 convolution_convert_fusion.2
  9.8 2.3 convolution_convert_fusion.3
  13.4 2.6 convolution_convert_fusion
  16.1 2.4 convolution_convert_fusion.1
  18.8 2.4 fusion.124
  24.9 7.9 fusion.80
  32.8 8.8 copy.240
  41.7 5.9 fusion.68
  47.6 2.3 copy.167
  49.9 12.9 %all-gather.9.cloned.1.call-done = bf16[512,2,512]{2,0,1:T(8,128)(2,1)} async-done(((bf16[64,2,512]{2,0,1:T(8,128)(2,1)}), bf16[512,2,512]{2,0,1:T(8,128)(2,1)}) %all-gather.9.cloned.1.call-update) | async-done | bytes 1048592 | tf_op jit(solution)/shard_map/all_gather | solution.py:151
  62.8 2.3 copy.166
  65.0 28.1 %all-gather.7.cloned.1.call-done = bf16[1024,2,512]{2,0,1:T(8,128)(2,1)} async-done(((bf16[128,2,512]{2,0,1:T(8,128)(2,1)}), bf16[1024,2,512]{2,0,1:T(8,128)(2,1)}) %all-gather.7.cloned.1.call-update) | async-done | bytes 2097168 | tf_op jit(solution)/shard_map/all_gather | solution.py:144
  93.2 4.0 copy.160
  97.1 26.3 %all-gather.5.cloned.1.call-done = bf16[1024,2,512]{2,0,1:T(8,128)(2,1)} async-done(((bf16[128,2,512]{2,0,1:T(8,128)(2,1)}), bf16[1024,2,512]{2,0,1:T(8,128)(2,1)}) %all-gather.5.cloned.1.call-update) | async-done | bytes 2097168 | tf_op jit(solution)/shard_map/all_gather | solution.py:145
  123.4 4.0 copy.159
  127.5 24.2 %while.70 = (s32[]{:T(128)}, bf16[128,2,1024]{0,2,1:T(8,128)(2,1)S(1)}, f32[2,8,2,128]{3,2,1,0:T(2,128)S(1)}, bf16[1024,2,512]{0,2,1:T(8,128)(2,1)}, s32[2]{0:T(...) while((s32[]{:T(128)}, ...), condition=%wide.region_6.7_spmd.clone, body=%wide.region_3.6_spmd.clone.sunk | while | flops 556137472 | bytes 41749132 | solution.py:176
  129.9 1.7 constant_dynamic-slice_fusion.26
  131.6 5.1 fusion.286
  141.9 1.7 constant_dynamic-slice_fusion.26
  143.6 5.1 fusion.286
  152.5 2.7 multiply_reduce_fusion.5
  156.9 2.1 copy.168
  159.8 15.2 %while.71 = (s32[]{:T(128)}, bf16[128,2,1024]{0,2,1:T(8,128)(2,1)}, f32[2,8,2,128]{3,2,1,0:T(2,128)S(1)}, bf16[512,2,512]{0,2,1:T(8,128)(2,1)}, s32[2]{0:T(128)S...) while((s32[]{:T(128)}, bf16[128,2,1024]{0,2,1:T(8,128)(2,1)}, ...), condition=%wide.region_11.12_spmd.clone, body=%wide.region_8.11_spmd.clone.sunk | while | flops 281147904 | bytes 21563572 | solution.py:200
  175.0 2.6 multiply_reduce_fusion.4
  177.8 5.0 fusion.74
  182.9 7.6 fusion.87
  192.3 2.5 multiply_reduce_fusion
  198.7 49.9 %while.72 = (s32[]{:T(128)}, bf16[128,2,1024]{0,2,1:T(8,128)(2,1)}, bf16[512,2,512]{2,0,1:T(8,128)(2,1)}, bf16[512,2,512]{2,0,1:T(8,128)(2,1)}, bf16[512,2,512]{...) while((s32[]{:T(128)}, bf16[128,2,1024]{0,2,1:T(8,128)(2,1)}, ...), condition=%wide.region_16.17_spmd.clone, body=%wide.region_14.16_spmd.clone.sunk | while | flops 687602176 | bytes 78440688 | solution.py:250
  202.6 1.9 constant_dynamic-slice_fusion.32
  206.3 2.0 copy-done.5
  208.4 1.9 fusion.308
  211.6 4.1 fusion.305
  227.2 1.9 constant_dynamic-slice_fusion.32
  231.0 2.0 copy-done.5
  233.1 1.9 fusion.308
  236.3 4.1 fusion.305
  248.6 2.1 copy.181
  250.8 3.0 multiply_reduce_fusion.1
  256.7 87.1 %while.73 = (s32[]{:T(128)}, bf16[128,2,1024]{0,2,1:T(8,128)(2,1)}, bf16[1024,2,512]{2,0,1:T(8,128)(2,1)}, bf16[1024,2,512]{2,0,1:T(8,128)(2,1)}, f32[8,2,32]{2,...) while((s32[]{:T(128)}, bf16[128,2,1024]{0,2,1:T(8,128)(2,1)}, ...), condition=%wide.region_20.21_spmd.clone, body=%wide.region_18.20_spmd.clone.sunk | while | flops 1507328000 | bytes 165722976 | solution.py:307
  264.5 10.2 fusion.324
  274.8 7.0 fusion.325
  281.8 6.4 fusion.327
  290.2 5.0 fusion.328
  308.0 10.2 fusion.324
  318.2 7.1 fusion.325
  325.3 6.4 fusion.327
  333.7 5.0 fusion.328
  346.8 4.2 pad_maximum_fusion.1
  350.9 9.4 copy.238
  362.4 2.8 convolution_bitcast_fusion.7
  365.3 9.7 convolution_bitcast_fusion.1
  374.9 3.7 convolution_bitcast_fusion.6
  378.6 5.5 copy.192
  385.3 44.9 %reduce-scatter.12.cloned.1.call-done = bf16[128,2,512]{2,0,1:T(8,128)(2,1)} async-done(((bf16[1024,2,512]{2,0,1:T(8,128)(2,1)}), bf16[128,2,512]{2,0,1:T(8,128)(2,1)}) %reduce-scatter.12.cloned.1.call-update) | async-done | bytes 262160 | tf_op jit(solution)/shard_map/reduce_scatter | solution.py:322
  430.2 5.9 convolution_bitcast_fusion.3
  436.2 26.2 %pad_maximum_fusion = f32[1024,9728]{1,0:T(8,128)} fusion(f32[1024,5632]{1,0:T(8,128)} %convolution_bitcast_fusion.1, f32[1024,1024]{1,0:T(8,128)} %copy.192, f32[1024,1024]{1,0:T(8,128)S(1)} %copy-done.12, f32[1024,2048]{1,0:T(8,128)} %convolution_bitcast_fusion.3), kind=kLoop, calls=%fused_computation.99 | loop fusion | flops 29884416 | bytes 79691776 | tf_op jit(solution)/shard_map/concatenate | solution.py:342
  464.0 6.0 convolution_bitcast_fusion.2
  471.2 4.5 fusion.121
  481.8 1.8 copy.200
  483.6 42.2 %all-reduce = (f32[3072]{0:T(1024)S(1)}, f32[32,16]{0,1:T(8,128)}) all-reduce(f32[3072]{0:T(1024)S(1)} %pad_maximum_fusion.2, f32[32,16]{0,1:T(8,128)S(1)} %bitcast.483), channel_id=1, replica_groups=mesh['dp'=4,'seq'=8] {'dp','seq'}, use_global_device_ids=true, to_apply=%region_29.30 | all-reduce | flops 3584 | bytes 28672 | tf_op jit(solution)/shard_map/psum | solution.py:341
  526.4 55.1 %reduce-scatter.22.cloned.1.call-done = f32[32,2048]{1,0:T(8,128)} async-done(((f32[1024,2048]{1,0:T(8,128)}), f32[32,2048]{1,0:T(8,128)}) %reduce-scatter.22.cloned.1.call-update) | async-done | bytes 262160
  583.2 415.0 %reduce-scatter.18.cloned.1.call-done = f32[32,9728]{1,0:T(8,128)} async-done(((f32[1024,9728]{1,0:T(8,128)}), f32[32,9728]{1,0:T(8,128)}) %reduce-scatter.18.cloned.1.call-update) | async-done | bytes 1245200 | tf_op jit(solution)/shard_map/reduce_scatter | solution.py:347
  1001.5 2.0 fusion.186
  1003.5 161.4 %reduce-scatter.20.cloned.1.call-done = f32[88,1024]{1,0:T(8,128)} async-done(((f32[2816,1024]{1,0:T(8,128)}), f32[88,1024]{1,0:T(8,128)}) %reduce-scatter.20.cloned.1.call-update) | async-done | bytes 360464 | tf_op jit(solution)/shard_map/reduce_scatter | solution.py:349
  (349 shorter events, 121.7 us)
Async XLA Ops:
  7.2 148.0 %copy-start = (bf16[1024,1024]{1,0:T(8,128)(2,1)S(1)}, bf16[1024,1024]{1,0:T(8,128)(2,1)}, u32[]{:S(2)}) copy-start(bf16[1024,1024]{1,0:T(8,128)(2,1)} %param.41) | copy-start | bytes 6291460
  7.2 8.9 copy-start.19
  7.2 8.9 copy-start.55
  7.2 40.4 %all-gather.11.cloned.1.call-start = ((), (), s32[]{:S(2)}) async-start(), calls=%async_computation.10 | async-start | bytes 1179648 | tf_op jit(solution)/shard_map/all_gather | solution.py:150
  9.7 8.9 copy-start.68
  9.7 53.0 %all-gather.9.cloned.1.call-start = ((), (), s32[]{:S(2)}) async-start(), calls=%async_computation.9 | async-start | bytes 1179648 | tf_op jit(solution)/shard_map/all_gather | solution.py:151
  12.1 81.1 %all-gather.7.cloned.1.call-start = ((), (), s32[]{:S(2)}) async-start(), calls=%async_computation.8 | async-start | bytes 2359296 | tf_op jit(solution)/shard_map/all_gather | solution.py:144
  13.4 5.4 copy-start.65
  13.4 7.9 copy-start.61
  16.0 8.9 copy-start.67
  16.1 107.4 %all-gather.5.cloned.1.call-start = ((), (), s32[]{:S(2)}) async-start(), calls=%async_computation.7 | async-start | bytes 2359296 | tf_op jit(solution)/shard_map/all_gather | solution.py:145
  18.6 356.3 %reduce-scatter.16.cloned.1.call-start = ((), (), s32[]{:S(2)}) async-start(), calls=%async_computation.14 | async-start | bytes 1179648 | tf_op jit(solution)/shard_map/reduce_scatter | solution.py:264
  32.8 8.8 copy-start.74
  32.8 8.9 copy-start.41
  41.7 5.9 copy-start.70
  152.5 2.8 copy-start.57
  152.5 7.4 copy-start.73
  155.2 19.8 %copy-start.8 = (f32[128,2,1024]{2,0,1:T(8,128)}, f32[128,2,1024]{2,0,1:T(8,128)S(1)}, u32[]{:S(2)}) copy-start(f32[128,2,1024]{2,0,1:T(8,128)S(1)} %get-tuple-element.1180) | copy-start | bytes 3145732
  155.2 98.6 %copy-start.59 = (f32[128,2]{0,1:T(2,128)}, f32[128,2]{0,1:T(2,128)S(1)}, u32[]{:S(2)}) copy-start(f32[128,2]{0,1:T(2,128)S(1)} %fusion.174) | copy-start | bytes 3076
  177.6 17.2 %copy-start.22 = (f32[128,2,1024]{2,0,1:T(8,128)}, f32[128,2,1024]{2,0,1:T(8,128)S(1)}, u32[]{:S(2)}) copy-start(f32[128,2,1024]{2,0,1:T(8,128)S(1)} %get-tuple-element.1182) | copy-start | bytes 3145732
  177.6 5.2 copy-start.75
  177.8 5.0 copy-start.32
  177.8 12.7 %slice-start = ((s8[5767168]{0:T(1024)(128)(4,1)}), s8[4194304]{0:T(1024)(128)(4,1)S(1)}, s32[]{:S(2)}) async-start(s8[5767168]{0:T(1024)(128)(4,1)} %bitcast.479), calls=%async_computation.18 | async-start | bytes 8388608
  177.8 14.4 %slice-start.2 = ((s8[5767168]{0:T(1024)(128)(4,1)}), s8[4194304]{0:T(1024)(128)(4,1)S(1)}, s32[]{:S(2)}) async-start(s8[5767168]{0:T(1024)(128)(4,1)} %bitcast.484), calls=%async_computation.20 | async-start | bytes 8388608
  182.8 7.7 slice-start.1
  182.8 9.4 slice-start.3
  192.3 3.9 copy-start.24
  201.5 8.9 copy-start.11
  211.6 4.1 copy-start.6
  226.2 8.9 copy-start.11
  236.3 4.1 copy-start.6
  248.6 5.3 copy-start.9
  248.6 126.3 %reduce-scatter.14.cloned.1.call-start = ((), (), s32[]{:S(2)}) async-start(), calls=%async_computation.13 | async-start | bytes 1179648 | tf_op jit(solution)/shard_map/reduce_scatter | solution.py:261
  250.8 3.1 copy-start.14
  250.8 3.4 copy-start.25
  255.8 129.5 %reduce-scatter.10.cloned.1.call-start = ((), (), s32[]{:S(2)}) async-start(), calls=%async_computation.11 | async-start | bytes 2359296 | tf_op jit(solution)/shard_map/reduce_scatter | solution.py:319
  259.5 5.0 copy-start.7
  264.5 10.2 copy-start.2
  281.8 6.4 copy-start.3
  290.2 5.0 copy-start.4
  303.0 5.0 copy-start.7
  308.0 10.2 copy-start.2
  325.3 6.4 copy-start.3
  333.7 5.0 copy-start.4
  343.9 86.3 %reduce-scatter.12.cloned.1.call-start = ((), (), s32[]{:S(2)}) async-start(), calls=%async_computation.12 | async-start | bytes 2359296 | tf_op jit(solution)/shard_map/reduce_scatter | solution.py:322
  344.7 236.8 %reduce-scatter.22.cloned.1.call-start = ((), (), s32[]{:S(2)}) async-start(), calls=%async_computation.17 | async-start | bytes 8650752
  360.4 4.9 copy-start.33
  360.4 637.8 %reduce-scatter.18.cloned.1.call-start = ((), (), s32[]{:S(2)}) async-start(), calls=%async_computation.15 | async-start | bytes 41091072 | tf_op jit(solution)/shard_map/reduce_scatter | solution.py:347
  362.4 2.9 copy-start.46
  362.4 2.8 copy-start.48
  365.2 9.7 copy-start.38
  378.6 51.6 %copy-start.20 = (bf16[128,2,1024]{2,1,0:T(2,128)(2,1)S(1)}, bf16[128,2,1024]{2,1,0:T(2,128)(2,1)}, u32[]{:S(2)}) copy-start(bf16[128,2,1024]{2,1,0:T(2,128)(2,1)} %param.29) | copy-start | bytes 1572868
  378.6 51.6 %copy-start.40 = (bf16[128,2,1024]{2,0,1:T(8,128)(2,1)S(1)}, bf16[128,2,1024]{2,0,1:T(8,128)(2,1)}, u32[]{:S(2)}) copy-start(bf16[128,2,1024]{2,0,1:T(8,128)(2,1)} %copy.187) | copy-start | bytes 1572868
  378.6 51.6 %copy-start.56 = (f32[1024]{0:T(1024)S(1)}, f32[1024]{0:T(1024)}, u32[]{:S(2)}) copy-start(f32[1024]{0:T(1024)} %param.35) | copy-start | bytes 12292
  378.6 51.6 %copy-start.62 = (f32[128,2]{0,1:T(2,128)S(1)}, f32[128,2]{0,1:T(2,128)}, u32[]{:S(2)}) copy-start(f32[128,2]{0,1:T(2,128)} %copy-done.61) | copy-start | bytes 3076
  430.2 6.0 copy-start.12
  462.5 702.5 %reduce-scatter.20.cloned.1.call-start = ((), (), s32[]{:S(2)}) async-start(), calls=%async_computation.16 | async-start | bytes 11894784 | tf_op jit(solution)/shard_map/reduce_scatter | solution.py:349
  471.2 5.9 copy-start.39
  477.1 3.1 copy-start.51
  477.1 3.0 copy-start.52
  477.9 2.7 copy-start.49
  480.7 2.9 copy-start.64
  480.7 2.9 copy-start.69
  481.5 683.5 %copy-start.1 = (bf16[1024,1024]{1,0:T(8,128)(2,1)S(1)}, bf16[1024,1024]{1,0:T(8,128)(2,1)}, u32[]{:S(2)}) copy-start(bf16[1024,1024]{1,0:T(8,128)(2,1)} %param.41) | copy-start | bytes 6291460
  (36 other events, 65.9 us)
Sparse Core Ops, SparseCore 0:
  10.5 26.1 all-gather.10
  39.2 23.4 all-gather.8
  65.3 27.8 all-gather.6
  95.5 27.8 all-gather.4
  248.7 36.0 reduce-scatter.15
  287.9 35.9 reduce-scatter.13
  344.0 41.2 reduce-scatter.9
  388.9 41.2 reduce-scatter.11
  432.5 148.9 reduce-scatter.21
  583.6 414.5 reduce-scatter.17
  1001.1 163.7 reduce-scatter.19
where the time goes:
time: 1180 us; the launch traced here: 1170 us
  waiting for transfers between devices  746 us (63%)
  matrix products  182 us (15%)
  local copies, waits for them, and re-layouts  123 us (10%)
  other arithmetic  61.6 us (5%)
  blocking collectives  42.2 us (4%)
  between operations  15 us (1%)
    reduce_scatter x1, waiting for transfers between devices, per_device(): lax.psum_scatter(rows_block, ('dp', 'seq'), scatter_dimension=0, tiled=True)  415 us
    reduce_scatter x1, waiting for transfers between devices, per_device(): lax.psum_scatter(down_grad, ('dp', 'seq'), scatter_dimension=0, tiled=True)  161 us
    unnamed x12, waiting for transfers between devices  56 us
    unnamed x154, local copies, waits for them, and re-layouts  46.7 us
    reduce_scatter x1, waiting for transfers between devices, per_device(): lax.psum_scatter(value_part.astype(jnp.bfloat16), 'seq', scatter_dimensio...  44.9 us
    psum x1, blocking collectives, per_device(): gain_sum, table_sum = lax.psum((gains, table_grad), ('dp', 'seq'))  42.2 us
    dot_general x11, matrix products, project(): jnp.einsum('tsd,de->tse', left, right, preferred_element_type=jnp.float32)  36.2 us
    dot_general x8, matrix products, raw_scores(): jnp.einsum('tgrd,lgd->grtl', heads, keyset, preferred_element_type=jnp.fl...  34.3 us
  transfers between devices with their start and end apart: 11, of which 8 were waited for; matrix products, arithmetic and copies ran while one was open for 20% of the time, Pallas kernels for 0%

commit v1 on v0

--- a/solution.py
+++ b/solution.py
@@ -1,6 +1,7 @@
 import jax
 import jax.numpy as jnp
 from jax import lax
+from jax.experimental import pallas as pl
 from jax.sharding import PartitionSpec as P
 
 GROUPS = 8
@@ -10,6 +11,10 @@
 scale = 0.125
 negative = -1e30
 highest = lax.Precision.HIGHEST
+
+
+def copy_kernel(a_ref, b_ref):
+    b_ref[...] = a_ref[...]
 
 
 def rms_norm(value, gain):
@@ -337,6 +342,7 @@
     input_part, self_gain_grad = norm_back(self_in)
     input_grad = first_grad + input_part
     table_grad = table_all.reshape(-1, buckets).T
+    table_grad = pl.pallas_call(copy_kernel, out_shape=jax.ShapeDtypeStruct(table_grad.shape, jnp.float32))(table_grad)
     gains = jnp.concatenate([self_gain_grad, cross_gain_grad, feed_gain_grad])
     gain_sum, table_sum = lax.psum((gains, table_grad), ("dp", "seq"))
     rows_block = jnp.concatenate(

time: 1180 us -> 1180 us (level)
    unnamed x154 -> x153, local copies, waits for them, and re-layouts: 46.7 us -> 47.2 us
where the time goes in v1:
time: 1180 us; the launch traced here: 1170 us
  waiting for transfers between devices  741 us (63%)
  matrix products  185 us (16%)
  local copies, waits for them, and re-layouts  124 us (11%)
  other arithmetic  61.6 us (5%)
  blocking collectives  41.5 us (4%)
  between operations  15 us (1%)
    reduce_scatter x1, waiting for transfers between devices, per_device(): lax.psum_scatter(rows_block, ('dp', 'seq'), scatter_dimension=0, tiled=True)  415 us
    reduce_scatter x1, waiting for transfers between devices, per_device(): lax.psum_scatter(down_grad, ('dp', 'seq'), scatter_dimension=0, tiled=True)  162 us
    unnamed x12, waiting for transfers between devices  51.2 us
    unnamed x153, local copies, waits for them, and re-layouts  47.2 us
    reduce_scatter x1, waiting for transfers between devices, per_device(): lax.psum_scatter(value_part.astype(jnp.bfloat16), 'seq', scatter_dimensio...  44.9 us
    psum x1, blocking collectives, per_device(): gain_sum, table_sum = lax.psum((gains, table_grad), ('dp', 'seq'))  41.5 us
    dot_general x11, matrix products, project(): jnp.einsum('tsd,de->tse', left, right, preferred_element_type=jnp.float32)  36 us
    dot_general x8, matrix products, raw_scores(): jnp.einsum('tgrd,lgd->grtl', heads, keyset, preferred_element_type=jnp.fl...  34.3 us
  transfers between devices with their start and end apart: 11, of which 8 were waited for; matrix products, arithmetic and copies ran while one was open for 20% of the time, Pallas kernels for 0%

profile of v1, /device:TPU:0, one launch (start us, length us, event | category | flops | bytes accessed | tf_op | source)
XLA Modules:
  0.0 1172.0 jit_solution(16900762099300026027)
XLA Ops:
  7.3 2.4 convolution_convert_fusion.2
  9.8 2.3 convolution_convert_fusion.3
  13.4 2.6 convolution_convert_fusion
  16.1 2.4 convolution_convert_fusion.1
  18.8 2.4 fusion.124
  24.9 7.9 fusion.80
  32.9 8.8 copy.302
  41.7 5.9 fusion.68
  47.6 2.3 copy.227
  49.9 12.9 %all-gather.9.cloned.1.call-done = bf16[512,2,512]{2,0,1:T(8,128)(2,1)} async-done(((bf16[64,2,512]{2,0,1:T(8,128)(2,1)}), bf16[512,2,512]{2,0,1:T(8,128)(2,1)}) %all-gather.9.cloned.1.call-update) | async-done | bytes 1048592 | tf_op jit(solution)/shard_map/all_gather | solution.py:156
  62.8 2.3 copy.226
  65.0 28.1 %all-gather.7.cloned.1.call-done = bf16[1024,2,512]{2,0,1:T(8,128)(2,1)} async-done(((bf16[128,2,512]{2,0,1:T(8,128)(2,1)}), bf16[1024,2,512]{2,0,1:T(8,128)(2,1)}) %all-gather.7.cloned.1.call-update) | async-done | bytes 2097168 | tf_op jit(solution)/shard_map/all_gather | solution.py:149
  93.2 3.9 copy.220
  97.1 26.3 %all-gather.5.cloned.1.call-done = bf16[1024,2,512]{2,0,1:T(8,128)(2,1)} async-done(((bf16[128,2,512]{2,0,1:T(8,128)(2,1)}), bf16[1024,2,512]{2,0,1:T(8,128)(2,1)}) %all-gather.5.cloned.1.call-update) | async-done | bytes 2097168 | tf_op jit(solution)/shard_map/all_gather | solution.py:150
  123.4 4.0 copy.219
  127.5 24.2 %while.70 = (s32[]{:T(128)}, bf16[128,2,1024]{0,2,1:T(8,128)(2,1)S(1)}, f32[2,8,2,128]{3,2,1,0:T(2,128)S(1)}, bf16[1024,2,512]{0,2,1:T(8,128)(2,1)}, s32[2]{0:T(...) while((s32[]{:T(128)}, ...), condition=%wide.region_6.7_spmd.clone, body=%wide.region_3.6_spmd.clone.sunk | while | flops 556137472 | bytes 41749132 | solution.py:181
  131.6 5.1 fusion.286
  143.6 5.1 fusion.286
  152.5 2.7 multiply_reduce_fusion.5
  156.9 2.1 copy.228
  159.8 15.1 %while.71 = (s32[]{:T(128)}, bf16[128,2,1024]{0,2,1:T(8,128)(2,1)}, f32[2,8,2,128]{3,2,1,0:T(2,128)S(1)}, bf16[512,2,512]{0,2,1:T(8,128)(2,1)}, s32[2]{0:T(128)S...) while((s32[]{:T(128)}, bf16[128,2,1024]{0,2,1:T(8,128)(2,1)}, ...), condition=%wide.region_11.12_spmd.clone, body=%wide.region_8.11_spmd.clone.sunk | while | flops 281147904 | bytes 21563572 | solution.py:205
  175.0 2.6 multiply_reduce_fusion.4
  177.8 5.0 fusion.74
  182.8 7.6 fusion.87
  192.2 2.5 multiply_reduce_fusion
  198.6 49.9 %while.72 = (s32[]{:T(128)}, bf16[128,2,1024]{0,2,1:T(8,128)(2,1)}, bf16[512,2,512]{2,0,1:T(8,128)(2,1)}, bf16[512,2,512]{2,0,1:T(8,128)(2,1)}, bf16[512,2,512]{...) while((s32[]{:T(128)}, bf16[128,2,1024]{0,2,1:T(8,128)(2,1)}, ...), condition=%wide.region_16.17_spmd.clone, body=%wide.region_14.16_spmd.clone.sunk | while | flops 687602176 | bytes 78440688 | solution.py:255
  202.5 1.9 constant_dynamic-slice_fusion.32
  206.3 2.1 copy-done.5
  208.3 2.0 fusion.308
  211.6 4.1 fusion.305
  227.2 1.9 constant_dynamic-slice_fusion.32
  231.0 2.1 copy-done.5
  233.0 2.0 fusion.308
  236.3 4.1 fusion.305
  248.6 2.1 copy.241
  250.7 3.0 multiply_reduce_fusion.1
  256.7 87.1 %while.73 = (s32[]{:T(128)}, bf16[128,2,1024]{0,2,1:T(8,128)(2,1)}, bf16[1024,2,512]{2,0,1:T(8,128)(2,1)}, bf16[1024,2,512]{2,0,1:T(8,128)(2,1)}, f32[8,2,32]{2,...) while((s32[]{:T(128)}, bf16[128,2,1024]{0,2,1:T(8,128)(2,1)}, ...), condition=%wide.region_20.21_spmd.clone, body=%wide.region_18.20_spmd.clone.sunk | while | flops 1507328000 | bytes 165722976 | solution.py:312
  264.5 10.2 fusion.324
  274.7 7.0 fusion.325
  281.7 6.4 fusion.327
  290.2 5.0 fusion.328
  308.0 10.2 fusion.324
  318.2 7.1 fusion.325
  325.3 6.4 fusion.327
  333.7 5.0 fusion.328
  346.7 4.1 pad_maximum_fusion.1
  350.9 9.3 copy.300
  362.3 2.8 convolution_bitcast_fusion.7
  365.2 9.7 convolution_bitcast_fusion.1
  374.9 3.7 convolution_bitcast_fusion.6
  378.6 5.5 copy.252
  385.1 44.9 %reduce-scatter.12.cloned.1.call-done = bf16[128,2,512]{2,0,1:T(8,128)(2,1)} async-done(((bf16[1024,2,512]{2,0,1:T(8,128)(2,1)}), bf16[128,2,512]{2,0,1:T(8,128)(2,1)}) %reduce-scatter.12.cloned.1.call-update) | async-done | bytes 262160 | tf_op jit(solution)/shard_map/reduce_scatter | solution.py:327
  430.1 5.9 convolution_bitcast_fusion.3
  436.0 26.3 %pad_maximum_fusion = f32[1024,9728]{1,0:T(8,128)} fusion(f32[1024,5632]{1,0:T(8,128)} %convolution_bitcast_fusion.1, f32[1024,1024]{1,0:T(8,128)} %copy.252, f32[1024,1024]{1,0:T(8,128)S(1)} %copy-done.12, f32[1024,2048]{1,0:T(8,128)} %convolution_bitcast_fusion.3), kind=kLoop, calls=%fused_computation.99 | loop fusion | flops 29884416 | bytes 79691776 | tf_op jit(solution)/shard_map/concatenate | solution.py:348
  463.8 6.0 convolution_bitcast_fusion.2
  471.0 4.4 fusion.121
  478.8 2.4 fusion.103
  481.3 1.8 fusion.150
  486.5 1.8 copy.261
  488.3 41.5 %all-reduce = (f32[3072]{0:T(1024)S(1)}, f32[32,16]{1,0:T(8,128)S(1)}) all-reduce(f32[3072]{0:T(1024)S(1)} %pad_maximum_fusion.2, f32[32,16]{1,0:T(8,128)S(1)} %copy-done.55), channel_id=1, replica_groups=mesh['dp'=4,'seq'=8] {'dp','seq'}, use_global_device_ids=true, to_apply=%region_29.30 | all-reduce | flops 3584 | bytes 28672 | tf_op jit(solution)/shard_map/psum | solution.py:347
  531.1 50.3 %reduce-scatter.22.cloned.1.call-done = f32[32,2048]{1,0:T(8,128)} async-done(((f32[1024,2048]{1,0:T(8,128)}), f32[32,2048]{1,0:T(8,128)}) %reduce-scatter.22.cloned.1.call-update) | async-done | bytes 262160
  583.1 415.1 %reduce-scatter.18.cloned.1.call-done = f32[32,9728]{1,0:T(8,128)} async-done(((f32[1024,9728]{1,0:T(8,128)}), f32[32,9728]{1,0:T(8,128)}) %reduce-scatter.18.cloned.1.call-update) | async-done | bytes 1245200 | tf_op jit(solution)/shard_map/reduce_scatter | solution.py:353
  1001.6 2.0 fusion.186
  1003.6 161.7 %reduce-scatter.20.cloned.1.call-done = f32[88,1024]{1,0:T(8,128)} async-done(((f32[2816,1024]{1,0:T(8,128)}), f32[88,1024]{1,0:T(8,128)}) %reduce-scatter.20.cloned.1.call-update) | async-done | bytes 360464 | tf_op jit(solution)/shard_map/reduce_scatter | solution.py:355
  (350 shorter events, 126.5 us)
Async XLA Ops:
  7.2 148.0 %copy-start = (bf16[1024,1024]{1,0:T(8,128)(2,1)S(1)}, bf16[1024,1024]{1,0:T(8,128)(2,1)}, u32[]{:S(2)}) copy-start(bf16[1024,1024]{1,0:T(8,128)(2,1)} %param.41) | copy-start | bytes 6291460
  7.2 8.9 copy-start.19
  7.2 8.9 copy-start.53
  7.2 40.4 %all-gather.11.cloned.1.call-start = ((), (), s32[]{:S(2)}) async-start(), calls=%async_computation.10 | async-start | bytes 1179648 | tf_op jit(solution)/shard_map/all_gather | solution.py:155
  9.7 8.9 copy-start.67
  9.7 53.0 %all-gather.9.cloned.1.call-start = ((), (), s32[]{:S(2)}) async-start(), calls=%async_computation.9 | async-start | bytes 1179648 | tf_op jit(solution)/shard_map/all_gather | solution.py:156
  12.1 81.1 %all-gather.7.cloned.1.call-start = ((), (), s32[]{:S(2)}) async-start(), calls=%async_computation.8 | async-start | bytes 2359296 | tf_op jit(solution)/shard_map/all_gather | solution.py:149
  13.4 5.4 copy-start.64
  13.4 7.9 copy-start.60
  16.0 8.9 copy-start.66
  16.1 107.4 %all-gather.5.cloned.1.call-start = ((), (), s32[]{:S(2)}) async-start(), calls=%async_computation.7 | async-start | bytes 2359296 | tf_op jit(solution)/shard_map/all_gather | solution.py:150
  18.6 356.3 %reduce-scatter.16.cloned.1.call-start = ((), (), s32[]{:S(2)}) async-start(), calls=%async_computation.14 | async-start | bytes 1179648 | tf_op jit(solution)/shard_map/reduce_scatter | solution.py:269
  32.8 8.8 copy-start.73
  32.8 8.9 copy-start.39
  41.7 5.9 copy-start.69
  152.5 7.3 copy-start.72
  155.2 19.8 %copy-start.8 = (f32[128,2,1024]{2,0,1:T(8,128)}, f32[128,2,1024]{2,0,1:T(8,128)S(1)}, u32[]{:S(2)}) copy-start(f32[128,2,1024]{2,0,1:T(8,128)S(1)} %get-tuple-element.1238) | copy-start | bytes 3145732
  155.2 98.6 %copy-start.58 = (f32[128,2]{0,1:T(2,128)}, f32[128,2]{0,1:T(2,128)S(1)}, u32[]{:S(2)}) copy-start(f32[128,2]{0,1:T(2,128)S(1)} %fusion.174) | copy-start | bytes 3076
  177.6 17.2 %copy-start.22 = (f32[128,2,1024]{2,0,1:T(8,128)}, f32[128,2,1024]{2,0,1:T(8,128)S(1)}, u32[]{:S(2)}) copy-start(f32[128,2,1024]{2,0,1:T(8,128)S(1)} %get-tuple-element.1240) | copy-start | bytes 3145732
  177.6 5.2 copy-start.74
  177.8 5.0 copy-start.32
  177.8 12.7 %slice-start = ((s8[5767168]{0:T(1024)(128)(4,1)}), s8[4194304]{0:T(1024)(128)(4,1)S(1)}, s32[]{:S(2)}) async-start(s8[5767168]{0:T(1024)(128)(4,1)} %bitcast.478), calls=%async_computation.18 | async-start | bytes 8388608
  177.8 14.4 %slice-start.2 = ((s8[5767168]{0:T(1024)(128)(4,1)}), s8[4194304]{0:T(1024)(128)(4,1)S(1)}, s32[]{:S(2)}) async-start(s8[5767168]{0:T(1024)(128)(4,1)} %bitcast.484), calls=%async_computation.20 | async-start | bytes 8388608
  182.8 7.7 slice-start.1
  182.8 9.4 slice-start.3
  192.2 3.9 copy-start.24
  201.4 8.9 copy-start.11
  211.5 4.1 copy-start.6
  226.1 8.9 copy-start.11
  236.3 4.1 copy-start.6
  248.5 5.3 copy-start.9
  248.5 126.3 %reduce-scatter.14.cloned.1.call-start = ((), (), s32[]{:S(2)}) async-start(), calls=%async_computation.13 | async-start | bytes 1179648 | tf_op jit(solution)/shard_map/reduce_scatter | solution.py:266
  250.7 3.1 copy-start.14
  250.7 3.4 copy-start.25
  255.7 129.4 %reduce-scatter.10.cloned.1.call-start = ((), (), s32[]{:S(2)}) async-start(), calls=%async_computation.11 | async-start | bytes 2359296 | tf_op jit(solution)/shard_map/reduce_scatter | solution.py:324
  259.5 5.0 copy-start.7
  264.5 10.2 copy-start.2
  281.7 6.4 copy-start.3
  290.2 5.0 copy-start.4
  303.0 5.0 copy-start.7
  308.0 10.2 copy-start.2
  325.3 6.4 copy-start.3
  333.7 5.0 copy-start.4
  343.9 86.2 %reduce-scatter.12.cloned.1.call-start = ((), (), s32[]{:S(2)}) async-start(), calls=%async_computation.12 | async-start | bytes 2359296 | tf_op jit(solution)/shard_map/reduce_scatter | solution.py:327
  344.6 236.8 %reduce-scatter.22.cloned.1.call-start = ((), (), s32[]{:S(2)}) async-start(), calls=%async_computation.17 | async-start | bytes 8650752
  360.3 4.9 copy-start.33
  360.3 638.0 %reduce-scatter.18.cloned.1.call-start = ((), (), s32[]{:S(2)}) async-start(), calls=%async_computation.15 | async-start | bytes 41091072 | tf_op jit(solution)/shard_map/reduce_scatter | solution.py:353
  365.1 9.7 copy-start.37
  378.6 51.5 %copy-start.20 = (bf16[128,2,1024]{2,1,0:T(2,128)(2,1)S(1)}, bf16[128,2,1024]{2,1,0:T(2,128)(2,1)}, u32[]{:S(2)}) copy-start(bf16[128,2,1024]{2,1,0:T(2,128)(2,1)} %param.29) | copy-start | bytes 1572868
  378.6 51.5 %copy-start.38 = (bf16[128,2,1024]{2,0,1:T(8,128)(2,1)S(1)}, bf16[128,2,1024]{2,0,1:T(8,128)(2,1)}, u32[]{:S(2)}) copy-start(bf16[128,2,1024]{2,0,1:T(8,128)(2,1)} %copy.247) | copy-start | bytes 1572868
  378.6 51.5 %copy-start.54 = (f32[1024]{0:T(1024)S(1)}, f32[1024]{0:T(1024)}, u32[]{:S(2)}) copy-start(f32[1024]{0:T(1024)} %param.35) | copy-start | bytes 12292
  378.6 51.5 %copy-start.61 = (f32[128,2]{0,1:T(2,128)S(1)}, f32[128,2]{0,1:T(2,128)}, u32[]{:S(2)}) copy-start(f32[128,2]{0,1:T(2,128)} %copy-done.60) | copy-start | bytes 3076
  430.1 5.9 copy-start.12
  462.3 702.9 %reduce-scatter.20.cloned.1.call-start = ((), (), s32[]{:S(2)}) async-start(), calls=%async_computation.16 | async-start | bytes 11894784 | tf_op jit(solution)/shard_map/reduce_scatter | solution.py:355
  475.4 5.8 copy-start.52
  475.4 7.7 copy-start.36
  475.4 7.7 copy-start.51
  478.8 6.1 copy-start.49
  478.8 6.1 copy-start.50
  481.3 4.1 copy-start.47
  481.3 4.1 copy-start.48
  485.3 3.0 copy-start.63
  485.4 2.9 copy-start.68
  486.2 679.1 %copy-start.1 = (bf16[1024,1024]{1,0:T(8,128)(2,1)S(1)}, bf16[1024,1024]{1,0:T(8,128)(2,1)}, u32[]{:S(2)}) copy-start(bf16[1024,1024]{1,0:T(8,128)(2,1)} %param.41) | copy-start | bytes 6291460
  (35 other events, 65.0 us)
Sparse Core Ops, SparseCore 0:
  10.5 26.1 all-gather.10
  39.2 23.4 all-gather.8
  65.3 27.8 all-gather.6
  95.5 27.8 all-gather.4
  248.7 36.0 reduce-scatter.15
  287.8 35.9 reduce-scatter.13
  344.0 41.1 reduce-scatter.9
  388.8 41.2 reduce-scatter.11
  432.3 149.0 reduce-scatter.21
  583.6 414.5 reduce-scatter.17
  1001.1 164.0 reduce-scatter.19

commit v2 on v0

v2 whole, which is shorter than its diff:
```python
import functools

import jax
import jax.numpy as jnp
from jax import lax
from jax.experimental import pallas as pl
from jax.experimental.pallas import tpu as pltpu
from jax.sharding import PartitionSpec as P

GROUPS = 8


epsilon = 1e-06
scale = 0.125
negative = -1e30
highest = lax.Precision.HIGHEST
bf16 = jnp.bfloat16
f32 = jnp.float32


def norm_rate(value):
    return lax.rsqrt(jnp.mean(value * value, axis=-1, keepdims=True) + epsilon)


def norm_back(value, rate, gain, incoming):
    scaled = incoming * gain
    inner = jnp.mean(scaled * value, axis=-1, keepdims=True)
    grad = rate * (scaled - value * (rate * rate * inner))
    return grad, jnp.sum(incoming * value * rate, axis=0)


def mm(left, right):
    return jnp.dot(left, right, preferred_element_type=f32)


def mm_t(grad, weight):
    return lax.dot_general(grad, weight, (((1,), (1,)), ((), ())), preferred_element_type=f32)


def exchange(value, axis, bit):
    size = lax.axis_size(axis)
    return lax.ppermute(value, axis, [(i, i ^ bit) for i in range(size)])


def bits_of(size, lowest):
    bits = []
    bit = lowest
    while bit < size:
        bits.append(bit)
        bit = bit * 2
    return bits


TILE = 256


def grad_order(flip):
    seq_bits = bits_of(lax.axis_size("seq"), 2)
    if flip:
        seq_bits = seq_bits[::-1]
    return [("seq", b) for b in seq_bits] + [("dp", b) for b in bits_of(lax.axis_size("dp"), 1)]


def grads_kernel(chips, orders, tasks, sources, count, me_ref, *refs):
    ins, refs = refs[:sources], refs[count:]
    outs, (turned, total) = refs[:4], refs[4:]
    blocks = 2 ** len(orders[0])
    filled = [0, 0]
    for (xo, xp, do, dp), tokens, rows, rchip, tiles in tasks:
        for half, (place, lane) in enumerate((xo, xp)):
            turned[:rows, half * tokens : (half + 1) * tokens] = ins[place][:, lane : lane + rows].T
        for stack, lane in tiles:
            value = mm(turned[:rows, :tokens], ins[do[0]][:, do[1] + lane : do[1] + lane + TILE])
            value = value + mm(
                turned[:rows, tokens : 2 * tokens], ins[dp[0]][:, dp[1] + lane : dp[1] + lane + TILE]
            )
            for block in range(blocks):
                total[block, :rchip] = value[block * rchip : (block + 1) * rchip]
            order = orders[stack]
            for slot in range(blocks):
                seq_part, dp_part = 0, 0
                for place, (axis, bit) in enumerate(order):
                    if (slot >> (len(order) - 1 - place)) & 1:
                        if axis == "seq":
                            seq_part = seq_part | (bit // 2)
                        else:
                            dp_part = dp_part | bit
                block = (me_ref[0] ^ dp_part) * chips + (me_ref[1] ^ seq_part)
                outs[2 * stack + slot // (blocks // 2)][
                    slot % (blocks // 2), filled[stack] : filled[stack] + rchip
                ] = total[block, :rchip].astype(bf16)
            filled[stack] += rchip


def group_grads(arrays, tasks, after=()):
    chips = lax.axis_size("seq") // 2
    orders = [grad_order(False), grad_order(True)]
    blocks = 2 ** len(orders[0])
    full = []
    depth = [0, 0]
    flops = 0
    for names, rows, tiles in tasks:
        tokens = arrays[names[0][0]].shape[0]
        full.append((names, tokens, rows, rows // blocks, tiles))
        flops += 4 * tokens * rows * TILE * len(tiles)
        for stack, lane in tiles:
            depth[stack] += rows // blocks
    me = jnp.stack([lax.axis_index("dp"), lax.axis_index("seq") // 2]).astype(jnp.int32)
    vmem = pl.BlockSpec(memory_space=pltpu.VMEM)
    most = max(t[2] for t in full)
    shapes = [jax.ShapeDtypeStruct((blocks // 2, depth[i // 2], TILE), bf16) for i in range(4)]
    total = arrays[0].dtype.itemsize * sum(a.size for a in arrays)
    return pl.pallas_call(
        functools.partial(grads_kernel, chips, orders, full, len(arrays), len(arrays) + len(after)),
        in_specs=[pl.BlockSpec(memory_space=pltpu.SMEM)]
        + [vmem] * len(arrays)
        + [pl.BlockSpec(memory_space=pl.ANY)] * len(after),
        out_specs=[vmem] * 4,
        scratch_shapes=[
            pltpu.VMEM((most, max(2 * t[1] for t in full)), bf16),
            pltpu.VMEM((blocks, most // blocks, TILE), f32),
        ],
        out_shape=shapes,
        compiler_params=pltpu.CompilerParams(vmem_limit_bytes=44 * 1024 * 1024),
        cost_estimate=pl.CostEstimate(
            flops=flops, bytes_accessed=total + 4 * sum(depth) * blocks * TILE, transcendentals=0
        ),
    )(me, *arrays, *after)


class Chain:
    def __init__(self, outs):
        self.keep, self.send = [outs[0], outs[2]], [outs[1], outs[3]]
        self.orders = [grad_order(False), grad_order(True)]
        self.level = 0
        self.joint = False

    def step(self):
        order = self.orders[0]
        joint = order[self.level][0] == "dp"
        if joint and not self.joint:
            self.keep = [jnp.concatenate(self.keep, axis=1)]
            self.send = [jnp.concatenate(self.send, axis=1)]
            self.joint = True
        got = [
            exchange(v, *self.orders[i][self.level]) for i, v in enumerate(self.send)
        ]
        self.level += 1
        half = got[0].shape[0] // 2
        if half:
            self.send = [k[half:] + g[half:] for k, g in zip(self.keep, got)]
            self.keep = [k[:half] + g[:half] for k, g in zip(self.keep, got)]
        else:
            self.keep = [k.astype(f32) + g.astype(f32) for k, g in zip(self.keep, got)]
        return got

    def finish(self):
        while self.level < len(self.orders[0]):
            self.step()
        return self.keep[0][0]


def swap_rows(parts):
    lows, highs = [], []
    for part in parts:
        half = part.shape[1] // 2
        lows.append(part[:, :half].reshape(-1, TILE))
        highs.append(part[:, half:].reshape(-1, TILE))
    low = jnp.concatenate(lows, axis=0)
    high = jnp.concatenate(highs, axis=0)
    mine, other = core_halves(low, high)
    got = exchange(other.astype(bf16), "seq", 1).astype(f32)
    first, second = core_halves(mine, got)
    done = []
    start = 0
    for part in parts:
        tiles, half = part.shape[0], part.shape[1] // 2
        pair = []
        for whole in (first, second):
            piece = whole[start : start + tiles * half].reshape(tiles, half, TILE)
            pair.append(jnp.transpose(piece, (1, 0, 2)).reshape(half, tiles * TILE))
        done.append(tuple(pair))
        start += tiles * half
    return done


def core_halves(left, right):
    core = lax.axis_index("seq") % 2
    return jnp.where(core == 0, left, right), jnp.where(core == 0, right, left)


def pair_grad(left, right):
    mine, other = core_halves(left, right)
    return mine, exchange(other, "seq", 1)


def cut(value):
    half = value.shape[1] // 2
    return value[:, :half], value[:, half:]


def gather_seq(value):
    pieces = {0: value}
    for bit in bits_of(lax.axis_size("seq"), 2) + [1]:
        for off in list(pieces):
            pieces[off ^ bit] = exchange(pieces[off], "seq", bit)
    return [pieces[off] for off in range(len(pieces))]


def scatter_seq(mine, other):
    got = exchange(other, "seq", 1)
    size = mine.shape[0]
    total = mine[:2].astype(f32) + got[:2].astype(f32)
    for chip in range(1, size // 2):
        part = mine[2 * chip : 2 * chip + 2].astype(f32) + got[2 * chip : 2 * chip + 2].astype(f32)
        total = total + exchange(part.astype(bf16), "seq", 2 * chip).astype(f32)
    total = total.astype(bf16)
    return total[0], total[1], exchange(total[1], "seq", 1)


def sum_all(value):
    for axis, bit in [("seq", b) for b in bits_of(lax.axis_size("seq"), 1)] + [
        ("dp", b) for b in bits_of(lax.axis_size("dp"), 1)
    ]:
        value = value + exchange(value, axis, bit)
    return value


UNIT = 256


def nt(left, right):
    return lax.dot_general(left, right, (((1,), (1,)), ((), ())), preferred_element_type=f32)


def make_strip(e_ref, strip, tokens):
    heads, parts = strip.shape[0], strip.shape[1]
    for h in range(heads):
        line = e_ref[0, h : h + 1, :]
        turned = pltpu.roll(
            jnp.broadcast_to(line, (tokens, line.shape[1])), 0, 1, stride=1, stride_axis=0
        )
        for d in range(parts):
            strip[h, d] = turned[:, tokens * (d + 1) : tokens * (d + 2)]


def two_heads(ref, rows, lane, head):
    return jnp.concatenate(
        [ref[rows, lane : lane + head], ref[rows, lane + head : lane + 2 * head]], axis=0
    )


def unit_rows(refs, unit, per_unit, count, s, lane, head):
    return jnp.concatenate(
        [
            refs[unit * per_unit + p][s * count : (s + 1) * count, lane : lane + head]
            for p in range(per_unit)
        ],
        axis=0,
    )


def unit_bias(strip, me, unit, per_unit, group):
    rows = []
    for p in range(per_unit):
        place = me - (me ^ (unit * per_unit + p)) + 1
        rows.append(jnp.concatenate([strip[2 * group, place], strip[2 * group + 1, place]], axis=1))
    return jnp.concatenate(rows, axis=0)


def attend_kernel(biased, seqs, tokens, count, pieces, batch, *refs):
    info, refs = refs[0], refs[1:]
    if biased:
        e_ref, refs = refs[0], refs[1:]
    q_ref, refs = refs[0], refs[1:]
    k_refs, v_refs = refs[:pieces], refs[pieces : 2 * pieces]
    out_ref, lse_ref, peak, total, mixed, queries = refs[2 * pieces : 2 * pieces + 6]
    if biased:
        strip = refs[2 * pieces + 6]
        make_strip(e_ref, strip, tokens)
    per_unit = UNIT // count
    units = pieces // per_unit
    me = info[0]
    mine = me // per_unit
    head = q_ref.shape[1] // (2 * batch)
    for s in range(seqs):
        rows = slice(s * tokens, (s + 1) * tokens)

        @pl.when(info[1 + s] > 0)
        def _(s=s, rows=rows):
            for g in range(batch):
                queries[g] = two_heads(q_ref, rows, 2 * g * head, head) * scale
            peak[...] = jnp.full(peak.shape, -3e38, f32)
            total[...] = jnp.zeros(total.shape, f32)
            mixed[...] = jnp.zeros(mixed.shape, f32)
            for unit in range(units):
                if biased:
                    used = (unit ^ mine) <= mine
                else:
                    used = (unit ^ mine) < info[1 + s]

                @pl.when(used)
                def _(unit=unit):
                    states = []
                    for g in range(batch):
                        k = unit_rows(k_refs, unit, per_unit, count, s, g * head, head)
                        scores = nt(k, queries[g])
                        if biased:
                            scores = scores + unit_bias(strip, me, unit, per_unit, g)
                        states.append((scores, peak[g], total[g], mixed[g]))
                    done = []
                    for g, (scores, old, summed, part) in enumerate(states):
                        v = unit_rows(v_refs, unit, per_unit, count, s, g * head, head)
                        top = jnp.maximum(old, jnp.max(scores, axis=0, keepdims=True))
                        raised = jnp.exp(scores - top)
                        fade = jnp.exp(old - top)
                        done.append(
                            (
                                top,
                                summed * fade + jnp.sum(raised, axis=0, keepdims=True),
                                part * fade + mm(v.T, raised.astype(bf16)),
                            )
                        )
                    for g in range(batch):
                        peak[g], total[g], mixed[g] = done[g]

            for g in range(batch):
                lse_ref[0, batch * s + g : batch * s + g + 1, :] = peak[g] + jnp.log(total[g])
                done = (mixed[g] / total[g]).T.astype(bf16)
                out_ref[rows, 2 * g * head : 2 * (g + 1) * head] = jnp.concatenate(
                    [done[:tokens], done[tokens:]], axis=1
                )

        @pl.when(info[1 + s] <= 0)
        def _(s=s, rows=rows):
            lse_ref[0, batch * s : batch * (s + 1), :] = jnp.zeros((batch, 2 * tokens), f32)
            out_ref[rows, :] = jnp.zeros((tokens, out_ref.shape[1]), bf16)


def back_kernel(biased, seqs, tokens, count, pieces, after, batch, *refs):
    info, refs = refs[0], refs[1 + after :]
    if biased:
        e_ref, refs = refs[0], refs[1:]
    q_ref, o_ref, do_ref, lse_ref, refs = refs[0], refs[1], refs[2], refs[3], refs[4:]
    k_refs, v_refs, refs = refs[:pieces], refs[pieces : 2 * pieces], refs[2 * pieces :]
    dq_ref, keep, send, refs = refs[0], refs[1], refs[2], refs[3:]
    if biased:
        table_ref, refs = refs[0], refs[1:]
    dq, queries, grads, inner = refs[:4]
    if biased:
        strip, sums = refs[4:]
        make_strip(e_ref, strip, tokens)
        sums[...] = jnp.zeros(sums.shape, f32)
    per_unit = UNIT // count
    units = pieces // per_unit
    me = info[0]
    mine = me // per_unit
    first = me % 2 == 0
    head = q_ref.shape[1] // (2 * batch)
    for s in range(seqs):
        rows = slice(s * tokens, (s + 1) * tokens)
        keys = slice(s * count, (s + 1) * count)

        def clear(unit, keys=keys):
            for p in range(per_unit):
                piece = unit * per_unit + p
                keep[piece, keys, :] = jnp.zeros((count, batch * head), bf16)
                send[piece ^ 1, keys, :] = jnp.zeros((count, batch * head), bf16)

        @pl.when(info[1 + s] > 0)
        def _(s=s, rows=rows, keys=keys, clear=clear):
            for g in range(batch):
                lane = 2 * g * head
                queries[g] = two_heads(q_ref, rows, lane, head) * scale
                do2 = two_heads(do_ref, rows, lane, head)
                o2 = two_heads(o_ref, rows, lane, head)
                grads[g] = do2
                inner[g] = jnp.sum((o2.astype(f32) * do2.astype(f32)).T, axis=0, keepdims=True)
            dq[...] = jnp.zeros(dq.shape, f32)
            for unit in range(units):
                if biased:
                    used = (unit ^ mine) <= mine
                else:
                    used = (unit ^ mine) < info[1 + s]

                @pl.when(used)
                def _(unit=unit):
                    states = []
                    for g in range(batch):
                        k = unit_rows(k_refs, unit, per_unit, count, s, g * head, head)
                        v = unit_rows(v_refs, unit, per_unit, count, s, g * head, head)
                        scores = nt(k, queries[g])
                        if biased:
                            scores = scores + unit_bias(strip, me, unit, per_unit, g)
                        states.append((k, scores, nt(v, grads[g])))
                    done, turned = [], []
                    for g, (k, scores, down) in enumerate(states):
                        share = jnp.exp(scores - lse_ref[0, batch * s + g : batch * s + g + 1, :])
                        grad = (share * (down - inner[g])).astype(bf16)
                        dv = mm(share.astype(bf16), grads[g])
                        dk = mm(grad, queries[g])
                        turned.append(mm(k.T, grad))
                        done.append(
                            (
                                grad,
                                jnp.where(first, dk, dv).astype(bf16),
                                jnp.where(first, dv, dk).astype(bf16),
                            )
                        )
                    for g in range(batch):
                        dq[g] += turned[g]
                    kept = jnp.concatenate([d[1] for d in done], axis=1)
                    sent = jnp.concatenate([d[2] for d in done], axis=1)
                    for p in range(per_unit):
                        piece = unit * per_unit + p
                        part = slice(p * count, (p + 1) * count)
                        keep[piece, keys, :] = kept[part]
                        send[piece ^ 1, keys, :] = sent[part]
                        if biased:
                            place = me - (me ^ piece) + 1
                            for g in range(batch):
                                for h in range(2):
                                    sums[2 * g + h, place] += done[g][0][
                                        part, h * tokens : (h + 1) * tokens
                                    ].astype(f32)

                @pl.when(jnp.logical_not(used))
                def _(unit=unit):
                    clear(unit)

            for g in range(batch):
                done = (dq[g] * scale).T.astype(bf16)
                dq_ref[rows, 2 * g * head : 2 * (g + 1) * head] = jnp.concatenate(
                    [done[:tokens], done[tokens:]], axis=1
                )

        @pl.when(info[1 + s] <= 0)
        def _(rows=rows, clear=clear):
            for unit in range(units):
                clear(unit)
            dq_ref[rows, :] = jnp.zeros((tokens, dq_ref.shape[1]), bf16)

    if biased:
        parts = sums.shape[1]
        span = tokens * (parts + 1)
        for h in range(2 * batch):
            line = jnp.concatenate(
                [jnp.zeros((tokens, tokens), f32)] + [sums[h, d] for d in range(parts)], axis=1
            )
            height = tokens
            while height > 8:
                height = height // 2
                line = line[:height] + pltpu.roll(line[height:], span - height, 1)
            while height > 1:
                height = height // 2
                upper = pltpu.roll(line, span - height, 1)
                line = line[:height] + upper[height : 2 * height]
            table_ref[0, h : h + 1, :] = line


def block_of(array, lanes, offset=0):
    return pl.BlockSpec((array.shape[0], lanes), lambda i, info: (0, offset + i))


BATCH = 4


def attend(query, pieces, info, seqs, line):
    tokens = query.shape[0] // seqs
    count = pieces[0].shape[0] // seqs
    n = len(pieces)
    steps = GROUPS // BATCH
    wide, narrow = query.shape[1] // steps, pieces[0].shape[1] // 2 // steps
    head = narrow // BATCH
    biased = line is not None
    scratch = [pltpu.VMEM((BATCH, 1, 2 * tokens), f32)] * 2 + [
        pltpu.VMEM((BATCH, head, 2 * tokens), f32),
        pltpu.VMEM((BATCH, 2 * tokens, head), bf16),
    ]
    extra = []
    if biased:
        scratch.append(pltpu.VMEM((2 * BATCH, n + 1, tokens, tokens), f32))
        extra = [pl.BlockSpec((1, 2 * BATCH, line.shape[2]), lambda i, info: (i, 0, 0))]
    pairs = n * count * seqs * tokens * GROUPS * 2
    return pl.pallas_call(
        functools.partial(attend_kernel, biased, seqs, tokens, count, n, BATCH),
        grid_spec=pltpu.PrefetchScalarGridSpec(
            num_scalar_prefetch=1,
            grid=(steps,),
            in_specs=extra
            + [block_of(query, wide)]
            + [block_of(p, narrow) for p in pieces]
            + [block_of(p, narrow, steps) for p in pieces],
            out_specs=[
                block_of(query, wide),
                pl.BlockSpec((1, BATCH * seqs, 2 * tokens), lambda i, info: (i, 0, 0)),
            ],
            scratch_shapes=scratch,
        ),
        out_shape=[
            jax.ShapeDtypeStruct(query.shape, bf16),
            jax.ShapeDtypeStruct((steps, BATCH * seqs, 2 * tokens), f32),
        ],
        compiler_params=pltpu.CompilerParams(vmem_limit_bytes=40 * 1024 * 1024),
        cost_estimate=pl.CostEstimate(
            flops=256 * pairs, bytes_accessed=4 * query.size + 2 * n * pieces[0].size, transcendentals=pairs
        ),
    )(info, *([line] if biased else []), query, *pieces, *pieces)


def attend_back(query, mixed, upstream, logsum, pieces, info, seqs, line, after=()):
    tokens = query.shape[0] // seqs
    count = pieces[0].shape[0] // seqs
    n = len(pieces)
    steps = GROUPS // BATCH
    wide, narrow = query.shape[1] // steps, pieces[0].shape[1] // 2 // steps
    head = narrow // BATCH
    biased = line is not None
    scratch = [
        pltpu.VMEM((BATCH, head, 2 * tokens), f32),
        pltpu.VMEM((BATCH, 2 * tokens, head), bf16),
        pltpu.VMEM((BATCH, 2 * tokens, head), bf16),
        pltpu.VMEM((BATCH, 1, 2 * tokens), f32),
    ]
    extra, extra_out, extra_shape = [], [], []
    if biased:
        scratch += [pltpu.VMEM((2 * BATCH, n + 1, tokens, tokens), f32)] * 2
        extra = [pl.BlockSpec((1, 2 * BATCH, line.shape[2]), lambda i, info: (i, 0, 0))]
        extra_out = [pl.BlockSpec((1, 2 * BATCH, tokens * (n + 2)), lambda i, info: (i, 0, 0))]
        extra_shape = [jax.ShapeDtypeStruct((steps, 2 * BATCH, tokens * (n + 2)), f32)]
    part = pl.BlockSpec((n, seqs * count, narrow), lambda i, info: (0, 0, i))
    part_shape = jax.ShapeDtypeStruct((n, seqs * count, narrow * steps), bf16)
    pairs = n * count * seqs * tokens * GROUPS * 2
    return pl.pallas_call(
        functools.partial(back_kernel, biased, seqs, tokens, count, n, len(after), BATCH),
        grid_spec=pltpu.PrefetchScalarGridSpec(
            num_scalar_prefetch=1,
            grid=(steps,),
            in_specs=[pl.BlockSpec(memory_space=pl.ANY)] * len(after)
            + extra
            + [block_of(query, wide)] * 3
            + [pl.BlockSpec((1, BATCH * seqs, 2 * tokens), lambda i, info: (i, 0, 0))]
            + [block_of(p, narrow) for p in pieces]
            + [block_of(p, narrow, steps) for p in pieces],
            out_specs=[block_of(query, wide), part, part] + extra_out,
            scratch_shapes=scratch,
        ),
        out_shape=[jax.ShapeDtypeStruct(query.shape, bf16), part_shape, part_shape] + extra_shape,
        compiler_params=pltpu.CompilerParams(vmem_limit_bytes=44 * 1024 * 1024),
        cost_estimate=pl.CostEstimate(
            flops=640 * pairs, bytes_accessed=8 * query.size + 6 * n * pieces[0].size, transcendentals=pairs
        ),
    )(info, *after, *([line] if biased else []), query, mixed, upstream, logsum, *pieces, *pieces)


def feed_kernel(core_ref, second, live, gain, normed, grad_low, gate_w, up_w, down_w, hidden, own, pair, outputs, grad, gain_grad, result, feed_in):
    step = pl.program_id(0)

    @pl.when(step == 0)
    def _():
        result[...] = jnp.zeros(result.shape, f32)
        feed_in[...] = jnp.zeros(feed_in.shape, f32)

    gate = mm(normed[...], gate_w[...])
    upper = mm(normed[...], up_w[...])
    incoming = nt(grad_low[...], down_w[...])
    square = gate * gate
    slope = 0.7978845608028654 * 0.044715
    bend = jnp.tanh(gate * (0.7978845608028654 + slope * square))
    rise = 0.5 * (1.0 + bend)
    curve = gate * rise
    steep = rise + 0.5 * gate * (1.0 - bend * bend) * (0.7978845608028654 + 3.0 * slope * square)
    acted = (curve * upper).astype(bf16)
    gate_grad = (incoming * upper * steep).astype(bf16)
    upper_grad = (incoming * curve).astype(bf16)
    hidden[...] = acted
    first = core_ref[0] == 0
    own[...] = jnp.where(first, gate_grad, upper_grad)
    pair[...] = jnp.where(first, upper_grad, gate_grad)
    result[...] += mm(acted, down_w[...])
    feed_in[...] += nt(gate_grad, gate_w[...]) + nt(upper_grad, up_w[...])

    @pl.when(step == pl.num_programs(0) - 1)
    def _():
        value = second[...]
        outputs[...] = ((value + result[...]) * live[...]).astype(bf16)
        rate = norm_rate(value)
        scaled = feed_in[...] * gain[...]
        inner = jnp.mean(scaled * value, axis=-1, keepdims=True)
        grad[...] = grad_low[...].astype(f32) + rate * (scaled - value * (rate * rate * inner))
        gain_grad[...] = jnp.sum(feed_in[...] * value * rate, axis=0, keepdims=True)


def feed_forward(core, second, live, gain, normed, grad_low, gate_weight, up_weight, down_weight):
    tokens, width = second.shape
    units = gate_weight.shape[1]
    whole = pl.BlockSpec((tokens, width), lambda i: (0, 0))
    line = pl.BlockSpec((1, width), lambda i: (0, 0))
    tall = pl.BlockSpec((width, TILE), lambda i: (0, i))
    part = pl.BlockSpec((tokens, TILE), lambda i: (0, i))
    part_shape = jax.ShapeDtypeStruct((tokens, units), bf16)
    return pl.pallas_call(
        feed_kernel,
        grid=(units // TILE,),
        in_specs=[
            pl.BlockSpec(memory_space=pltpu.SMEM),
            whole,
            pl.BlockSpec((tokens, 1), lambda i: (0, 0)),
            line,
            whole,
            whole,
            tall,
            tall,
            pl.BlockSpec((TILE, width), lambda i: (i, 0)),
        ],
        out_specs=[part, part, part, whole, whole, line],
        out_shape=[part_shape] * 3
        + [
            jax.ShapeDtypeStruct((tokens, width), bf16),
            jax.ShapeDtypeStruct((tokens, width), f32),
            jax.ShapeDtypeStruct((1, width), f32),
        ],
        scratch_shapes=[pltpu.VMEM((tokens, width), f32)] * 2,
        compiler_params=pltpu.CompilerParams(vmem_limit_bytes=32 * 1024 * 1024),
        cost_estimate=pl.CostEstimate(
            flops=12 * tokens * width * units,
            bytes_accessed=6 * width * units + 6 * tokens * units + 14 * tokens * width,
            transcendentals=tokens * units,
        ),
    )(core, second, live, gain.reshape(1, -1), normed, grad_low, gate_weight, up_weight, down_weight)


def per_device(
    inputs,
    memory,
    target_length,
    memory_length,
    distance_bucket,
    bias_table,
    self_gain,
    self_query,
    self_key,
    self_value,
    self_out,
    cross_gain,
    cross_query,
    cross_key,
    cross_value,
    cross_out,
    feed_gain,
    gate_weight,
    up_weight,
    down_weight,
    upstream,
):
    tokens, seqs, width = inputs.shape
    mem_tokens = memory.shape[0]
    size = lax.axis_size("seq")
    length = tokens * size
    buckets = bias_table.shape[0]
    me = lax.axis_index("seq")

    def flat(array):
        return jnp.transpose(array, (1, 0, 2)).reshape(-1, array.shape[2])

    def unflat(array):
        return jnp.transpose(array.reshape(seqs, -1, array.shape[1]), (1, 0, 2))

    positions = me * tokens + jnp.arange(tokens, dtype=jnp.int32)
    live = (positions[None, :] < target_length[:, None]).reshape(-1, 1)
    held = me * mem_tokens + jnp.arange(mem_tokens, dtype=jnp.int32)
    held = (held[None, :] < memory_length[:, None]).reshape(-1, 1)
    me_line = me.astype(jnp.int32).reshape(1)
    self_info = jnp.concatenate([me_line, (me * tokens < target_length).astype(jnp.int32)])
    cross_info = jnp.concatenate([me_line, (memory_length + UNIT - 1) // UNIT])

    x = flat(inputs)
    xf = x.astype(f32)
    mem = jnp.where(held, flat(memory), 0)
    grad_low = jnp.where(live, flat(upstream), 0)
    rate_self = norm_rate(xf)
    normed_self = (xf * rate_self * self_gain).astype(bf16)
    keys = mm(normed_self, self_key).astype(bf16)
    values = mm(normed_self, self_value).astype(bf16)
    gathered = gather_seq(jnp.concatenate([keys, values], axis=1))
    memory_kv = jnp.concatenate(
        [mm(mem, cross_key).astype(bf16), mm(mem, cross_value).astype(bf16)], axis=1
    )
    recalled = gather_seq(memory_kv)
    query = mm(normed_self, self_query).astype(bf16)

    bucket_match = distance_bucket[:, None] == jnp.arange(buckets, dtype=jnp.int32)[None, :]
    bucket_onehot = bucket_match.astype(f32)
    line = jnp.dot(bias_table.T, bucket_onehot.T, precision=highest, preferred_element_type=f32)
    line = jnp.concatenate([jnp.full((line.shape[0], 2 * tokens), negative, f32), line], axis=1)
    line = line.reshape(GROUPS // BATCH, -1, length + 2 * tokens)

    self_mixed, self_logsum = attend(query, gathered, self_info, seqs, line)
    first = xf + mm(self_mixed, self_out)
    rate_cross = norm_rate(first)
    normed_cross = (first * rate_cross * cross_gain).astype(bf16)
    recall_query = mm(normed_cross, cross_query).astype(bf16)
    cross_mixed, cross_logsum = attend(recall_query, recalled, cross_info, seqs, None)
    second = first + mm(cross_mixed, cross_out)
    rate_feed = norm_rate(second)
    normed_feed = (second * rate_feed * feed_gain).astype(bf16)
    core = (me % 2).astype(jnp.int32).reshape(1)
    hidden, gu_own, gu_other, outputs, second_grad, feed_gain_grad = feed_forward(
        core, second, live.astype(f32), feed_gain, normed_feed, grad_low, gate_weight, up_weight, down_weight
    )
    feed_gain_grad = feed_gain_grad.reshape(-1)
    low_own, low_pair = pair_grad(*cut(grad_low))
    mem_pair = exchange(mem, "seq", 1)
    shared = exchange(
        jnp.concatenate([normed_self, self_mixed, normed_cross, cross_mixed, normed_feed], axis=1), "seq", 1
    )
    hidden_pair = exchange(hidden, "seq", 1)
    gu_pair = exchange(gu_other, "seq", 1)
    hidden_cols = hidden.shape[1]
    tiles = hidden_cols // TILE
    cutting = tiles // 2
    second_low = second_grad.astype(bf16)
    cross_mixed_grad = mm_t(second_low, cross_out).astype(bf16)
    recall_query_grad, kept, sent = attend_back(
        recall_query, cross_mixed, cross_mixed_grad, cross_logsum, recalled, cross_info, seqs, None
    )
    gu_task = (((1, 0), (2, 4 * width), (5, 0), (6, 0)), width)
    feed_chain = Chain(
        group_grads(
            [hidden, normed_feed, shared, low_own, low_pair, gu_own, gu_pair, hidden_pair],
            [
                gu_task + ([(0, j * TILE) for j in range(cutting)],),
                gu_task + ([(1, j * TILE) for j in range(cutting, tiles)],),
                (((0, 0), (7, 0), (3, 0), (4, 0)), hidden_cols, [(0, 0), (1, TILE)]),
            ],
            [recall_query_grad],
        )
    )
    early = list(feed_chain.send)
    feed_first = feed_chain.step()
    memory_half, memory_half_pair, memory_other = scatter_seq(kept, sent)
    cross_in = mm_t(recall_query_grad, cross_query)
    first_part, cross_gain_grad = norm_back(first, rate_cross, cross_gain, cross_in)
    first_grad = second_grad + first_part
    first_low = first_grad.astype(bf16)
    self_mixed_grad = mm_t(first_low, self_out).astype(bf16)
    halves = [core_halves(*cut(v)) for v in (second_low, recall_query_grad, first_low)]
    grads_own = jnp.concatenate([h[0] for h in halves], axis=1)
    grads_pair = exchange(jnp.concatenate([h[1] for h in halves], axis=1), "seq", 1)
    memory_key_low, memory_value_low = core_halves(memory_half, memory_other)
    memory_grad = mm_t(memory_key_low, cross_key) + mm_t(memory_value_low, cross_value)

    query_grad, kept, sent, line_grad = attend_back(
        query, self_mixed, self_mixed_grad, self_logsum, gathered, self_info, seqs, line, early
    )
    line_grad = line_grad.reshape(-1, line_grad.shape[2])[:, 2 * tokens :]
    table_grad = jnp.dot(line_grad, bucket_onehot, precision=highest, preferred_element_type=f32).T
    key_half, key_half_pair, key_other = scatter_seq(kept, sent)
    two = [(0, 0), (1, TILE)]
    out_chain = Chain(
        group_grads(
            [cross_mixed, normed_cross, self_mixed, shared, mem, mem_pair, grads_own, grads_pair, memory_half, memory_half_pair],
            [
                (((0, 0), (3, 3 * width), (6, 0), (7, 0)), width, two),
                (((1, 0), (3, 2 * width), (6, width // 2), (7, width // 2)), width, two),
                (((2, 0), (3, width), (6, width), (7, width)), width, two),
                (((4, 0), (5, 0), (8, 0), (9, 0)), width, two),
            ],
            [query_grad] + feed_first,
        )
    )
    query_own, query_pair = pair_grad(*cut(query_grad))
    in_chain = Chain(
        group_grads(
            [normed_self, shared, query_own, query_pair, key_half, key_half_pair],
            [
                (((0, 0), (1, 0), (2, 0), (3, 0)), width, two),
                (((0, 0), (1, 0), (4, 0), (5, 0)), width, two),
            ],
            [out_chain.send[0]],
        )
    )
    key_low, value_low = core_halves(key_half, key_other)
    self_in = mm_t(query_grad, self_query) + mm_t(key_low, self_key) + mm_t(value_low, self_value)
    input_part, self_gain_grad = norm_back(xf, rate_self, self_gain, self_in)
    input_grad = first_grad + input_part
    small = jnp.concatenate(
        [self_gain_grad, cross_gain_grad, feed_gain_grad, table_grad.reshape(-1)]
    ).reshape(-1, 128)
    small = sum_all(small).reshape(-1)

    blocks = 2 ** len(grad_order(False))
    narrow, broad = width // blocks, hidden_cols // blocks
    piece = feed_chain.finish()
    middle = cutting * narrow
    feed_tiles = jnp.concatenate([piece[:middle], piece[middle + broad : -broad]], axis=0)
    down_tiles = jnp.concatenate([piece[middle : middle + broad], piece[-broad:]], axis=0)
    (gate_out, up_out), down_out = swap_rows(
        [
            feed_tiles.reshape(tiles, narrow, TILE),
            down_tiles.reshape(2, broad, TILE),
        ]
    )

    def by_weight(piece):
        stacks = piece.reshape(2, -1, narrow, TILE)
        return swap_rows([stacks[:, i] for i in range(stacks.shape[1])])

    cross_out_out, cross_query_out, self_out_out, cross_kv_out = by_weight(out_chain.finish())
    self_query_out, self_kv_out = by_weight(in_chain.finish())

    def joined(pair):
        return jnp.concatenate(pair, axis=1)

    return (
        unflat(outputs),
        unflat(input_grad),
        unflat(memory_grad),
        small[:width],
        joined(self_query_out),
        self_kv_out[0],
        self_kv_out[1],
        joined(self_out_out),
        small[3 * width :].reshape(buckets, -1),
        small[width : 2 * width],
        joined(cross_query_out),
        cross_kv_out[0],
        cross_kv_out[1],
        joined(cross_out_out),
        small[2 * width : 3 * width],
        gate_out,
        up_out,
        joined(down_out),
    )


def solution(mesh):
    placed = P("seq", "dp", None)
    rows = P(("dp", "seq"), None)
    return jax.shard_map(
        per_device,
        mesh=mesh,
        in_specs=(placed, placed, P("dp"), P("dp")) + (P(),) * 16 + (placed,),
        out_specs=(
            placed,
            placed,
            placed,
            P(),
            rows,
            rows,
            rows,
            rows,
            P(),
            P(),
            rows,
            rows,
            rows,
            rows,
            P(),
            rows,
            rows,
            rows,
        ),
        check_vma=False,
    )
```

time: 1180 us -> 447 us (0.38)
  waiting for transfers between devices: 746 us -> 217 us
  matrix products: 182 us -> 14.9 us
  local copies, waits for them, and re-layouts: 123 us -> 32.1 us
  Pallas kernels: 0 us -> 82.9 us
  starting transfers between devices: 0.92 us -> 57.8 us
  blocking collectives: 42.2 us -> 0 us
  other arithmetic: 61.6 us -> 34.3 us
  between operations: 15 us -> 2.47 us
    reduce_scatter x6 -> x0, waiting for transfers between devices: 622 us -> none  [the longest x1 415 us: per_device(): lax.psum_scatter(rows_block, ('dp', 'seq'), scatter_dimension=0, tiled=True)]
    ppermute x0 -> x57, waiting for transfers between devices: none -> 217 us  [exchange(): return lax.ppermute(value, axis, [(i, i ^ bit) for i in range(size)])]
    dot_general x60 -> x18, matrix products: 182 us -> 14.9 us  [the longest x8 8.5 us: mm(): return jnp.dot(left, right, preferred_element_type=f32)]
    pallas_call x0 -> x8, Pallas kernels: none -> 82.9 us  [the longest x2 29.7 us: attend_back(): pl.pallas_call(functools.partial(back_kernel, biased, seqs, tokens, count...]
    all_gather x4 -> x0, waiting for transfers between devices: 67.3 us -> none  [the longest x1 28.1 us: per_device(): lax.all_gather(keys, 'seq', axis=0, tiled=True)]
    ppermute x0 -> x57, starting transfers between devices: none -> 57.8 us  [exchange(): return lax.ppermute(value, axis, [(i, i ^ bit) for i in range(size)])]
    unnamed x12 -> x0, waiting for transfers between devices: 56 us -> none
    psum x1 -> x0, blocking collectives: 42.2 us -> none  [per_device(): gain_sum, table_sum = lax.psum((gains, table_grad), ('dp', 'seq'))]
  transfers between devices with their start and end apart: 11 -> 57, of which waited for: 8 -> 19; matrix products, arithmetic and copies ran while one was open for 20% -> 12% of each run, Pallas kernels for 0% -> 17%
where the time goes in v2:
time: 447 us; the launch traced here: 442 us
  waiting for transfers between devices  217 us (49%)
  Pallas kernels  82.9 us (19%)
  starting transfers between devices  57.8 us (13%)
  other arithmetic  34.3 us (8%)
  local copies, waits for them, and re-layouts  32.1 us (7%)
  matrix products  14.9 us (3%)
    ppermute x57, waiting for transfers between devices, exchange(): return lax.ppermute(value, axis, [(i, i ^ bit) for i in range(size)])  217 us
    ppermute x57, starting transfers between devices, exchange(): return lax.ppermute(value, axis, [(i, i ^ bit) for i in range(size)])  57.8 us
    pallas_call x2, Pallas kernels, attend_back(): pl.pallas_call(functools.partial(back_kernel, biased, seqs, tokens, count...  29.7 us
    pallas_call x3, Pallas kernels, group_grads(): pl.pallas_call(functools.partial(grads_kernel, chips, orders, full, len(a...  20.6 us
    unnamed x170, local copies, waits for them, and re-layouts  18.7 us
    pallas_call x2, Pallas kernels, attend(): pl.pallas_call(functools.partial(attend_kernel, biased, seqs, tokens, cou...  16.4 us
    pallas_call x1, Pallas kernels, feed_forward(): pl.pallas_call(feed_kernel, grid=(units // TILE,), in_specs=[pl.BlockSpec...  16.1 us
    add x12, other arithmetic, step(): self.keep = [k[:half] + g[:half] for k, g in zip(self.keep, got)]  13.3 us
  transfers between devices with their start and end apart: 57, of which 19 were waited for; matrix products, arithmetic and copies ran while one was open for 12% of the time, Pallas kernels for 17%

profile of v2, /device:TPU:0, one launch (start us, length us, event | category | flops | bytes accessed | tf_op | source)
XLA Modules:
  0.0 442.0 jit_solution(10833365886705038699)
XLA Ops:
  2.8 1.7 convolution_convert_fusion.6
  4.9 3.0 collective-permute-start.10
  7.9 1.5 collective-permute-start.8
  14.4 3.3 convolution_convert_fusion.3.refs_2_.refs_4_
  17.7 9.3 %collective-permute-done.1.refs_5_.refs_13_.refs_10_.refs_18_ = bf16[256,1024]{1,0:T(8,128)(2,1)} collective-permute-done((bf16[256,1024]{1,0:T(8,128)(2,1)S(1)}, bf16[256,1024]{1,0:T(8,128)(2,1)}, u32[]{:S(2)}, u32[]{:S(2)}) %collective-permute-start.1) | collective-permute-done | bytes 524320 | tf_op jit(solution)/shard_map/ppermute | solution.py:42
  27.0 1.3 collective-permute-start.5
  29.0 10.5 %collective-permute-done.5.refs_9_.refs_17_.refs_14_.refs_22_ = bf16[256,1024]{1,0:T(8,128)(2,1)} collective-permute-done((bf16[256,1024]{1,0:T(8,128)(2,1)}, bf16[256,1024]{1,0:T(8,128)(2,1)}, u32[]{:S(2)}, u32[]{:S(2)}) %collective-permute-start.5) | collective-permute-done | bytes 524320 | tf_op jit(solution)/shard_map/ppermute | solution.py:42
  42.0 6.6 %collective-permute-done.12.refs_8_.refs_16_.refs_11_.refs_19_ = bf16[128,1024]{1,0:T(8,128)(2,1)} collective-permute-done((bf16[128,1024]{1,0:T(8,128)(2,1)}, bf16[128,1024]{1,0:T(8,128)(2,1)}, u32[]{:S(2)}, u32[]{:S(2)}) %collective-permute-start.12) | collective-permute-done | bytes 262176 | tf_op jit(solution)/shard_map/ppermute | solution.py:42
  50.7 9.2 %shard_map.340 = (bf16[256,1024]{1,0:T(8,128)(2,1)S(1)}, f32[2,8,256]{2,1,0:T(8,128)S(1)}) custom-call(s32[3]{0:T(128)S(1)} %pad_add_fusion.refs_0_, f32[2,8,1280]{2,1,0:T(8,128)S(1)} %pad_bitcast_fusion.refs_1_.refs_3_, bf16[256,1024]{1,0:T(8,128)(2,1)S(1)} %copy-done.25, bf16[256,1024]{1,0:T(8,128)(2,1)S(1)} %pad_maximum_fusion.7.refs_3_.refs_11_.refs_8_.refs_16_, ...), custom_call_target="tpu_custom_call" | custom-call | flops 1073741824 | bytes 5242880 | tf_op jit(solution)/shard_map/pallas_call | solution.py:485
  63.6 7.2 %shard_map.341 = (bf16[256,1024]{1,0:T(8,128)(2,1)S(1)}, f32[2,8,256]{2,1,0:T(8,128)S(1)}) custom-call(s32[3]{0:T(128)S(1)} %pad_add_fusion.1.refs_0_, bf16[256,1024]{1,0:T(8,128)(2,1)S(1)} %convolution_convert_fusion.2.refs_1_, bf16[128,1024]{1,0:T(8,128)(2,1)S(1)} %pad_maximum_fusion.12.refs_2_.refs_10_.refs_5_.refs_13_, ...), custom_call_target="tpu_custom_call" | custom-call | flops 536870912 | bytes 3145728 | tf_op jit(solution)/shard_map/pallas_call | solution.py:485
  81.5 2.6 copy-done.44
  84.1 2.6 copy-done.45
  86.7 16.1 %shard_map.342 = (bf16[256,2816]{1,0:T(8,128)(2,1)S(1)}, bf16[256,2816]{1,0:T(8,128)(2,1)S(1)}, bf16[256,2816]{1,0:T(8,128)(2,1)S(1)}, bf16[256,1024]{1,0:T(8,12...) custom-call(s32[1]{0:T(128)} %bitcast.core_ref, f32[256,1024]{1,0:T(8,128)S(1)} %copy-done.21, ...), custom_call_target="tpu_custom_call" | custom-call | flops 8858370048 | bytes 25296896 | tf_op jit(solution)/shard_map/pallas_call | solution.py:602
  105.7 10.2 %shard_map.343 = (bf16[256,1024]{1,0:T(8,128)(2,1)S(1)}, bf16[8,128,512]{2,1,0:T(8,128)(2,1)S(1)}, bf16[8,128,512]{2,1,0:T(8,128)(2,1)}) custom-call(s32[3]{0:T(128)S(1)} %pad_add_fusion.1.refs_0_, bf16[256,1024]{1,0:T(8,128)(2,1)S(1)} %copy-done.28, bf16[256,1024]{1,0:T(8,128)(2,1)S(1)} %copy-done.3, ...), custom_call_target="tpu_custom_call" | custom-call | flops 1342177280 | bytes 8388608 | tf_op jit(solution)/shard_map/pallas_call | solution.py:534
  117.1 1.3 fusion.37
  120.1 10.4 %shard_map.344 = (bf16[8,496,256]{2,1,0:T(8,128)(2,1)S(1)}, bf16[8,496,256]{2,1,0:T(8,128)(2,1)}, bf16[8,560,256]{2,1,0:T(8,128)(2,1)}, bf16[8,560,256]{2,1,0:T(8,128)(2,1)}) custom-call(s32[2]{0:T(128)S(1)} %pad_add_fusion.2.me_ref, bf16[256,2816]{1,0:T(8,128)(2,1)S(1)} %get-tuple-element.53.refs_0_, bf16[256,1024]{1,0:T(8,128)(2,1)S(1)} %copy-done.40, ...), custom_call_target="tpu_custom_call" | custom-call | flops 4429185024 | bytes 26738688 | tf_op jit(solution)/shard_map/pallas_call | solution.py:113
  130.5 1.3 copy-done.33
  131.8 19.5 %shard_map.345 = (bf16[256,1024]{1,0:T(8,128)(2,1)S(1)}, bf16[8,256,512]{2,1,0:T(8,128)(2,1)}, bf16[8,256,512]{2,1,0:T(8,128)(2,1)}, f32[2,8,1280]{2,1,0:T(8,128)S(1)}) custom-call(s32[3]{0:T(128)S(1)} %pad_add_fusion.refs_0_, bf16[8,496,256]{2,1,0:T(8,128)(2,1)} %get-tuple-element.56.refs_1_, bf16[8,560,256]{2,1,0:T(8,128)(2,1)} %get-tuple-element.57.refs_2_, ...), custom_call_target="tpu_custom_call" | custom-call | flops 2684354560 | bytes 14680064 | tf_op jit(solution)/shard_map/pallas_call | solution.py:534
  151.9 1.3 add_convert_fusion.7
  153.3 8.3 %collective-permute-start.24 = (bf16[2,128,512]{2,1,0:T(8,128)(2,1)S(1)}, bf16[2,128,512]{2,1,0:T(8,128)(2,1)S(1)}, u32[]{:S(2)}, u32[]{:S(2)}) collective-permute-start(bf16[2,128,512]{2,1,0:T(8,128)(2,1)S(1)} %get-tuple-element.171), channel_id=1, source_target_pairs={{0,2},{1,3},{2,0},{3,1},{4,6},{5,7},{6,4},{7,5},{8,10},{9,11},{10,... | collective-permute-start | bytes 786440 | tf_op jit(solution)/shard_map/ppermute | solution.py:42
  161.6 6.6 %collective-permute-start.26 = (bf16[2,128,512]{2,1,0:T(8,128)(2,1)S(1)}, bf16[2,128,512]{2,1,0:T(8,128)(2,1)S(1)}, u32[]{:S(2)}, u32[]{:S(2)}) collective-permute-start(bf16[2,128,512]{2,1,0:T(8,128)(2,1)S(1)} %get-tuple-element.172), channel_id=1, source_target_pairs={{0,6},{1,7},{2,4},{3,5},{4,2},{5,3},{6,0},{7,1},{8,14},{9,15},{10,... | collective-permute-start | bytes 786440 | tf_op jit(solution)/shard_map/ppermute | solution.py:42
  168.2 1.3 copy.156
  170.6 9.6 %collective-permute-done.26 = bf16[2,128,512]{2,1,0:T(8,128)(2,1)S(1)} collective-permute-done((bf16[2,128,512]{2,1,0:T(8,128)(2,1)S(1)}, bf16[2,128,512]{2,1,0:T(8,128)(2,1)S(1)}, u32[]{:S(2)}, u32[]{:S(2)}) %collective-permute-start.26) | collective-permute-done | bytes 262176 | tf_op jit(solution)/shard_map/ppermute | solution.py:42
  180.2 1.4 collective-permute-done.25
  184.7 1.4 add_convert_fusion.3
  186.5 1.7 collective-permute-start.19
  188.4 1.5 collective-permute-start.20
  192.8 48.6 %collective-permute-done.19 = bf16[2,256,512]{2,1,0:T(8,128)(2,1)} collective-permute-done((bf16[2,256,512]{2,1,0:T(8,128)(2,1)}, bf16[2,256,512]{2,1,0:T(8,128)(2,1)}, u32[]{:S(2)}, u32[]{:S(2)}) %collective-permute-start.19) | collective-permute-done | bytes 524320 | tf_op jit(solution)/shard_map/ppermute | solution.py:42
  241.4 10.4 %collective-permute-done.21 = bf16[2,256,512]{2,1,0:T(8,128)(2,1)} collective-permute-done((bf16[2,256,512]{2,1,0:T(8,128)(2,1)}, bf16[2,256,512]{2,1,0:T(8,128)(2,1)}, u32[]{:S(2)}, u32[]{:S(2)}) %collective-permute-start.21) | collective-permute-done | bytes 524320 | tf_op jit(solution)/shard_map/ppermute | solution.py:42
  252.3 2.1 add_convert_fusion
  254.7 3.2 slice_add_fusion.3
  257.9 2.0 collective-permute-start.52
  262.2 1.3 collective-permute-done.37.refs_12_
  263.6 6.0 %shard_map.346 = (bf16[8,256,256]{2,1,0:T(8,128)(2,1)S(1)}, bf16[8,256,256]{2,1,0:T(8,128)(2,1)}, bf16[8,256,256]{2,1,0:T(8,128)(2,1)S(1)}, bf16[8,256,256]{2,1,0:T(8,128)(2,1)}) custom-call(s32[2]{0:T(128)S(1)} %pad_add_fusion.2.me_ref, bf16[256,1024]{1,0:T(8,128)(2,1)S(1)} %copy-done.4, bf16[256,1024]{1,0:T(8,128)(2,1)S(1)} %copy-done.30, ...), custom_call_target="tpu_custom_call" | custom-call | flops 1879048192 | bytes 14942208 | tf_op jit(solution)/shard_map/pallas_call | solution.py:113
  269.6 1.3 collective-permute-start.47
  270.9 2.3 collective-permute-start.45
  273.3 3.3 slice_add_fusion.1
  276.6 18.6 %collective-permute-done.29 = f32[28,128]{1,0:T(8,128)S(1)} collective-permute-done((f32[28,128]{1,0:T(8,128)S(1)}, f32[28,128]{1,0:T(8,128)S(1)}, u32[]{:S(2)}, u32[]{:S(2)}) %collective-permute-start.29) | collective-permute-done | bytes 14368 | tf_op jit(solution)/shard_map/ppermute | solution.py:42
  296.0 4.3 shard_map.347
  300.6 6.4 %collective-permute-done.30 = f32[28,128]{1,0:T(8,128)S(1)} collective-permute-done((f32[28,128]{1,0:T(8,128)S(1)}, f32[28,128]{1,0:T(8,128)S(1)}, u32[]{:S(2)}, u32[]{:S(2)}) %collective-permute-start.30) | collective-permute-done | bytes 14368 | tf_op jit(solution)/shard_map/ppermute | solution.py:42
  307.0 1.6 collective-permute-start.31
  308.6 2.2 collective-permute-done.31
  310.8 2.6 collective-permute-start.32
  313.7 2.0 copy.154
  315.7 1.5 collective-permute-start.53
  318.5 1.7 collective-permute-start.40
  320.3 1.3 slice_add_fusion.12
  323.1 10.0 %collective-permute-done.40 = bf16[8,128,256]{2,1,0:T(8,128)(2,1)S(1)} collective-permute-done((bf16[8,128,256]{2,1,0:T(8,128)(2,1)}, bf16[8,128,256]{2,1,0:T(8,128)(2,1)S(1)}, u32[]{:S(2)}, u32[]{:S(2)}) %collective-permute-start.40) | collective-permute-done | bytes 524320 | tf_op jit(solution)/shard_map/ppermute | solution.py:42
  334.0 1.4 slice_add_fusion.8
  335.4 1.4 collective-permute-start.48
  336.8 12.9 %collective-permute-done.41 = bf16[4,128,256]{2,1,0:T(8,128)(2,1)S(1)} collective-permute-done((bf16[4,128,256]{2,1,0:T(8,128)(2,1)S(1)}, bf16[4,128,256]{2,1,0:T(8,128)(2,1)S(1)}, u32[]{:S(2)}, u32[]{:S(2)}) %collective-permute-start.41) | collective-permute-done | bytes 262176 | tf_op jit(solution)/shard_map/ppermute | solution.py:42
  349.8 1.6 collective-permute-start.42
  351.5 1.3 slice_add_fusion.10
  352.8 1.6 collective-permute-start.46
  354.4 3.3 collective-permute-done.42
  357.7 1.7 collective-permute-start.43
  359.4 1.4 slice_add_fusion.5
  360.8 4.2 collective-permute-done.43
  365.6 2.1 collective-permute-start.54
  368.4 11.9 %collective-permute-done.49 = bf16[2,512,256]{2,1,0:T(8,128)(2,1)S(1)} collective-permute-done((bf16[2,512,256]{2,1,0:T(8,128)(2,1)S(1)}, bf16[2,512,256]{2,1,0:T(8,128)(2,1)S(1)}, u32[]{:S(2)}, u32[]{:S(2)}) %collective-permute-start.49) | collective-permute-done | bytes 524320 | tf_op jit(solution)/shard_map/ppermute | solution.py:42
  382.8 23.6 %collective-permute-done.50 = bf16[1,512,256]{2,1,0:T(8,128)(2,1)S(1)} collective-permute-done((bf16[1,512,256]{2,1,0:T(8,128)(2,1)S(1)}, bf16[1,512,256]{2,1,0:T(8,128)(2,1)S(1)}, u32[]{:S(2)}, u32[]{:S(2)}) %collective-permute-start.50) | collective-permute-done | bytes 262176 | tf_op jit(solution)/shard_map/ppermute | solution.py:42
  406.7 1.9 collective-permute-done.54
  408.8 1.6 collective-permute-start.55
  410.5 24.7 %collective-permute-done.55 = bf16[1,1056,256]{2,1,0:T(8,128)(2,1)S(1)} collective-permute-done((bf16[1,1056,256]{2,1,0:T(8,128)(2,1)S(1)}, bf16[1,1056,256]{2,1,0:T(8,128)(2,1)S(1)}, u32[]{:S(2)}, u32[]{:S(2)}) %collective-permute-start.55) | collective-permute-done | bytes 540704 | tf_op jit(solution)/shard_map/ppermute | solution.py:42
  (374 shorter events, 59.4 us)
Async XLA Ops:
  0.7 62.1 %copy-start = (bf16[1024,1024]{1,0:T(8,128)(2,1)S(1)}, bf16[1024,1024]{1,0:T(8,128)(2,1)}, u32[]{:S(2)}) copy-start(bf16[1024,1024]{1,0:T(8,128)(2,1)} %param.33) | copy-start | bytes 6291460
  4.9 23.5 %collective-permute-start.10 = (bf16[128,1024]{1,0:T(8,128)(2,1)S(1)}, bf16[128,1024]{1,0:T(8,128)(2,1)}, u32[]{:S(2)}, u32[]{:S(2)}) collective-permute-start(bf16[128,1024]{1,0:T(8,128)(2,1)S(1)} %pad_maximum_fusion.12.refs_2_.refs_10_.refs_5_.refs_13_), channel_id=1, source_target_pairs={{0,4},{1,5},{2,6},{3,7},{4,0},{5,1},{6,2},{7,3},{8,12},{9,13},{10,... | collective-permute-start | bytes 786440 | tf_op jit(solution)/shard_map/ppermute | solution.py:42
  7.9 31.7 %collective-permute-start.8 = (bf16[128,1024]{1,0:T(8,128)(2,1)S(1)}, bf16[128,1024]{1,0:T(8,128)(2,1)}, u32[]{:S(2)}, u32[]{:S(2)}) collective-permute-start(bf16[128,1024]{1,0:T(8,128)(2,1)S(1)} %pad_maximum_fusion.12.refs_2_.refs_10_.refs_5_.refs_13_), channel_id=1, source_target_pairs={{0,2},{1,3},{2,0},{3,1},{4,6},{5,7},{6,4},{7,5},{8,10},{9,11},{10,... | collective-permute-start | bytes 786440 | tf_op jit(solution)/shard_map/ppermute | solution.py:42
  13.3 26.2 %copy-start.82 = (s32[2]{0:T(128)S(1)}, s32[2]{0:T(128)}, u32[]{:S(2)}) copy-start(s32[2]{0:T(128)} %param.24) | copy-start | bytes 28
  13.3 15.2 %collective-permute-start.3 = (bf16[256,1024]{1,0:T(8,128)(2,1)S(1)}, bf16[256,1024]{1,0:T(8,128)(2,1)S(1)}, u32[]{:S(2)}, u32[]{:S(2)}) collective-permute-start(bf16[256,1024]{1,0:T(8,128)(2,1)S(1)} %pad_maximum_fusion.7.refs_3_.refs_11_.refs_8_.refs_16_), channel_id=1, source_target_pairs={{0,4},{1,5},{2,6},{3,7},{4,0},{5,1},{6,2},{7,3},{8,12},{9,13},{10,... | collective-permute-start | bytes 1572872 | tf_op jit(solution)/shard_map/ppermute | solution.py:42
  13.8 13.2 %collective-permute-start.1 = (bf16[256,1024]{1,0:T(8,128)(2,1)S(1)}, bf16[256,1024]{1,0:T(8,128)(2,1)}, u32[]{:S(2)}, u32[]{:S(2)}) collective-permute-start(bf16[256,1024]{1,0:T(8,128)(2,1)S(1)} %pad_maximum_fusion.7.refs_3_.refs_11_.refs_8_.refs_16_), channel_id=1, source_target_pairs={{0,2},{1,3},{2,0},{3,1},{4,6},{5,7},{6,4},{7,5},{8,10},{9,11},{10,... | collective-permute-start | bytes 1572872 | tf_op jit(solution)/shard_map/ppermute | solution.py:42
  13.9 34.7 %collective-permute-start = (bf16[256,1024]{1,0:T(8,128)(2,1)S(1)}, bf16[256,1024]{1,0:T(8,128)(2,1)}, u32[]{:S(2)}, u32[]{:S(2)}) collective-permute-start(bf16[256,1024]{1,0:T(8,128)(2,1)S(1)} %pad_maximum_fusion.7.refs_3_.refs_11_.refs_8_.refs_16_), channel_id=1, source_target_pairs={{0,1},{1,0},{2,3},{3,2},{4,5},{5,4},{6,7},{7,6},{8,9},{9,8},{10,11... | collective-permute-start | bytes 1572872 | tf_op jit(solution)/shard_map/ppermute | solution.py:42
  27.0 12.5 %collective-permute-start.5 = (bf16[256,1024]{1,0:T(8,128)(2,1)}, bf16[256,1024]{1,0:T(8,128)(2,1)}, u32[]{:S(2)}, u32[]{:S(2)}) collective-permute-start(bf16[256,1024]{1,0:T(8,128)(2,1)} %collective-permute-done.1.refs_5_.refs_13_.refs_10_.refs_18_), channel_id=1, source_target_pairs={{0,4},{1,5},{2,6},{3,7},{4,0},{5,1},{6,2},{7,3},{8,12},{9,13},{10,... | collective-permute-start | bytes 1572872 | tf_op jit(solution)/shard_map/ppermute | solution.py:42
  28.4 20.8 %collective-permute-start.2 = (bf16[256,1024]{1,0:T(8,128)(2,1)}, bf16[256,1024]{1,0:T(8,128)(2,1)}, u32[]{:S(2)}, u32[]{:S(2)}) collective-permute-start(bf16[256,1024]{1,0:T(8,128)(2,1)} %collective-permute-done.1.refs_5_.refs_13_.refs_10_.refs_18_), channel_id=1, source_target_pairs={{0,1},{1,0},{2,3},{3,2},{4,5},{5,4},{6,7},{7,6},{8,9},{9,8},{10,11... | collective-permute-start | bytes 1572872 | tf_op jit(solution)/shard_map/ppermute | solution.py:42
  28.5 21.2 %copy-start.5 = (bf16[256,1024]{1,0:T(8,128)(2,1)}, bf16[256,1024]{1,0:T(8,128)(2,1)S(1)}, u32[]{:S(2)}) copy-start(bf16[256,1024]{1,0:T(8,128)(2,1)S(1)} %collective-permute-done.3.refs_7_.refs_15_.refs_12_.refs_20_) | copy-start | bytes 1572868
  28.5 20.6 %collective-permute-start.4 = (bf16[256,1024]{1,0:T(8,128)(2,1)S(1)}, bf16[256,1024]{1,0:T(8,128)(2,1)}, u32[]{:S(2)}, u32[]{:S(2)}) collective-permute-start(bf16[256,1024]{1,0:T(8,128)(2,1)S(1)} %collective-permute-done.3.refs_7_.refs_15_.refs_12_.refs_20_), channel_id=1, source_target_pairs={{0,1},{1,0},{2,3},{3,2},{4,5},{5,4},{6,7},{7,6},{8,9},{9,8},{10,11... | collective-permute-start | bytes 1572872 | tf_op jit(solution)/shard_map/ppermute | solution.py:42
  39.5 10.2 %collective-permute-start.6 = (bf16[256,1024]{1,0:T(8,128)(2,1)}, bf16[256,1024]{1,0:T(8,128)(2,1)}, u32[]{:S(2)}, u32[]{:S(2)}) collective-permute-start(bf16[256,1024]{1,0:T(8,128)(2,1)} %collective-permute-done.5.refs_9_.refs_17_.refs_14_.refs_22_), channel_id=1, source_target_pairs={{0,1},{1,0},{2,3},{3,2},{4,5},{5,4},{6,7},{7,6},{8,9},{9,8},{10,11... | collective-permute-start | bytes 1572872 | tf_op jit(solution)/shard_map/ppermute | solution.py:42
  39.6 9.0 %collective-permute-start.12 = (bf16[128,1024]{1,0:T(8,128)(2,1)}, bf16[128,1024]{1,0:T(8,128)(2,1)}, u32[]{:S(2)}, u32[]{:S(2)}) collective-permute-start(bf16[128,1024]{1,0:T(8,128)(2,1)} %collective-permute-done.8.refs_4_.refs_12_.refs_7_.refs_15_), channel_id=1, source_target_pairs={{0,4},{1,5},{2,6},{3,7},{4,0},{5,1},{6,2},{7,3},{8,12},{9,13},{10,... | collective-permute-start | bytes 786440 | tf_op jit(solution)/shard_map/ppermute | solution.py:42
  41.9 18.9 %copy-start.49 = (f32[2,128,1024]{2,1,0:T(8,128)S(1)}, f32[2,128,1024]{2,1,0:T(8,128)}, u32[]{:S(2)}) copy-start(f32[2,128,1024]{2,1,0:T(8,128)} %copy-done.48) | copy-start | bytes 3145732
  42.0 33.1 %copy-start.31 = (bf16[256,1024]{1,0:T(8,128)(2,1)}, bf16[256,1024]{1,0:T(8,128)(2,1)S(1)}, u32[]{:S(2)}) copy-start(bf16[256,1024]{1,0:T(8,128)(2,1)S(1)} %bitcast_select_fusion.grad_low) | copy-start | bytes 1572868
  48.6 14.9 %collective-permute-start.7 = (bf16[128,1024]{1,0:T(8,128)(2,1)S(1)}, bf16[128,1024]{1,0:T(8,128)(2,1)S(1)}, u32[]{:S(2)}, u32[]{:S(2)}) collective-permute-start(bf16[128,1024]{1,0:T(8,128)(2,1)S(1)} %pad_maximum_fusion.12.refs_2_.refs_10_.refs_5_.refs_13_), channel_id=1, source_target_pairs={{0,1},{1,0},{2,3},{3,2},{4,5},{5,4},{6,7},{7,6},{8,9},{9,8},{10,11... | collective-permute-start | bytes 786440 | tf_op jit(solution)/shard_map/ppermute | solution.py:42
  48.6 15.0 %collective-permute-start.9 = (bf16[128,1024]{1,0:T(8,128)(2,1)}, bf16[128,1024]{1,0:T(8,128)(2,1)S(1)}, u32[]{:S(2)}, u32[]{:S(2)}) collective-permute-start(bf16[128,1024]{1,0:T(8,128)(2,1)} %collective-permute-done.8.refs_4_.refs_12_.refs_7_.refs_15_), channel_id=1, source_target_pairs={{0,1},{1,0},{2,3},{3,2},{4,5},{5,4},{6,7},{7,6},{8,9},{9,8},{10,11... | collective-permute-start | bytes 786440 | tf_op jit(solution)/shard_map/ppermute | solution.py:42
  49.1 14.4 %collective-permute-start.11 = (bf16[128,1024]{1,0:T(8,128)(2,1)}, bf16[128,1024]{1,0:T(8,128)(2,1)S(1)}, u32[]{:S(2)}, u32[]{:S(2)}) collective-permute-start(bf16[128,1024]{1,0:T(8,128)(2,1)} %collective-permute-done.10.refs_6_.refs_14_.refs_9_.refs_17_), channel_id=1, source_target_pairs={{0,1},{1,0},{2,3},{3,2},{4,5},{5,4},{6,7},{7,6},{8,9},{9,8},{10,11... | collective-permute-start | bytes 786440 | tf_op jit(solution)/shard_map/ppermute | solution.py:42
  49.2 14.4 %collective-permute-start.13 = (bf16[128,1024]{1,0:T(8,128)(2,1)}, bf16[128,1024]{1,0:T(8,128)(2,1)S(1)}, u32[]{:S(2)}, u32[]{:S(2)}) collective-permute-start(bf16[128,1024]{1,0:T(8,128)(2,1)} %collective-permute-done.12.refs_8_.refs_16_.refs_11_.refs_19_), channel_id=1, source_target_pairs={{0,1},{1,0},{2,3},{3,2},{4,5},{5,4},{6,7},{7,6},{8,9},{9,8},{10,11... | collective-permute-start | bytes 786440 | tf_op jit(solution)/shard_map/ppermute | solution.py:42
  75.0 44.8 %collective-permute-start.14 = (bf16[256,5120]{1,0:T(8,128)(2,1)}, bf16[256,5120]{1,0:T(8,128)(2,1)}, u32[]{:S(2)}, u32[]{:S(2)}) collective-permute-start(bf16[256,5120]{1,0:T(8,128)(2,1)} %get-tuple-element.154), channel_id=1, source_target_pairs={{0,1},{1,0},{2,3},{3,2},{4,5},{5,4},{6,7},{7,6},{8,9},{9,8},{10,11... | collective-permute-start | bytes 7864328 | tf_op jit(solution)/shard_map/ppermute | solution.py:42
  75.9 43.8 %collective-permute-start.15 = (bf16[256,512]{1,0:T(8,128)(2,1)}, bf16[256,512]{1,0:T(8,128)(2,1)}, u32[]{:S(2)}, u32[]{:S(2)}) collective-permute-start(bf16[256,512]{1,0:T(8,128)(2,1)} %get-tuple-element.210), channel_id=1, source_target_pairs={{0,1},{1,0},{2,3},{3,2},{4,5},{5,4},{6,7},{7,6},{8,9},{9,8},{10,11... | collective-permute-start | bytes 786440 | tf_op jit(solution)/shard_map/ppermute | solution.py:42
  104.2 15.6 %collective-permute-start.16 = (bf16[256,2816]{1,0:T(8,128)(2,1)S(1)}, bf16[256,2816]{1,0:T(8,128)(2,1)S(1)}, u32[]{:S(2)}, u32[]{:S(2)}) collective-permute-start(bf16[256,2816]{1,0:T(8,128)(2,1)S(1)} %get-tuple-element.55), channel_id=1, source_target_pairs={{0,1},{1,0},{2,3},{3,2},{4,5},{5,4},{6,7},{7,6},{8,9},{9,8},{10,11... | collective-permute-start | bytes 4325384 | tf_op jit(solution)/shard_map/ppermute | solution.py:42
  104.4 15.4 %collective-permute-start.17 = (bf16[256,2816]{1,0:T(8,128)(2,1)S(1)}, bf16[256,2816]{1,0:T(8,128)(2,1)S(1)}, u32[]{:S(2)}, u32[]{:S(2)}) collective-permute-start(bf16[256,2816]{1,0:T(8,128)(2,1)S(1)} %get-tuple-element.53.refs_0_), channel_id=1, source_target_pairs={{0,1},{1,0},{2,3},{3,2},{4,5},{5,4},{6,7},{7,6},{8,9},{9,8},{10,11... | collective-permute-start | bytes 4325384 | tf_op jit(solution)/shard_map/ppermute | solution.py:42
  115.9 36.0 %collective-permute-start.23 = (bf16[8,128,512]{2,1,0:T(8,128)(2,1)}, bf16[8,128,512]{2,1,0:T(8,128)(2,1)}, u32[]{:S(2)}, u32[]{:S(2)}) collective-permute-start(bf16[8,128,512]{2,1,0:T(8,128)(2,1)} %get-tuple-element.63), channel_id=1, source_target_pairs={{0,1},{1,0},{2,3},{3,2},{4,5},{5,4},{6,7},{7,6},{8,9},{9,8},{10,11... | collective-permute-start | bytes 3145736 | tf_op jit(solution)/shard_map/ppermute | solution.py:42
  151.3 33.3 %collective-permute-start.18 = (bf16[8,256,512]{2,1,0:T(8,128)(2,1)}, bf16[8,256,512]{2,1,0:T(8,128)(2,1)S(1)}, u32[]{:S(2)}, u32[]{:S(2)}) collective-permute-start(bf16[8,256,512]{2,1,0:T(8,128)(2,1)} %get-tuple-element.61), channel_id=1, source_target_pairs={{0,1},{1,0},{2,3},{3,2},{4,5},{5,4},{6,7},{7,6},{8,9},{9,8},{10,11... | collective-permute-start | bytes 6291464 | tf_op jit(solution)/shard_map/ppermute | solution.py:42
  153.3 17.3 %collective-permute-start.24 = (bf16[2,128,512]{2,1,0:T(8,128)(2,1)S(1)}, bf16[2,128,512]{2,1,0:T(8,128)(2,1)S(1)}, u32[]{:S(2)}, u32[]{:S(2)}) collective-permute-start(bf16[2,128,512]{2,1,0:T(8,128)(2,1)S(1)} %get-tuple-element.171), channel_id=1, source_target_pairs={{0,2},{1,3},{2,0},{3,1},{4,6},{5,7},{6,4},{7,5},{8,10},{9,11},{10,... | collective-permute-start | bytes 786440 | tf_op jit(solution)/shard_map/ppermute | solution.py:42
  161.6 18.6 %collective-permute-start.26 = (bf16[2,128,512]{2,1,0:T(8,128)(2,1)S(1)}, bf16[2,128,512]{2,1,0:T(8,128)(2,1)S(1)}, u32[]{:S(2)}, u32[]{:S(2)}) collective-permute-start(bf16[2,128,512]{2,1,0:T(8,128)(2,1)S(1)} %get-tuple-element.172), channel_id=1, source_target_pairs={{0,6},{1,7},{2,4},{3,5},{4,2},{5,3},{6,0},{7,1},{8,14},{9,15},{10,... | collective-permute-start | bytes 786440 | tf_op jit(solution)/shard_map/ppermute | solution.py:42
  168.2 13.3 %collective-permute-start.25 = (bf16[2,128,512]{2,1,0:T(8,128)(2,1)S(1)}, bf16[2,128,512]{2,1,0:T(8,128)(2,1)S(1)}, u32[]{:S(2)}, u32[]{:S(2)}) collective-permute-start(bf16[2,128,512]{2,1,0:T(8,128)(2,1)S(1)} %get-tuple-element.173), channel_id=1, source_target_pairs={{0,4},{1,5},{2,6},{3,7},{4,0},{5,1},{6,2},{7,3},{8,12},{9,13},{10,... | collective-permute-start | bytes 786440 | tf_op jit(solution)/shard_map/ppermute | solution.py:42
  182.7 1.4 collective-permute-start.27
  182.8 71.7 %collective-permute-start.36 = (bf16[8,496,256]{2,1,0:T(8,128)(2,1)}, bf16[8,496,256]{2,1,0:T(8,128)(2,1)}, u32[]{:S(2)}, u32[]{:S(2)}) collective-permute-start(bf16[8,496,256]{2,1,0:T(8,128)(2,1)} %get-tuple-element.56.refs_1_), channel_id=1, source_target_pairs={{0,2},{1,3},{2,0},{3,1},{4,6},{5,7},{6,4},{7,5},{8,10},{9,11},{10,... | collective-permute-start | bytes 6094856 | tf_op jit(solution)/shard_map/ppermute | solution.py:42
  186.5 55.0 %collective-permute-start.19 = (bf16[2,256,512]{2,1,0:T(8,128)(2,1)}, bf16[2,256,512]{2,1,0:T(8,128)(2,1)}, u32[]{:S(2)}, u32[]{:S(2)}) collective-permute-start(bf16[2,256,512]{2,1,0:T(8,128)(2,1)} %get-tuple-element.160), channel_id=1, source_target_pairs={{0,2},{1,3},{2,0},{3,1},{4,6},{5,7},{6,4},{7,5},{8,10},{9,11},{10,... | collective-permute-start | bytes 1572872 | tf_op jit(solution)/shard_map/ppermute | solution.py:42
  188.1 63.7 %collective-permute-start.21 = (bf16[2,256,512]{2,1,0:T(8,128)(2,1)}, bf16[2,256,512]{2,1,0:T(8,128)(2,1)}, u32[]{:S(2)}, u32[]{:S(2)}) collective-permute-start(bf16[2,256,512]{2,1,0:T(8,128)(2,1)} %get-tuple-element.161), channel_id=1, source_target_pairs={{0,6},{1,7},{2,4},{3,5},{4,2},{5,3},{6,0},{7,1},{8,14},{9,15},{10,... | collective-permute-start | bytes 1572872 | tf_op jit(solution)/shard_map/ppermute | solution.py:42
  188.4 53.0 %copy-start.23 = (bf16[128,1024]{1,0:T(8,128)(2,1)S(1)}, bf16[128,1024]{1,0:T(8,128)(2,1)}, u32[]{:S(2)}) copy-start(bf16[128,1024]{1,0:T(8,128)(2,1)} %copy-done.22) | copy-start | bytes 786436
  188.4 63.4 %collective-permute-start.20 = (bf16[2,256,512]{2,1,0:T(8,128)(2,1)}, bf16[2,256,512]{2,1,0:T(8,128)(2,1)}, u32[]{:S(2)}, u32[]{:S(2)}) collective-permute-start(bf16[2,256,512]{2,1,0:T(8,128)(2,1)} %get-tuple-element.162), channel_id=1, source_target_pairs={{0,4},{1,5},{2,6},{3,7},{4,0},{5,1},{6,2},{7,3},{8,12},{9,13},{10,... | collective-permute-start | bytes 1572872 | tf_op jit(solution)/shard_map/ppermute | solution.py:42
  191.6 71.9 %collective-permute-start.37 = (bf16[8,560,256]{2,1,0:T(8,128)(2,1)}, bf16[8,560,256]{2,1,0:T(8,128)(2,1)}, u32[]{:S(2)}, u32[]{:S(2)}) collective-permute-start(bf16[8,560,256]{2,1,0:T(8,128)(2,1)} %get-tuple-element.57.refs_2_), channel_id=1, source_target_pairs={{0,4},{1,5},{2,6},{3,7},{4,0},{5,1},{6,2},{7,3},{8,12},{9,13},{10,... | collective-permute-start | bytes 6881288 | tf_op jit(solution)/shard_map/ppermute | solution.py:42
  241.4 20.6 %collective-permute-start.34 = (bf16[128,1024]{1,0:T(8,128)(2,1)S(1)}, bf16[128,1024]{1,0:T(8,128)(2,1)S(1)}, u32[]{:S(2)}, u32[]{:S(2)}) collective-permute-start(bf16[128,1024]{1,0:T(8,128)(2,1)S(1)} %copy-done.23), channel_id=1, source_target_pairs={{0,1},{1,0},{2,3},{3,2},{4,5},{5,4},{6,7},{7,6},{8,9},{9,8},{10,11... | collective-permute-start | bytes 786440 | tf_op jit(solution)/shard_map/ppermute | solution.py:42
  251.8 10.4 %collective-permute-start.35 = (bf16[256,1536]{1,0:T(8,128)(2,1)}, bf16[256,1536]{1,0:T(8,128)(2,1)S(1)}, u32[]{:S(2)}, u32[]{:S(2)}) collective-permute-start(bf16[256,1536]{1,0:T(8,128)(2,1)} %pad_maximum_fusion.2), channel_id=1, source_target_pairs={{0,1},{1,0},{2,3},{3,2},{4,5},{5,4},{6,7},{7,6},{8,9},{9,8},{10,11... | collective-permute-start | bytes 2359304 | tf_op jit(solution)/shard_map/ppermute | solution.py:42
  251.8 44.2 %collective-permute-start.33 = (bf16[256,512]{1,0:T(8,128)(2,1)S(1)}, bf16[256,512]{1,0:T(8,128)(2,1)S(1)}, u32[]{:S(2)}, u32[]{:S(2)}) collective-permute-start(bf16[256,512]{1,0:T(8,128)(2,1)S(1)} %get-tuple-element.208), channel_id=1, source_target_pairs={{0,1},{1,0},{2,3},{3,2},{4,5},{5,4},{6,7},{7,6},{8,9},{9,8},{10,11... | collective-permute-start | bytes 786440 | tf_op jit(solution)/shard_map/ppermute | solution.py:42
  254.5 3.4 collective-permute-start.22
  257.9 60.7 %collective-permute-start.52 = (bf16[4,496,256]{2,1,0:T(8,128)(2,1)}, bf16[4,496,256]{2,1,0:T(8,128)(2,1)}, u32[]{:S(2)}, u32[]{:S(2)}) collective-permute-start(bf16[4,496,256]{2,1,0:T(8,128)(2,1)} %get-tuple-element.164), channel_id=1, source_target_pairs={{0,4},{1,5},{2,6},{3,7},{4,0},{5,1},{6,2},{7,3},{8,12},{9,13},{10,... | collective-permute-start | bytes 3047432 | tf_op jit(solution)/shard_map/ppermute | solution.py:42
  262.0 11.2 %collective-permute-start.28 = (f32[28,128]{1,0:T(8,128)S(1)}, f32[28,128]{1,0:T(8,128)S(1)}, u32[]{:S(2)}, u32[]{:S(2)}) collective-permute-start(f32[28,128]{1,0:T(8,128)S(1)} %maximum_bitcast_fusion), channel_id=1, source_target_pairs={{0,1},{1,0},{2,3},{3,2},{4,5},{5,4},{6,7},{7,6},{8,9},{9,8},{10,11... | collective-permute-start | bytes 43016 | tf_op jit(solution)/shard_map/ppermute | solution.py:42
  269.6 64.4 %collective-permute-start.47 = (bf16[8,256,256]{2,1,0:T(8,128)(2,1)}, bf16[8,256,256]{2,1,0:T(8,128)(2,1)}, u32[]{:S(2)}, u32[]{:S(2)}) collective-permute-start(bf16[8,256,256]{2,1,0:T(8,128)(2,1)} %get-tuple-element.73), channel_id=1, source_target_pairs={{0,4},{1,5},{2,6},{3,7},{4,0},{5,1},{6,2},{7,3},{8,12},{9,13},{10,... | collective-permute-start | bytes 3145736 | tf_op jit(solution)/shard_map/ppermute | solution.py:42
  270.9 80.5 %collective-permute-start.45 = (bf16[8,256,256]{2,1,0:T(8,128)(2,1)}, bf16[8,256,256]{2,1,0:T(8,128)(2,1)}, u32[]{:S(2)}, u32[]{:S(2)}) collective-permute-start(bf16[8,256,256]{2,1,0:T(8,128)(2,1)} %get-tuple-element.66.refs_6_), channel_id=1, source_target_pairs={{0,2},{1,3},{2,0},{3,1},{4,6},{5,7},{6,4},{7,5},{8,10},{9,11},{10,... | collective-permute-start | bytes 3145736 | tf_op jit(solution)/shard_map/ppermute | solution.py:42
  273.2 22.0 %collective-permute-start.29 = (f32[28,128]{1,0:T(8,128)S(1)}, f32[28,128]{1,0:T(8,128)S(1)}, u32[]{:S(2)}, u32[]{:S(2)}) collective-permute-start(f32[28,128]{1,0:T(8,128)S(1)} %fusion.36), channel_id=1, source_target_pairs={{0,2},{1,3},{2,0},{3,1},{4,6},{5,7},{6,4},{7,5},{8,10},{9,11},{10,... | collective-permute-start | bytes 43016 | tf_op jit(solution)/shard_map/ppermute | solution.py:42
  273.3 22.7 %copy-start.9 = (bf16[256,1024]{1,0:T(8,128)(2,1)S(1)}, bf16[256,1024]{1,0:T(8,128)(2,1)}, u32[]{:S(2)}) copy-start(bf16[256,1024]{1,0:T(8,128)(2,1)} %copy-done.8) | copy-start | bytes 1572868
  295.3 11.8 %collective-permute-start.30 = (f32[28,128]{1,0:T(8,128)S(1)}, f32[28,128]{1,0:T(8,128)S(1)}, u32[]{:S(2)}, u32[]{:S(2)}) collective-permute-start(f32[28,128]{1,0:T(8,128)S(1)} %fusion.79), channel_id=1, source_target_pairs={{0,4},{1,5},{2,6},{3,7},{4,0},{5,1},{6,2},{7,3},{8,12},{9,13},{10,... | collective-permute-start | bytes 43016 | tf_op jit(solution)/shard_map/ppermute | solution.py:42
  300.3 21.3 %collective-permute-start.38 = (bf16[8,128,256]{2,1,0:T(8,128)(2,1)}, bf16[8,128,256]{2,1,0:T(8,128)(2,1)}, u32[]{:S(2)}, u32[]{:S(2)}) collective-permute-start(bf16[8,128,256]{2,1,0:T(8,128)(2,1)} %get-tuple-element.68), channel_id=1, source_target_pairs={{0,2},{1,3},{2,0},{3,1},{4,6},{5,7},{6,4},{7,5},{8,10},{9,11},{10,... | collective-permute-start | bytes 1572872 | tf_op jit(solution)/shard_map/ppermute | solution.py:42
  307.0 3.7 collective-permute-start.31
  310.8 4.9 %collective-permute-start.32 = (f32[28,128]{1,0:T(8,128)S(1)}, f32[28,128]{1,0:T(8,128)S(1)}, u32[]{:S(2)}, u32[]{:S(2)}) collective-permute-start(f32[28,128]{1,0:T(8,128)S(1)} %add.285), channel_id=1, source_target_pairs={{0,16},{8,24},{16,0},{24,8},{1,17},{9,25},{17,1},{25,9},{2,18},{10... | collective-permute-start | bytes 43016 | tf_op jit(solution)/shard_map/ppermute | solution.py:42
  315.7 43.7 %collective-permute-start.53 = (bf16[4,560,256]{2,1,0:T(8,128)(2,1)}, bf16[4,560,256]{2,1,0:T(8,128)(2,1)}, u32[]{:S(2)}, u32[]{:S(2)}) collective-permute-start(bf16[4,560,256]{2,1,0:T(8,128)(2,1)} %get-tuple-element.159), channel_id=1, source_target_pairs={{0,2},{1,3},{2,0},{3,1},{4,6},{5,7},{6,4},{7,5},{8,10},{9,11},{10,... | collective-permute-start | bytes 3440648 | tf_op jit(solution)/shard_map/ppermute | solution.py:42
  318.5 14.6 %collective-permute-start.40 = (bf16[8,128,256]{2,1,0:T(8,128)(2,1)}, bf16[8,128,256]{2,1,0:T(8,128)(2,1)S(1)}, u32[]{:S(2)}, u32[]{:S(2)}) collective-permute-start(bf16[8,128,256]{2,1,0:T(8,128)(2,1)} %get-tuple-element.70), channel_id=1, source_target_pairs={{0,4},{1,5},{2,6},{3,7},{4,0},{5,1},{6,2},{7,3},{8,12},{9,13},{10,... | collective-permute-start | bytes 1572872 | tf_op jit(solution)/shard_map/ppermute | solution.py:42
  322.8 14.0 %collective-permute-start.39 = (bf16[4,128,256]{2,1,0:T(8,128)(2,1)S(1)}, bf16[4,128,256]{2,1,0:T(8,128)(2,1)S(1)}, u32[]{:S(2)}, u32[]{:S(2)}) collective-permute-start(bf16[4,128,256]{2,1,0:T(8,128)(2,1)S(1)} %get-tuple-element.185), channel_id=1, source_target_pairs={{0,4},{1,5},{2,6},{3,7},{4,0},{5,1},{6,2},{7,3},{8,12},{9,13},{10,... | collective-permute-start | bytes 786440 | tf_op jit(solution)/shard_map/ppermute | solution.py:42
  333.2 16.5 %collective-permute-start.41 = (bf16[4,128,256]{2,1,0:T(8,128)(2,1)S(1)}, bf16[4,128,256]{2,1,0:T(8,128)(2,1)S(1)}, u32[]{:S(2)}, u32[]{:S(2)}) collective-permute-start(bf16[4,128,256]{2,1,0:T(8,128)(2,1)S(1)} %get-tuple-element.187), channel_id=1, source_target_pairs={{0,2},{1,3},{2,0},{3,1},{4,6},{5,7},{6,4},{7,5},{8,10},{9,11},{10,... | collective-permute-start | bytes 786440 | tf_op jit(solution)/shard_map/ppermute | solution.py:42
  335.4 29.8 %collective-permute-start.48 = (bf16[4,256,256]{2,1,0:T(8,128)(2,1)S(1)}, bf16[4,256,256]{2,1,0:T(8,128)(2,1)S(1)}, u32[]{:S(2)}, u32[]{:S(2)}) collective-permute-start(bf16[4,256,256]{2,1,0:T(8,128)(2,1)S(1)} %get-tuple-element.170), channel_id=1, source_target_pairs={{0,2},{1,3},{2,0},{3,1},{4,6},{5,7},{6,4},{7,5},{8,10},{9,11},{10,... | collective-permute-start | bytes 1572872 | tf_op jit(solution)/shard_map/ppermute | solution.py:42
  349.8 7.8 %collective-permute-start.42 = (bf16[2,256,256]{2,1,0:T(8,128)(2,1)S(1)}, bf16[2,256,256]{2,1,0:T(8,128)(2,1)S(1)}, u32[]{:S(2)}, u32[]{:S(2)}) collective-permute-start(bf16[2,256,256]{2,1,0:T(8,128)(2,1)S(1)} %pad_maximum_fusion.13), channel_id=1, source_target_pairs={{0,8},{8,0},{16,24},{24,16},{1,9},{9,1},{17,25},{25,17},{2,10},{10... | collective-permute-start | bytes 786440 | tf_op jit(solution)/shard_map/ppermute | solution.py:42
  352.8 12.6 %collective-permute-start.46 = (bf16[4,256,256]{2,1,0:T(8,128)(2,1)S(1)}, bf16[4,256,256]{2,1,0:T(8,128)(2,1)S(1)}, u32[]{:S(2)}, u32[]{:S(2)}) collective-permute-start(bf16[4,256,256]{2,1,0:T(8,128)(2,1)S(1)} %get-tuple-element.168), channel_id=1, source_target_pairs={{0,4},{1,5},{2,6},{3,7},{4,0},{5,1},{6,2},{7,3},{8,12},{9,13},{10,... | collective-permute-start | bytes 1572872 | tf_op jit(solution)/shard_map/ppermute | solution.py:42
  357.7 7.3 %collective-permute-start.43 = (bf16[1,256,256]{2,1,0:T(8,128)(2,1)S(1)}, bf16[1,256,256]{2,1,0:T(8,128)(2,1)S(1)}, u32[]{:S(2)}, u32[]{:S(2)}) collective-permute-start(bf16[1,256,256]{2,1,0:T(8,128)(2,1)S(1)} %slice_add_fusion.22), channel_id=1, source_target_pairs={{0,16},{8,24},{16,0},{24,8},{1,17},{9,25},{17,1},{25,9},{2,18},{10... | collective-permute-start | bytes 393224 | tf_op jit(solution)/shard_map/ppermute | solution.py:42
  365.2 2.5 collective-permute-start.44
  365.4 14.8 %collective-permute-start.49 = (bf16[2,512,256]{2,1,0:T(8,128)(2,1)S(1)}, bf16[2,512,256]{2,1,0:T(8,128)(2,1)S(1)}, u32[]{:S(2)}, u32[]{:S(2)}) collective-permute-start(bf16[2,512,256]{2,1,0:T(8,128)(2,1)S(1)} %pad_maximum_fusion.8), channel_id=1, source_target_pairs={{0,8},{8,0},{16,24},{24,16},{1,9},{9,1},{17,25},{25,17},{2,10},{10... | collective-permute-start | bytes 1572872 | tf_op jit(solution)/shard_map/ppermute | solution.py:42
  365.6 43.0 %collective-permute-start.54 = (bf16[2,1056,256]{2,1,0:T(8,128)(2,1)S(1)}, bf16[2,1056,256]{2,1,0:T(8,128)(2,1)S(1)}, u32[]{:S(2)}, u32[]{:S(2)}) collective-permute-start(bf16[2,1056,256]{2,1,0:T(8,128)(2,1)S(1)} %pad_maximum_fusion), channel_id=1, source_target_pairs={{0,8},{8,0},{16,24},{24,16},{1,9},{9,1},{17,25},{25,17},{2,10},{10... | collective-permute-start | bytes 3244040 | tf_op jit(solution)/shard_map/ppermute | solution.py:42
  380.3 26.1 %collective-permute-start.50 = (bf16[1,512,256]{2,1,0:T(8,128)(2,1)S(1)}, bf16[1,512,256]{2,1,0:T(8,128)(2,1)S(1)}, u32[]{:S(2)}, u32[]{:S(2)}) collective-permute-start(bf16[1,512,256]{2,1,0:T(8,128)(2,1)S(1)} %slice_add_fusion.13), channel_id=1, source_target_pairs={{0,16},{8,24},{16,0},{24,8},{1,17},{9,25},{17,1},{25,9},{2,18},{10... | collective-permute-start | bytes 786440 | tf_op jit(solution)/shard_map/ppermute | solution.py:42
  406.7 3.7 collective-permute-start.51
  408.8 26.4 %collective-permute-start.55 = (bf16[1,1056,256]{2,1,0:T(8,128)(2,1)S(1)}, bf16[1,1056,256]{2,1,0:T(8,128)(2,1)S(1)}, u32[]{:S(2)}, u32[]{:S(2)}) collective-permute-start(bf16[1,1056,256]{2,1,0:T(8,128)(2,1)S(1)} %slice_add_fusion.6), channel_id=1, source_target_pairs={{0,16},{8,24},{16,0},{24,8},{1,17},{9,25},{17,1},{25,9},{2,18},{10... | collective-permute-start | bytes 1622024 | tf_op jit(solution)/shard_map/ppermute | solution.py:42
  435.8 3.4 collective-permute-start.56
  (76 other events, 377.7 us)

commit v3 on v2

--- a/solution.py
+++ b/solution.py
@@ -26,7 +26,7 @@
     scaled = incoming * gain
     inner = jnp.mean(scaled * value, axis=-1, keepdims=True)
     grad = rate * (scaled - value * (rate * rate * inner))
-    return grad, jnp.sum(incoming * value * rate, axis=0)
+    return grad, jnp.sum(incoming * value * rate, axis=0, keepdims=True)
 
 
 def mm(left, right):
@@ -52,6 +52,7 @@
 
 
 TILE = 256
+LIGHT = pl.CostEstimate(flops=1, bytes_accessed=1, transcendentals=0)
 
 
 def grad_order(flip):
@@ -122,41 +123,57 @@
         ],
         out_shape=shapes,
         compiler_params=pltpu.CompilerParams(vmem_limit_bytes=44 * 1024 * 1024),
-        cost_estimate=pl.CostEstimate(
-            flops=flops, bytes_accessed=total + 4 * sum(depth) * blocks * TILE, transcendentals=0
-        ),
+        cost_estimate=LIGHT,
     )(me, *arrays, *after)
 
 
 class Chain:
-    def __init__(self, outs):
-        self.keep, self.send = [outs[0], outs[2]], [outs[1], outs[3]]
-        self.orders = [grad_order(False), grad_order(True)]
-        self.level = 0
-        self.joint = False
-
-    def step(self):
-        order = self.orders[0]
-        joint = order[self.level][0] == "dp"
-        if joint and not self.joint:
-            self.keep = [jnp.concatenate(self.keep, axis=1)]
-            self.send = [jnp.concatenate(self.send, axis=1)]
-            self.joint = True
-        got = [
-            exchange(v, *self.orders[i][self.level]) for i, v in enumerate(self.send)
-        ]
+    def __init__(self, keep, send, orders, level=0):
+        self.keep, self.send, self.orders, self.level, self.got = keep, send, orders, level, None
+
+    @staticmethod
+    def of(outs):
+        return Chain([outs[0], outs[2]], [outs[1], outs[3]], [grad_order(False), grad_order(True)])
+
+    @staticmethod
+    def merged(chains):
+        level = chains[0].level
+        if chains[0].orders[0][level][0] == "dp":
+            keeps = [[k for c in chains for k in c.keep]]
+            sends = [[v for c in chains for v in c.send]]
+        else:
+            keeps = [list(k) for k in zip(*[c.keep for c in chains])]
+            sends = [list(v) for v in zip(*[c.send for c in chains])]
+        joined = [[jnp.concatenate(v, axis=1) for v in group] for group in (keeps, sends)]
+        return Chain(joined[0], joined[1], chains[0].orders[: len(keeps)], level)
+
+    def start(self, tokens=()):
+        if tokens:
+            self.send = tie(self.send, tokens)
+        self.got = [exchange(v, *self.orders[i][self.level]) for i, v in enumerate(self.send)]
         self.level += 1
+        return self.got
+
+    def add(self):
+        got, self.got = self.got, None
         half = got[0].shape[0] // 2
         if half:
             self.send = [k[half:] + g[half:] for k, g in zip(self.keep, got)]
             self.keep = [k[:half] + g[:half] for k, g in zip(self.keep, got)]
         else:
             self.keep = [k.astype(f32) + g.astype(f32) for k, g in zip(self.keep, got)]
-        return got
+
+    def to_dp(self):
+        while self.orders[0][self.level][0] == "seq":
+            self.start()
+            self.add()
 
     def finish(self):
+        if self.got is not None:
+            self.add()
         while self.level < len(self.orders[0]):
-            self.step()
+            self.start()
+            self.add()
         return self.keep[0][0]
 
 
@@ -199,29 +216,50 @@
     return value[:, :half], value[:, half:]
 
 
-def gather_seq(value):
-    pieces = {0: value}
-    for bit in bits_of(lax.axis_size("seq"), 2) + [1]:
-        for off in list(pieces):
-            pieces[off ^ bit] = exchange(pieces[off], "seq", bit)
-    return [pieces[off] for off in range(len(pieces))]
-
-
-def scatter_seq(mine, other):
+def tie(values, tokens):
+    done = lax.optimization_barrier((tuple(values), tuple(tokens)))
+    return list(done[0])
+
+
+def gather_start(value):
+    chips = lax.axis_size("seq") // 2
+    return [value] + [exchange(value, "seq", 2 * chip) for chip in range(1, chips)]
+
+
+def gather_finish(mine):
+    own = exchange(mine[0], "seq", 1)
+    rest = exchange(jnp.concatenate(mine[1:], axis=1), "seq", 1)
+    pieces = []
+    for chip, value in enumerate(mine):
+        pieces.append((value, 0))
+        pieces.append((own, 0) if chip == 0 else (rest, chip - 1))
+    return pieces
+
+
+def scatter_start(mine, other):
     got = exchange(other, "seq", 1)
-    size = mine.shape[0]
-    total = mine[:2].astype(f32) + got[:2].astype(f32)
-    for chip in range(1, size // 2):
-        part = mine[2 * chip : 2 * chip + 2].astype(f32) + got[2 * chip : 2 * chip + 2].astype(f32)
-        total = total + exchange(part.astype(bf16), "seq", 2 * chip).astype(f32)
+    parts = []
+    for chip in range(mine.shape[0] // 2):
+        pair = slice(2 * chip, 2 * chip + 2)
+        part = mine[pair].astype(f32) + got[pair].astype(f32)
+        parts.append(part if chip == 0 else part.astype(bf16))
+    return parts
+
+
+def scatter_send(parts):
+    return [exchange(part, "seq", 2 * (chip + 1)) for chip, part in enumerate(parts[1:])]
+
+
+def scatter_finish(part, arrived):
+    total = part
+    for value in arrived:
+        total = total + value.astype(f32)
     total = total.astype(bf16)
     return total[0], total[1], exchange(total[1], "seq", 1)
 
 
-def sum_all(value):
-    for axis, bit in [("seq", b) for b in bits_of(lax.axis_size("seq"), 1)] + [
-        ("dp", b) for b in bits_of(lax.axis_size("dp"), 1)
-    ]:
+def sum_over(value, steps):
+    for axis, bit in steps:
         value = value + exchange(value, axis, bit)
     return value
 
@@ -467,10 +505,12 @@
 
 def attend(query, pieces, info, seqs, line):
     tokens = query.shape[0] // seqs
-    count = pieces[0].shape[0] // seqs
+    arrays = [p[0] for p in pieces]
+    count = arrays[0].shape[0] // seqs
     n = len(pieces)
     steps = GROUPS // BATCH
-    wide, narrow = query.shape[1] // steps, pieces[0].shape[1] // 2 // steps
+    wide, narrow = query.shape[1] // steps, arrays[0].shape[1] // 2 // steps
+    places = [2 * steps * p[1] for p in pieces]
     head = narrow // BATCH
     biased = line is not None
     scratch = [pltpu.VMEM((BATCH, 1, 2 * tokens), f32)] * 2 + [
@@ -489,8 +529,8 @@
             grid=(steps,),
             in_specs=extra
             + [block_of(query, wide)]
-            + [block_of(p, narrow) for p in pieces]
-            + [block_of(p, narrow, steps) for p in pieces],
+            + [block_of(a, narrow, p) for a, p in zip(arrays, places)]
+            + [block_of(a, narrow, p + steps) for a, p in zip(arrays, places)],
             out_specs=[
                 block_of(query, wide),
                 pl.BlockSpec((1, BATCH * seqs, 2 * tokens), lambda i, info: (i, 0, 0)),
@@ -502,18 +542,18 @@
             jax.ShapeDtypeStruct((steps, BATCH * seqs, 2 * tokens), f32),
         ],
         compiler_params=pltpu.CompilerParams(vmem_limit_bytes=40 * 1024 * 1024),
-        cost_estimate=pl.CostEstimate(
-            flops=256 * pairs, bytes_accessed=4 * query.size + 2 * n * pieces[0].size, transcendentals=pairs
-        ),
-    )(info, *([line] if biased else []), query, *pieces, *pieces)
+        cost_estimate=LIGHT,
+    )(info, *([line] if biased else []), query, *arrays, *arrays)
 
 
 def attend_back(query, mixed, upstream, logsum, pieces, info, seqs, line, after=()):
     tokens = query.shape[0] // seqs
-    count = pieces[0].shape[0] // seqs
+    arrays = [p[0] for p in pieces]
+    count = arrays[0].shape[0] // seqs
     n = len(pieces)
     steps = GROUPS // BATCH
-    wide, narrow = query.shape[1] // steps, pieces[0].shape[1] // 2 // steps
+    wide, narrow = query.shape[1] // steps, arrays[0].shape[1] // 2 // steps
+    places = [2 * steps * p[1] for p in pieces]
     head = narrow // BATCH
     biased = line is not None
     scratch = [
@@ -540,24 +580,25 @@
             + extra
             + [block_of(query, wide)] * 3
             + [pl.BlockSpec((1, BATCH * seqs, 2 * tokens), lambda i, info: (i, 0, 0))]
-            + [block_of(p, narrow) for p in pieces]
-            + [block_of(p, narrow, steps) for p in pieces],
+            + [block_of(a, narrow, p) for a, p in zip(arrays, places)]
+            + [block_of(a, narrow, p + steps) for a, p in zip(arrays, places)],
             out_specs=[block_of(query, wide), part, part] + extra_out,
             scratch_shapes=scratch,
         ),
         out_shape=[jax.ShapeDtypeStruct(query.shape, bf16), part_shape, part_shape] + extra_shape,
         compiler_params=pltpu.CompilerParams(vmem_limit_bytes=44 * 1024 * 1024),
-        cost_estimate=pl.CostEstimate(
-            flops=640 * pairs, bytes_accessed=8 * query.size + 6 * n * pieces[0].size, transcendentals=pairs
-        ),
-    )(info, *after, *([line] if biased else []), query, mixed, upstream, logsum, *pieces, *pieces)
-
-
-def feed_kernel(core_ref, second, live, gain, normed, grad_low, gate_w, up_w, down_w, hidden, own, pair, outputs, grad, gain_grad, result, feed_in):
+        cost_estimate=LIGHT,
+    )(info, *after, *([line] if biased else []), query, mixed, upstream, logsum, *arrays, *arrays)
+
+
+def feed_kernel(core_ref, first_ref, mixed, out_w, live, gain, grad_low, gate_w, up_w, down_w, normed, hidden, own, pair, outputs, grad, mixed_grad, gain_grad, second, result, feed_in):
     step = pl.program_id(0)
 
     @pl.when(step == 0)
     def _():
+        value = first_ref[...] + mm(mixed[...], out_w[...])
+        second[...] = value
+        normed[...] = (value * norm_rate(value) * gain[...]).astype(bf16)
         result[...] = jnp.zeros(result.shape, f32)
         feed_in[...] = jnp.zeros(feed_in.shape, f32)
 
@@ -584,50 +625,111 @@
     def _():
         value = second[...]
         outputs[...] = ((value + result[...]) * live[...]).astype(bf16)
-        rate = norm_rate(value)
-        scaled = feed_in[...] * gain[...]
-        inner = jnp.mean(scaled * value, axis=-1, keepdims=True)
-        grad[...] = grad_low[...].astype(f32) + rate * (scaled - value * (rate * rate * inner))
-        gain_grad[...] = jnp.sum(feed_in[...] * value * rate, axis=0, keepdims=True)
-
-
-def feed_forward(core, second, live, gain, normed, grad_low, gate_weight, up_weight, down_weight):
-    tokens, width = second.shape
+        part, gained = norm_back(value, norm_rate(value), gain[...], feed_in[...])
+        total = grad_low[...].astype(f32) + part
+        grad[...] = total
+        gain_grad[...] = gained
+        mixed_grad[...] = nt(total.astype(bf16), out_w[...]).astype(bf16)
+
+
+def feed_forward(core, first, mixed, out_weight, live, gain, grad_low, gate_weight, up_weight, down_weight, after):
+    tokens, width = first.shape
     units = gate_weight.shape[1]
     whole = pl.BlockSpec((tokens, width), lambda i: (0, 0))
     line = pl.BlockSpec((1, width), lambda i: (0, 0))
     tall = pl.BlockSpec((width, TILE), lambda i: (0, i))
     part = pl.BlockSpec((tokens, TILE), lambda i: (0, i))
     part_shape = jax.ShapeDtypeStruct((tokens, units), bf16)
+    low_shape = jax.ShapeDtypeStruct((tokens, width), bf16)
+    skip = len(after)
+
+    def body(core_ref, *refs):
+        feed_kernel(core_ref, *refs[skip:])
+
     return pl.pallas_call(
-        feed_kernel,
+        body,
         grid=(units // TILE,),
-        in_specs=[
-            pl.BlockSpec(memory_space=pltpu.SMEM),
+        in_specs=[pl.BlockSpec(memory_space=pltpu.SMEM)]
+        + [pl.BlockSpec(memory_space=pl.ANY)] * skip
+        + [
             whole,
+            whole,
+            pl.BlockSpec(out_weight.shape, lambda i: (0, 0)),
             pl.BlockSpec((tokens, 1), lambda i: (0, 0)),
             line,
-            whole,
             whole,
             tall,
             tall,
             pl.BlockSpec((TILE, width), lambda i: (i, 0)),
         ],
-        out_specs=[part, part, part, whole, whole, line],
-        out_shape=[part_shape] * 3
+        out_specs=[whole, part, part, part, whole, whole, whole, line],
+        out_shape=[low_shape]
+        + [part_shape] * 3
         + [
-            jax.ShapeDtypeStruct((tokens, width), bf16),
+            low_shape,
             jax.ShapeDtypeStruct((tokens, width), f32),
+            low_shape,
             jax.ShapeDtypeStruct((1, width), f32),
         ],
-        scratch_shapes=[pltpu.VMEM((tokens, width), f32)] * 2,
+        scratch_shapes=[pltpu.VMEM((tokens, width), f32)] * 3,
+        compiler_params=pltpu.CompilerParams(vmem_limit_bytes=60 * 1024 * 1024),
+        cost_estimate=LIGHT,
+    )(core, *after, first, mixed, out_weight, live, gain.reshape(1, -1), grad_low, gate_weight, up_weight, down_weight)
+
+
+def between_kernel(x, mixed, out_w, gain, query_w, first, normed, query):
+    value = x[...].astype(f32) + mm(mixed[...], out_w[...])
+    first[...] = value
+    low = (value * norm_rate(value) * gain[...]).astype(bf16)
+    normed[...] = low
+    query[...] = mm(low, query_w[...]).astype(bf16)
+
+
+def between_back_kernel(core_ref, query_grad, query_w, second_grad, first_ref, gain, out_w, grad, mixed_grad, own, other, gain_grad):
+    value = first_ref[...]
+    part, gained = norm_back(value, norm_rate(value), gain[...], nt(query_grad[...], query_w[...]))
+    total = second_grad[...] + part
+    grad[...] = total
+    gain_grad[...] = gained
+    low = total.astype(bf16)
+    mixed_grad[...] = nt(low, out_w[...]).astype(bf16)
+    first = core_ref[0] == 0
+    half = low.shape[1] // 2
+    for i, array in enumerate((second_grad[...].astype(bf16), query_grad[...], low)):
+        left, right = array[:, :half], array[:, half:]
+        own[:, i * half : (i + 1) * half] = jnp.where(first, left, right)
+        other[:, i * half : (i + 1) * half] = jnp.where(first, right, left)
+
+
+def enter_back_kernel(core_ref, query_grad, half, rest, query_w, key_w, value_w, x, gain, first_grad, grad, gain_grad):
+    first = core_ref[0] == 0
+    keys = jnp.where(first, half[...], rest[...])
+    values = jnp.where(first, rest[...], half[...])
+    incoming = nt(query_grad[...], query_w[...]) + nt(keys, key_w[...]) + nt(values, value_w[...])
+    value = x[...].astype(f32)
+    part, gained = norm_back(value, norm_rate(value), gain[...], incoming)
+    grad[...] = first_grad[...] + part
+    gain_grad[...] = gained
+
+
+def whole_call(kernel, shapes, *arrays, core=None, after=()):
+    vmem = pl.BlockSpec(memory_space=pltpu.VMEM)
+    scalars = [] if core is None else [core]
+    skip, lead = len(after), len(scalars)
+
+    def body(*refs):
+        kernel(*refs[:lead], *refs[lead + skip :])
+
+    return pl.pallas_call(
+        body,
+        in_specs=[pl.BlockSpec(memory_space=pltpu.SMEM)] * lead
+        + [pl.BlockSpec(memory_space=pl.ANY)] * skip
+        + [vmem] * len(arrays),
+        out_specs=[vmem] * len(shapes),
+        out_shape=[jax.ShapeDtypeStruct(*shape) for shape in shapes],
         compiler_params=pltpu.CompilerParams(vmem_limit_bytes=32 * 1024 * 1024),
-        cost_estimate=pl.CostEstimate(
-            flops=12 * tokens * width * units,
-            bytes_accessed=6 * width * units + 6 * tokens * units + 14 * tokens * width,
-            transcendentals=tokens * units,
-        ),
-    )(core, second, live, gain.reshape(1, -1), normed, grad_low, gate_weight, up_weight, down_weight)
+        cost_estimate=LIGHT,
+    )(*scalars, *after, *arrays)
 
 
 def per_device(
@@ -682,11 +784,12 @@
     normed_self = (xf * rate_self * self_gain).astype(bf16)
     keys = mm(normed_self, self_key).astype(bf16)
     values = mm(normed_self, self_value).astype(bf16)
-    gathered = gather_seq(jnp.concatenate([keys, values], axis=1))
+    held_kv = gather_start(jnp.concatenate([keys, values], axis=1))
     memory_kv = jnp.concatenate(
         [mm(mem, cross_key).astype(bf16), mm(mem, cross_value).astype(bf16)], axis=1
     )
-    recalled = gather_seq(memory_kv)
+    gathered = gather_finish(held_kv)
+    held_memory = gather_start(tie([memory_kv], held_kv[1:])[0])
     query = mm(normed_self, self_query).astype(bf16)
 
     bucket_match = distance_bucket[:, None] == jnp.arange(buckets, dtype=jnp.int32)[None, :]
@@ -696,118 +799,178 @@
     line = line.reshape(GROUPS // BATCH, -1, length + 2 * tokens)
 
     self_mixed, self_logsum = attend(query, gathered, self_info, seqs, line)
-    first = xf + mm(self_mixed, self_out)
-    rate_cross = norm_rate(first)
-    normed_cross = (first * rate_cross * cross_gain).astype(bf16)
-    recall_query = mm(normed_cross, cross_query).astype(bf16)
+    recalled = gather_finish(held_memory[:1] + tie(held_memory[1:], [self_mixed]))
+    full, low_full, row = (x.shape, f32), (x.shape, bf16), ((1, width), f32)
+    first, normed_cross, recall_query = whole_call(
+        between_kernel,
+        [full, low_full, (query.shape, bf16)],
+        x,
+        self_mixed,
+        self_out,
+        cross_gain.reshape(1, -1),
+        cross_query,
+    )
     cross_mixed, cross_logsum = attend(recall_query, recalled, cross_info, seqs, None)
-    second = first + mm(cross_mixed, cross_out)
-    rate_feed = norm_rate(second)
-    normed_feed = (second * rate_feed * feed_gain).astype(bf16)
     core = (me % 2).astype(jnp.int32).reshape(1)
-    hidden, gu_own, gu_other, outputs, second_grad, feed_gain_grad = feed_forward(
-        core, second, live.astype(f32), feed_gain, normed_feed, grad_low, gate_weight, up_weight, down_weight
-    )
-    feed_gain_grad = feed_gain_grad.reshape(-1)
+    shared = jnp.concatenate([normed_self, self_mixed, normed_cross, cross_mixed], axis=1)
+    normed_feed, hidden, gu_own, gu_other, outputs, second_grad, cross_mixed_grad, feed_gain_grad = feed_forward(
+        core,
+        first,
+        cross_mixed,
+        cross_out,
+        live.astype(f32),
+        feed_gain,
+        grad_low,
+        gate_weight,
+        up_weight,
+        down_weight,
+        [shared],
+    )
     low_own, low_pair = pair_grad(*cut(grad_low))
     mem_pair = exchange(mem, "seq", 1)
-    shared = exchange(
-        jnp.concatenate([normed_self, self_mixed, normed_cross, cross_mixed, normed_feed], axis=1), "seq", 1
-    )
+    feed_pair = exchange(normed_feed, "seq", 1)
     hidden_pair = exchange(hidden, "seq", 1)
     gu_pair = exchange(gu_other, "seq", 1)
     hidden_cols = hidden.shape[1]
     tiles = hidden_cols // TILE
     cutting = tiles // 2
-    second_low = second_grad.astype(bf16)
-    cross_mixed_grad = mm_t(second_low, cross_out).astype(bf16)
-    recall_query_grad, kept, sent = attend_back(
-        recall_query, cross_mixed, cross_mixed_grad, cross_logsum, recalled, cross_info, seqs, None
-    )
-    gu_task = (((1, 0), (2, 4 * width), (5, 0), (6, 0)), width)
-    feed_chain = Chain(
+    gu_task = (((0, 0), (1, 0), (2, 0), (3, 0)), width)
+    feed_chain = Chain.of(
         group_grads(
-            [hidden, normed_feed, shared, low_own, low_pair, gu_own, gu_pair, hidden_pair],
+            [normed_feed, feed_pair, gu_own, gu_pair, hidden, hidden_pair, low_own, low_pair],
             [
+                (((4, 0), (5, 0), (6, 0), (7, 0)), hidden_cols, [(0, 0), (1, TILE)]),
                 gu_task + ([(0, j * TILE) for j in range(cutting)],),
                 gu_task + ([(1, j * TILE) for j in range(cutting, tiles)],),
-                (((0, 0), (7, 0), (3, 0), (4, 0)), hidden_cols, [(0, 0), (1, TILE)]),
             ],
-            [recall_query_grad],
         )
     )
-    early = list(feed_chain.send)
-    feed_first = feed_chain.step()
-    memory_half, memory_half_pair, memory_other = scatter_seq(kept, sent)
-    cross_in = mm_t(recall_query_grad, cross_query)
-    first_part, cross_gain_grad = norm_back(first, rate_cross, cross_gain, cross_in)
-    first_grad = second_grad + first_part
-    first_low = first_grad.astype(bf16)
-    self_mixed_grad = mm_t(first_low, self_out).astype(bf16)
-    halves = [core_halves(*cut(v)) for v in (second_low, recall_query_grad, first_low)]
-    grads_own = jnp.concatenate([h[0] for h in halves], axis=1)
-    grads_pair = exchange(jnp.concatenate([h[1] for h in halves], axis=1), "seq", 1)
-    memory_key_low, memory_value_low = core_halves(memory_half, memory_other)
-    memory_grad = mm_t(memory_key_low, cross_key) + mm_t(memory_value_low, cross_value)
-
-    query_grad, kept, sent, line_grad = attend_back(
-        query, self_mixed, self_mixed_grad, self_logsum, gathered, self_info, seqs, line, early
+    before = [feed_chain.send[0]]
+    feed_first = feed_chain.start()
+    recall_query_grad, memory_kept, memory_rest = attend_back(
+        recall_query, cross_mixed, cross_mixed_grad, cross_logsum, recalled, cross_info, seqs, None, before
+    )
+    first_grad, self_mixed_grad, grads_own, grads_other, cross_gain_grad = whole_call(
+        between_back_kernel,
+        [full, (query.shape, bf16), ((x.shape[0], 3 * width // 2), bf16), ((x.shape[0], 3 * width // 2), bf16), row],
+        recall_query_grad,
+        cross_query,
+        second_grad,
+        first,
+        cross_gain.reshape(1, -1),
+        self_out,
+        core=core,
+    )
+    query_grad, kept, rest, line_grad = attend_back(
+        query, self_mixed, self_mixed_grad, self_logsum, gathered, self_info, seqs, line
+    )
+    grads_pair = exchange(grads_other, "seq", 1)
+    shared = exchange(shared, "seq", 1)
+
+    memory_parts = scatter_start(memory_kept, memory_rest)
+    kept, rest, query_grad = tie([kept, rest, query_grad], feed_first + [grads_pair, shared])
+    key_parts = scatter_start(kept, rest)
+    feed_chain.add()
+    feed_second = feed_chain.start([kept])
+    query_own, query_other = core_halves(*cut(query_grad))
+    query_pair = exchange(query_other, "seq", 1)
+    two = [(0, 0), (1, TILE)]
+    out_chain = Chain.of(
+        group_grads(
+            [cross_mixed, normed_cross, self_mixed, shared, grads_own, grads_pair],
+            [
+                (((0, 0), (3, 3 * width), (4, 0), (5, 0)), width, two),
+                (((1, 0), (3, 2 * width), (4, width // 2), (5, width // 2)), width, two),
+                (((2, 0), (3, width), (4, width), (5, width)), width, two),
+            ],
+            [query_grad],
+        )
     )
     line_grad = line_grad.reshape(-1, line_grad.shape[2])[:, 2 * tokens :]
     table_grad = jnp.dot(line_grad, bucket_onehot, precision=highest, preferred_element_type=f32).T
-    key_half, key_half_pair, key_other = scatter_seq(kept, sent)
-    two = [(0, 0), (1, TILE)]
-    out_chain = Chain(
+    arrived = feed_second + memory_parts[1:] + key_parts[1:] + [query_pair, out_chain.send[0]]
+
+    key_sent = scatter_send(key_parts[:1] + tie(key_parts[1:], arrived))
+    memory_sent = scatter_send(memory_parts[:1] + tie(memory_parts[1:], arrived))
+    feed_chain.add()
+    feed_chain.to_dp()
+    feed_chain = Chain.merged([feed_chain])
+    feed_z = feed_chain.start(arrived)
+    key_half, key_half_pair, key_other = scatter_finish(key_parts[0], key_sent)
+    memory_half, memory_half_pair, memory_other = scatter_finish(memory_parts[0], memory_sent)
+    arrived = key_sent + memory_sent + feed_z
+
+    out_first = out_chain.start(arrived)
+    feed_chain.add()
+    feed_z = feed_chain.start(arrived)
+    in_chain = Chain.of(
         group_grads(
-            [cross_mixed, normed_cross, self_mixed, shared, mem, mem_pair, grads_own, grads_pair, memory_half, memory_half_pair],
+            [normed_self, shared, query_own, query_pair, key_half, key_half_pair, mem, mem_pair, memory_half, memory_half_pair],
             [
-                (((0, 0), (3, 3 * width), (6, 0), (7, 0)), width, two),
-                (((1, 0), (3, 2 * width), (6, width // 2), (7, width // 2)), width, two),
-                (((2, 0), (3, width), (6, width), (7, width)), width, two),
-                (((4, 0), (5, 0), (8, 0), (9, 0)), width, two),
-            ],
-            [query_grad] + feed_first,
-        )
-    )
-    query_own, query_pair = pair_grad(*cut(query_grad))
-    in_chain = Chain(
-        group_grads(
-            [normed_self, shared, query_own, query_pair, key_half, key_half_pair],
-            [
+                (((6, 0), (7, 0), (8, 0), (9, 0)), width, two),
                 (((0, 0), (1, 0), (2, 0), (3, 0)), width, two),
                 (((0, 0), (1, 0), (4, 0), (5, 0)), width, two),
             ],
-            [out_chain.send[0]],
+            arrived,
         )
     )
-    key_low, value_low = core_halves(key_half, key_other)
-    self_in = mm_t(query_grad, self_query) + mm_t(key_low, self_key) + mm_t(value_low, self_value)
-    input_part, self_gain_grad = norm_back(xf, rate_self, self_gain, self_in)
-    input_grad = first_grad + input_part
+    in_first = in_chain.start()
+    memory_key_low, memory_value_low = core_halves(memory_half, memory_other)
+    memory_grad = mm_t(memory_key_low, cross_key) + mm_t(memory_value_low, cross_value)
+    input_grad, self_gain_grad = whole_call(
+        enter_back_kernel,
+        [full, row],
+        query_grad,
+        key_half,
+        key_other,
+        self_query,
+        self_key,
+        self_value,
+        x,
+        self_gain.reshape(1, -1),
+        first_grad,
+        core=core,
+        after=[in_chain.send[0]],
+    )
     small = jnp.concatenate(
-        [self_gain_grad, cross_gain_grad, feed_gain_grad, table_grad.reshape(-1)]
+        [v.reshape(-1) for v in (self_gain_grad, cross_gain_grad, feed_gain_grad, table_grad)]
     ).reshape(-1, 128)
-    small = sum_all(small).reshape(-1)
+    small = sum_over(small, [("seq", 1)])
+    arrived = in_first + out_first + feed_z + [small]
+
+    dp_bits, seq_bits = bits_of(lax.axis_size("dp"), 1), bits_of(lax.axis_size("seq"), 2)
+    small = sum_over(tie([small], arrived)[0], [("dp", bit) for bit in dp_bits[:1]])
+    in_chain.add()
+    out_chain.add()
+    in_second = in_chain.start(arrived)
+    out_second = out_chain.start(arrived)
+    feed_chain.add()
+    arrived = in_second + out_second + [small]
+
+    out_chain.add()
+    in_chain.add()
+    out_chain.to_dp()
+    in_chain.to_dp()
+    last_chain = Chain.merged([out_chain, in_chain])
+    last_z = last_chain.start(arrived)
+    small = sum_over(tie([small], arrived)[0], [("dp", bit) for bit in dp_bits[1:]])
+    small = sum_over(small, [("seq", bit) for bit in seq_bits]).reshape(-1)
+    last_chain.add()
 
     blocks = 2 ** len(grad_order(False))
     narrow, broad = width // blocks, hidden_cols // blocks
     piece = feed_chain.finish()
-    middle = cutting * narrow
-    feed_tiles = jnp.concatenate([piece[:middle], piece[middle + broad : -broad]], axis=0)
-    down_tiles = jnp.concatenate([piece[middle : middle + broad], piece[-broad:]], axis=0)
+    middle = broad + cutting * narrow
+    gate_up = jnp.concatenate([piece[broad:middle], piece[middle + broad :]], axis=0)
+    down = jnp.concatenate([piece[:broad], piece[middle : middle + broad]], axis=0)
     (gate_out, up_out), down_out = swap_rows(
-        [
-            feed_tiles.reshape(tiles, narrow, TILE),
-            down_tiles.reshape(2, broad, TILE),
-        ]
-    )
-
-    def by_weight(piece):
-        stacks = piece.reshape(2, -1, narrow, TILE)
-        return swap_rows([stacks[:, i] for i in range(stacks.shape[1])])
-
-    cross_out_out, cross_query_out, self_out_out, cross_kv_out = by_weight(out_chain.finish())
-    self_query_out, self_kv_out = by_weight(in_chain.finish())
+        [gate_up.reshape(tiles, narrow, TILE), down.reshape(2, broad, TILE)]
+    )
+    piece = last_chain.finish().reshape(-1, narrow, TILE)
+    outs, ins = piece[:6].reshape(2, 3, narrow, TILE), piece[6:].reshape(2, 3, narrow, TILE)
+    cross_out_out, cross_query_out, self_out_out, cross_kv_out, self_query_out, self_kv_out = swap_rows(
+        [outs[:, i] for i in range(3)] + [ins[:, i] for i in range(3)]
+    )
 
     def joined(pair):
         return jnp.concatenate(pair, axis=1)

time: 447 us -> 369 us (0.83)
  waiting for transfers between devices: 217 us -> 153 us
  starting transfers between devices: 57.8 us -> 43.5 us
  matrix products: 14.9 us -> 4.17 us
  Pallas kernels: 82.9 us -> 90.4 us
  local copies, waits for them, and re-layouts: 32.1 us -> 39.5 us
    ppermute x57 -> x51, waiting for transfers between devices: 217 us -> 153 us  [exchange(): return lax.ppermute(value, axis, [(i, i ^ bit) for i in range(size)])]
    ppermute x57 -> x51, starting transfers between devices: 57.8 us -> 43.5 us  [exchange(): return lax.ppermute(value, axis, [(i, i ^ bit) for i in range(size)])]
    pallas_call x1 -> x4, Pallas kernels: 16.1 us -> 27.6 us  [the longest x1 21.8 us: feed_forward(): pl.pallas_call(body, grid=(units // TILE,), in_specs=[pl.BlockSpec(memory...]
    unnamed x170 -> x198, local copies, waits for them, and re-layouts: 18.7 us -> 25.7 us
    dot_general x8 -> x5, matrix products: 8.5 us -> 2.2 us  [mm(): return jnp.dot(left, right, preferred_element_type=f32)]
    add x24 -> x21, other arithmetic: 14.2 us -> 9.15 us  [the longest x12 8.57 us: add(): self.keep = [k[:half] + g[:half] for k, g in zip(self.keep, got)]]
  transfers between devices with their start and end apart: 57 -> 51, of which waited for: 19 -> 25; matrix products, arithmetic and copies ran while one was open for 12% -> 10% of each run, Pallas kernels for 17% -> 14%
where the time goes in v3:
time: 369 us; the launch traced here: 365 us
  waiting for transfers between devices  153 us (41%)
  Pallas kernels  90.4 us (24%)
  starting transfers between devices  43.5 us (12%)
  local copies, waits for them, and re-layouts  39.5 us (11%)
  other arithmetic  31.8 us (9%)
  matrix products  4.17 us (1%)
    ppermute x51, waiting for transfers between devices, exchange(): return lax.ppermute(value, axis, [(i, i ^ bit) for i in range(size)])  153 us
    ppermute x51, starting transfers between devices, exchange(): return lax.ppermute(value, axis, [(i, i ^ bit) for i in range(size)])  43.5 us
    pallas_call x2, Pallas kernels, attend_back(): pl.pallas_call(functools.partial(back_kernel, biased, seqs, tokens, count...  29.2 us
    unnamed x198, local copies, waits for them, and re-layouts  25.7 us
    pallas_call x1, Pallas kernels, feed_forward(): pl.pallas_call(body, grid=(units // TILE,), in_specs=[pl.BlockSpec(memory...  21.8 us
    pallas_call x3, Pallas kernels, group_grads(): pl.pallas_call(functools.partial(grads_kernel, chips, orders, full, len(a...  17.9 us
    pallas_call x2, Pallas kernels, attend(): pl.pallas_call(functools.partial(attend_kernel, biased, seqs, tokens, cou...  15.6 us
    add x12, other arithmetic, add(): self.keep = [k[:half] + g[:half] for k, g in zip(self.keep, got)]  8.57 us
  transfers between devices with their start and end apart: 51, of which 25 were waited for; matrix products, arithmetic and copies ran while one was open for 10% of the time, Pallas kernels for 14%

profile of v3, /device:TPU:0, one launch (start us, length us, event | category | flops | bytes accessed | tf_op | source)
XLA Modules:
  0.0 364.8 jit_solution(6131047118332929907)
XLA Ops:
  0.7 1.8 multiply_reduce_fusion
  6.6 2.9 collective-permute-start.1
  9.5 1.5 collective-permute-start.2
  11.7 10.7 %collective-permute-done.1.refs_5_.refs_13_.refs_8_.refs_16_ = bf16[256,1024]{1,0:T(8,128)(2,1)S(1)} collective-permute-done((bf16[256,1024]{1,0:T(8,128)(2,1)}, bf16[256,1024]{1,0:T(8,128)(2,1)S(1)}, u32[]{:S(2)}, u32[]{:S(2)}) %collective-permute-start.1) | collective-permute-done | bytes 524320 | tf_op jit(solution)/shard_map/ppermute | solution.py:42
  22.5 11.9 %collective-permute-done.2.refs_7_.refs_15_.refs_10_.refs_18_ = bf16[256,1024]{1,0:T(8,128)(2,1)S(1)} collective-permute-done((bf16[256,1024]{1,0:T(8,128)(2,1)}, bf16[256,1024]{1,0:T(8,128)(2,1)S(1)}, u32[]{:S(2)}, u32[]{:S(2)}) %collective-permute-start.2) | collective-permute-done | bytes 524320 | tf_op jit(solution)/shard_map/ppermute | solution.py:42
  41.5 1.5 collective-permute-start.8
  43.1 8.9 %shard_map.340 = (bf16[256,1024]{1,0:T(8,128)(2,1)S(1)}, f32[2,8,256]{2,1,0:T(8,128)S(1)}) custom-call(s32[3]{0:T(128)S(1)} %pad_add_fusion.refs_0_, f32[2,8,1280]{2,1,0:T(8,128)S(1)} %pad_bitcast_fusion.refs_1_, bf16[256,1024]{1,0:T(8,128)(2,1)S(1)} %convolution_convert_fusion.refs_2_, ...), custom_call_target="tpu_custom_call" | custom-call | flops 1 | bytes 1 | tf_op jit(solution)/shard_map/pallas_call | solution.py:525
  53.3 1.5 collective-permute-done.8.refs_8_.refs_16_.refs_12_.refs_20_
  57.2 2.0 copy.135
  60.0 2.0 bitcast_select_fusion.refs_6_
  62.0 1.6 copy-done.13
  63.6 1.6 copy-done.15
  67.2 1.5 shard_map.341
  69.7 6.7 %shard_map.342 = (bf16[256,1024]{1,0:T(8,128)(2,1)S(1)}, f32[2,8,256]{2,1,0:T(8,128)S(1)}) custom-call(s32[3]{0:T(128)S(1)} %pad_add_fusion.1.refs_0_, bf16[256,1024]{1,0:T(8,128)(2,1)S(1)} %get-tuple-element.87.refs_1_.refs_2_, bf16[128,1024]{1,0:T(8,128)(2,1)} %pad_maximum_fusion.13.refs_2_.refs_10_.refs_6_.refs_14_, ...), custom_call_target="tpu_custom_call" | custom-call | flops 1 | bytes 1 | tf_op jit(solution)/shard_map/pallas_call | solution.py:525
  76.5 1.5 pad_maximum_fusion.refs_0_
  78.0 21.8 %shard_map.343 = (bf16[256,1024]{1,0:T(8,128)(2,1)}, bf16[256,2816]{1,0:T(8,128)(2,1)}, bf16[256,2816]{1,0:T(8,128)(2,1)}, bf16[256,2816]{1,0:T(8,128)(2,1)}, bf...) custom-call(s32[1]{0:T(128)} %bitcast.core_ref.refs_0_, ...), custom_call_target="tpu_custom_call" | custom-call | flops 1 | bytes 1 | tf_op jit(solution)/shard_map/pallas_call | solution.py:649
  100.5 1.9 broadcast_select_fusion.2
  102.9 3.8 %collective-permute-done.14.refs_7_ = bf16[256,512]{1,0:T(8,128)(2,1)} collective-permute-done((bf16[256,512]{1,0:T(8,128)(2,1)}, bf16[256,512]{1,0:T(8,128)(2,1)}, u32[]{:S(2)}, u32[]{:S(2)}) %collective-permute-start.14) | collective-permute-done | bytes 262176 | tf_op jit(solution)/shard_map/ppermute | solution.py:42
  106.7 1.4 copy-done.56
  108.0 1.4 copy-done.57
  111.4 10.7 %shard_map.344 = (bf16[8,496,256]{2,1,0:T(8,128)(2,1)S(1)}, bf16[8,496,256]{2,1,0:T(8,128)(2,1)}, bf16[8,560,256]{2,1,0:T(8,128)(2,1)}, bf16[8,560,256]{2,1,0:T(8,128)(2,1)}) custom-call(s32[2]{0:T(128)S(1)} %pad_add_fusion.2.me_ref, bf16[256,1024]{1,0:T(8,128)(2,1)S(1)} %copy-done.71, bf16[256,1024]{1,0:T(8,128)(2,1)} %collective-permute-done.11.refs_1_, ...), custom_call_target="tpu_custom_call" | custom-call | flops 1 | bytes 1 | tf_op jit(solution)/shard_map/pallas_call | solution.py:114
  123.5 4.7 %collective-permute-start.16 = (bf16[8,560,256]{2,1,0:T(8,128)(2,1)}, bf16[8,560,256]{2,1,0:T(8,128)(2,1)}, u32[]{:S(2)}, u32[]{:S(2)}) collective-permute-start(bf16[8,560,256]{2,1,0:T(8,128)(2,1)} %get-tuple-element.109), channel_id=1, source_target_pairs={{0,4},{1,5},{2,6},{3,7},{4,0},{5,1},{6,2},{7,3},{8,12},{9,13},{10,... | collective-permute-start | bytes 6881288 | tf_op jit(solution)/shard_map/ppermute | solution.py:42
  129.3 1.6 copy-done.55
  130.9 10.2 %shard_map.345 = (bf16[256,1024]{1,0:T(8,128)(2,1)S(1)}, bf16[8,128,512]{2,1,0:T(8,128)(2,1)S(1)}, bf16[8,128,512]{2,1,0:T(8,128)(2,1)}) custom-call(s32[3]{0:T(128)S(1)} %pad_add_fusion.1.refs_0_, bf16[8,496,256]{2,1,0:T(8,128)(2,1)S(1)} %copy-done.55, bf16[256,1024]{1,0:T(8,128)(2,1)S(1)} %copy-done.47, bf16[256,1024]{1,0:T(8,128)(2,1)S(1)} %copy-done.26, ...), custom_call_target="tpu_custom_call" | custom-call | flops 1 | bytes 1 | tf_op jit(solution)/shard_map/pallas_call | solution.py:574
  145.2 2.9 shard_map.346
  148.7 19.0 %shard_map.347 = (bf16[256,1024]{1,0:T(8,128)(2,1)S(1)}, bf16[8,256,512]{2,1,0:T(8,128)(2,1)S(1)}, bf16[8,256,512]{2,1,0:T(8,128)(2,1)}, f32[2,8,1280]{2,1,0:T(8,128)S(1)}) custom-call(s32[3]{0:T(128)S(1)} %pad_add_fusion.refs_0_, f32[2,8,1280]{2,1,0:T(8,128)S(1)} %pad_bitcast_fusion.refs_1_, bf16[256,1024]{1,0:T(8,128)(2,1)S(1)} %copy-done.52, ...), custom_call_target="tpu_custom_call" | custom-call | flops 1 | bytes 1 | tf_op jit(solution)/shard_map/pallas_call | solution.py:574
  167.7 7.5 %collective-permute-done.15 = bf16[8,496,256]{2,1,0:T(8,128)(2,1)} collective-permute-done((bf16[8,496,256]{2,1,0:T(8,128)(2,1)}, bf16[8,496,256]{2,1,0:T(8,128)(2,1)}, u32[]{:S(2)}, u32[]{:S(2)}) %collective-permute-start.15) | collective-permute-done | bytes 2031648 | tf_op jit(solution)/shard_map/ppermute | solution.py:42
  175.2 3.5 collective-permute-done.16
  178.7 3.0 slice_add_fusion.2
  181.6 2.0 slice_add_fusion
  183.7 1.8 collective-permute-start.20
  186.8 1.4 add_convert_fusion.5
  188.6 2.9 shard_map.348
  191.6 17.3 %collective-permute-done.20 = bf16[4,496,256]{2,1,0:T(8,128)(2,1)} collective-permute-done((bf16[4,496,256]{2,1,0:T(8,128)(2,1)}, bf16[4,496,256]{2,1,0:T(8,128)(2,1)}, u32[]{:S(2)}, u32[]{:S(2)}) %collective-permute-start.20) | collective-permute-done | bytes 1015840 | tf_op jit(solution)/shard_map/ppermute | solution.py:42
  208.9 2.1 slice_add_fusion.7
  211.1 1.8 collective-permute-done.21
  213.9 1.8 add_convert_fusion.1
  217.1 2.8 collective-permute-start.29
  221.1 1.6 collective-permute-start.30
  222.9 2.9 collective-permute-done.27.refs_13_
  226.2 3.6 collective-permute-done.28.refs_14_
  229.8 1.8 collective-permute-start.25
  232.3 1.4 add_convert_fusion.4
  233.8 9.0 %collective-permute-done.23.refs_10_ = bf16[2,256,512]{2,1,0:T(8,128)(2,1)} collective-permute-done((bf16[2,256,512]{2,1,0:T(8,128)(2,1)}, bf16[2,256,512]{2,1,0:T(8,128)(2,1)}, u32[]{:S(2)}, u32[]{:S(2)}) %collective-permute-start.23) | collective-permute-done | bytes 524320 | tf_op jit(solution)/shard_map/ppermute | solution.py:42
  242.7 9.9 %collective-permute-done.24.refs_11_ = bf16[2,256,512]{2,1,0:T(8,128)(2,1)} collective-permute-done((bf16[2,256,512]{2,1,0:T(8,128)(2,1)}, bf16[2,256,512]{2,1,0:T(8,128)(2,1)}, u32[]{:S(2)}, u32[]{:S(2)}) %collective-permute-start.24) | collective-permute-done | bytes 524320 | tf_op jit(solution)/shard_map/ppermute | solution.py:42
  252.6 2.0 add_convert_fusion
  255.0 2.7 collective-permute-start.38
  257.7 4.2 %shard_map.349 = (bf16[8,192,256]{2,1,0:T(8,128)(2,1)S(1)}, bf16[8,192,256]{2,1,0:T(8,128)(2,1)S(1)}, bf16[8,192,256]{2,1,0:T(8,128)(2,1)S(1)}, bf16[8,192,256]{2,1,0:T(8,128)(2,1)S(1)}) custom-call(s32[2]{0:T(128)S(1)} %pad_add_fusion.2.me_ref, bf16[256,1024]{1,0:T(8,128)(2,1)S(1)} %copy-done.3, bf16[256,4096]{1,0:T(8,128)(2,1)} %copy-done.20, ...), custom_call_target="tpu_custom_call" | custom-call | flops 1 | bytes 1 | tf_op jit(solution)/shard_map/pallas_call | solution.py:114
  262.0 1.5 shard_map.350
  264.4 1.5 collective-permute-start.34
  266.3 1.4 collective-permute-start.36
  268.5 13.7 %collective-permute-done.38 = bf16[1,1056,256]{2,1,0:T(8,128)(2,1)S(1)} collective-permute-done((bf16[1,1056,256]{2,1,0:T(8,128)(2,1)S(1)}, bf16[1,1056,256]{2,1,0:T(8,128)(2,1)S(1)}, u32[]{:S(2)}, u32[]{:S(2)}) %collective-permute-start.38) | collective-permute-done | bytes 540704 | tf_op jit(solution)/shard_map/ppermute | solution.py:42
  282.6 3.7 %collective-permute-done.37 = bf16[8,192,256]{2,1,0:T(8,128)(2,1)S(1)} collective-permute-done((bf16[8,192,256]{2,1,0:T(8,128)(2,1)S(1)}, bf16[8,192,256]{2,1,0:T(8,128)(2,1)S(1)}, u32[]{:S(2)}, u32[]{:S(2)}) %collective-permute-start.37) | collective-permute-done | bytes 786464 | tf_op jit(solution)/shard_map/ppermute | solution.py:42
  286.3 14.7 %collective-permute-done.36 = bf16[8,192,256]{2,1,0:T(8,128)(2,1)S(1)} collective-permute-done((bf16[8,192,256]{2,1,0:T(8,128)(2,1)S(1)}, bf16[8,192,256]{2,1,0:T(8,128)(2,1)S(1)}, u32[]{:S(2)}, u32[]{:S(2)}) %collective-permute-start.36) | collective-permute-done | bytes 786464 | tf_op jit(solution)/shard_map/ppermute | solution.py:42
  304.0 1.6 collective-permute-start.39
  306.6 1.4 collective-permute-start.41
  308.0 6.2 %collective-permute-done.42 = bf16[4,192,256]{2,1,0:T(8,128)(2,1)S(1)} collective-permute-done((bf16[4,192,256]{2,1,0:T(8,128)(2,1)S(1)}, bf16[4,192,256]{2,1,0:T(8,128)(2,1)S(1)}, u32[]{:S(2)}, u32[]{:S(2)}) %collective-permute-start.42) | collective-permute-done | bytes 393248 | tf_op jit(solution)/shard_map/ppermute | solution.py:42
  314.7 6.1 %collective-permute-done.40 = bf16[4,192,256]{2,1,0:T(8,128)(2,1)S(1)} collective-permute-done((bf16[4,192,256]{2,1,0:T(8,128)(2,1)S(1)}, bf16[4,192,256]{2,1,0:T(8,128)(2,1)S(1)}, u32[]{:S(2)}, u32[]{:S(2)}) %collective-permute-start.40) | collective-permute-done | bytes 393248 | tf_op jit(solution)/shard_map/ppermute | solution.py:42
  321.4 1.6 collective-permute-start.47
  324.3 15.0 %collective-permute-done.47 = bf16[2,768,256]{2,1,0:T(8,128)(2,1)S(1)} collective-permute-done((bf16[2,768,256]{2,1,0:T(8,128)(2,1)S(1)}, bf16[2,768,256]{2,1,0:T(8,128)(2,1)S(1)}, u32[]{:S(2)}, u32[]{:S(2)}) %collective-permute-start.47) | collective-permute-done | bytes 786464 | tf_op jit(solution)/shard_map/ppermute | solution.py:42
  342.0 1.8 copy.179
  345.2 2.4 collective-permute-done.45
  347.6 1.4 collective-permute-start.46
  352.1 4.8 %collective-permute-done.48 = bf16[1,768,256]{2,1,0:T(8,128)(2,1)S(1)} collective-permute-done((bf16[1,768,256]{2,1,0:T(8,128)(2,1)S(1)}, bf16[1,768,256]{2,1,0:T(8,128)(2,1)S(1)}, u32[]{:S(2)}, u32[]{:S(2)}) %collective-permute-start.48) | collective-permute-done | bytes 393248 | tf_op jit(solution)/shard_map/ppermute | solution.py:42
  (368 shorter events, 59.8 us)
Async XLA Ops:
  4.0 34.4 %copy-start.1 = (bf16[256,1024]{1,0:T(8,128)(2,1)}, bf16[256,1024]{1,0:T(8,128)(2,1)S(1)}, u32[]{:S(2)}) copy-start(bf16[256,1024]{1,0:T(8,128)(2,1)S(1)} %multiply_convert_fusion.refs_0_) | copy-start | bytes 1572868
  6.6 15.9 %collective-permute-start.1 = (bf16[256,1024]{1,0:T(8,128)(2,1)}, bf16[256,1024]{1,0:T(8,128)(2,1)S(1)}, u32[]{:S(2)}, u32[]{:S(2)}) collective-permute-start(bf16[256,1024]{1,0:T(8,128)(2,1)} %pad_maximum_fusion.10.refs_3_.refs_11_.refs_6_.refs_14_), channel_id=1, source_target_pairs={{0,2},{1,3},{2,0},{3,1},{4,6},{5,7},{6,4},{7,5},{8,10},{9,11},{10,... | collective-permute-start | bytes 1572872 | tf_op jit(solution)/shard_map/ppermute | solution.py:42
  9.5 24.8 %collective-permute-start.2 = (bf16[256,1024]{1,0:T(8,128)(2,1)}, bf16[256,1024]{1,0:T(8,128)(2,1)S(1)}, u32[]{:S(2)}, u32[]{:S(2)}) collective-permute-start(bf16[256,1024]{1,0:T(8,128)(2,1)} %pad_maximum_fusion.10.refs_3_.refs_11_.refs_6_.refs_14_), channel_id=1, source_target_pairs={{0,4},{1,5},{2,6},{3,7},{4,0},{5,1},{6,2},{7,3},{8,12},{9,13},{10,... | collective-permute-start | bytes 1572872 | tf_op jit(solution)/shard_map/ppermute | solution.py:42
  11.0 23.3 %collective-permute-start.3 = (bf16[256,1024]{1,0:T(8,128)(2,1)}, bf16[256,1024]{1,0:T(8,128)(2,1)S(1)}, u32[]{:S(2)}, u32[]{:S(2)}) collective-permute-start(bf16[256,1024]{1,0:T(8,128)(2,1)} %pad_maximum_fusion.10.refs_3_.refs_11_.refs_6_.refs_14_), channel_id=1, source_target_pairs={{0,6},{1,7},{2,4},{3,5},{4,2},{5,3},{6,0},{7,1},{8,14},{9,15},{10,... | collective-permute-start | bytes 1572872 | tf_op jit(solution)/shard_map/ppermute | solution.py:42
  11.0 32.0 %collective-permute-start = (bf16[256,1024]{1,0:T(8,128)(2,1)}, bf16[256,1024]{1,0:T(8,128)(2,1)}, u32[]{:S(2)}, u32[]{:S(2)}) collective-permute-start(bf16[256,1024]{1,0:T(8,128)(2,1)} %pad_maximum_fusion.10.refs_3_.refs_11_.refs_6_.refs_14_), channel_id=1, source_target_pairs={{0,1},{1,0},{2,3},{3,2},{4,5},{5,4},{6,7},{7,6},{8,9},{9,8},{10,11... | collective-permute-start | bytes 1572872 | tf_op jit(solution)/shard_map/ppermute | solution.py:42
  11.4 25.5 %copy-start.42 = (bf16[128,1024]{1,0:T(8,128)(2,1)}, bf16[128,1024]{1,0:T(8,128)(2,1)S(1)}, u32[]{:S(2)}) copy-start(bf16[128,1024]{1,0:T(8,128)(2,1)S(1)} %bitcast_select_fusion.1.refs_6_) | copy-start | bytes 786436
  11.7 25.2 %copy-start.82 = (bf16[1024,512]{1,0:T(8,128)(2,1)S(1)}, bf16[1024,512]{1,0:T(8,128)(2,1)}, u32[]{:S(2)}) copy-start(bf16[1024,512]{1,0:T(8,128)(2,1)} %param.34) | copy-start | bytes 3145732
  36.9 6.1 %collective-permute-start.4 = (bf16[256,3072]{1,0:T(8,128)(2,1)S(1)}, bf16[256,3072]{1,0:T(8,128)(2,1)S(1)}, u32[]{:S(2)}, u32[]{:S(2)}) collective-permute-start(bf16[256,3072]{1,0:T(8,128)(2,1)S(1)} %pad_maximum_fusion.1), channel_id=1, source_target_pairs={{0,1},{1,0},{2,3},{3,2},{4,5},{5,4},{6,7},{7,6},{8,9},{9,8},{10,11... | collective-permute-start | bytes 4718600 | tf_op jit(solution)/shard_map/ppermute | solution.py:42
  39.3 13.4 %collective-permute-start.6 = (bf16[128,1024]{1,0:T(8,128)(2,1)}, bf16[128,1024]{1,0:T(8,128)(2,1)S(1)}, u32[]{:S(2)}, u32[]{:S(2)}) collective-permute-start(bf16[128,1024]{1,0:T(8,128)(2,1)} %pad_maximum_fusion.13.refs_2_.refs_10_.refs_6_.refs_14_), channel_id=1, source_target_pairs={{0,2},{1,3},{2,0},{3,1},{4,6},{5,7},{6,4},{7,5},{8,10},{9,11},{10,... | collective-permute-start | bytes 786440 | tf_op jit(solution)/shard_map/ppermute | solution.py:42
  40.7 12.6 %collective-permute-start.7 = (bf16[128,1024]{1,0:T(8,128)(2,1)}, bf16[128,1024]{1,0:T(8,128)(2,1)S(1)}, u32[]{:S(2)}, u32[]{:S(2)}) collective-permute-start(bf16[128,1024]{1,0:T(8,128)(2,1)} %pad_maximum_fusion.13.refs_2_.refs_10_.refs_6_.refs_14_), channel_id=1, source_target_pairs={{0,4},{1,5},{2,6},{3,7},{4,0},{5,1},{6,2},{7,3},{8,12},{9,13},{10,... | collective-permute-start | bytes 786440 | tf_op jit(solution)/shard_map/ppermute | solution.py:42
  41.5 13.3 %collective-permute-start.8 = (bf16[128,1024]{1,0:T(8,128)(2,1)}, bf16[128,1024]{1,0:T(8,128)(2,1)S(1)}, u32[]{:S(2)}, u32[]{:S(2)}) collective-permute-start(bf16[128,1024]{1,0:T(8,128)(2,1)} %pad_maximum_fusion.13.refs_2_.refs_10_.refs_6_.refs_14_), channel_id=1, source_target_pairs={{0,6},{1,7},{2,4},{3,5},{4,2},{5,3},{6,0},{7,1},{8,14},{9,15},{10,... | collective-permute-start | bytes 786440 | tf_op jit(solution)/shard_map/ppermute | solution.py:42
  56.5 13.2 %collective-permute-start.9 = (bf16[128,3072]{1,0:T(8,128)(2,1)}, bf16[128,3072]{1,0:T(8,128)(2,1)S(1)}, u32[]{:S(2)}, u32[]{:S(2)}) collective-permute-start(bf16[128,3072]{1,0:T(8,128)(2,1)} %pad_maximum_fusion.3), channel_id=1, source_target_pairs={{0,1},{1,0},{2,3},{3,2},{4,5},{5,4},{6,7},{7,6},{8,9},{9,8},{10,11... | collective-permute-start | bytes 2359304 | tf_op jit(solution)/shard_map/ppermute | solution.py:42
  56.6 13.1 %collective-permute-start.5 = (bf16[128,1024]{1,0:T(8,128)(2,1)}, bf16[128,1024]{1,0:T(8,128)(2,1)}, u32[]{:S(2)}, u32[]{:S(2)}) collective-permute-start(bf16[128,1024]{1,0:T(8,128)(2,1)} %pad_maximum_fusion.13.refs_2_.refs_10_.refs_6_.refs_14_), channel_id=1, source_target_pairs={{0,1},{1,0},{2,3},{3,2},{4,5},{5,4},{6,7},{7,6},{8,9},{9,8},{10,11... | collective-permute-start | bytes 786440 | tf_op jit(solution)/shard_map/ppermute | solution.py:42
  99.8 6.8 %collective-permute-start.12 = (bf16[256,2816]{1,0:T(8,128)(2,1)}, bf16[256,2816]{1,0:T(8,128)(2,1)}, u32[]{:S(2)}, u32[]{:S(2)}) collective-permute-start(bf16[256,2816]{1,0:T(8,128)(2,1)} %get-tuple-element.97), channel_id=1, source_target_pairs={{0,1},{1,0},{2,3},{3,2},{4,5},{5,4},{6,7},{7,6},{8,9},{9,8},{10,11... | collective-permute-start | bytes 4325384 | tf_op jit(solution)/shard_map/ppermute | solution.py:42
  99.9 6.7 %collective-permute-start.13 = (bf16[256,2816]{1,0:T(8,128)(2,1)}, bf16[256,2816]{1,0:T(8,128)(2,1)}, u32[]{:S(2)}, u32[]{:S(2)}) collective-permute-start(bf16[256,2816]{1,0:T(8,128)(2,1)} %get-tuple-element.98.refs_4_), channel_id=1, source_target_pairs={{0,1},{1,0},{2,3},{3,2},{4,5},{5,4},{6,7},{7,6},{8,9},{9,8},{10,11... | collective-permute-start | bytes 4325384 | tf_op jit(solution)/shard_map/ppermute | solution.py:42
  100.4 6.2 %collective-permute-start.11 = (bf16[256,1024]{1,0:T(8,128)(2,1)}, bf16[256,1024]{1,0:T(8,128)(2,1)}, u32[]{:S(2)}, u32[]{:S(2)}) collective-permute-start(bf16[256,1024]{1,0:T(8,128)(2,1)} %get-tuple-element.95.refs_0_), channel_id=1, source_target_pairs={{0,1},{1,0},{2,3},{3,2},{4,5},{5,4},{6,7},{7,6},{8,9},{9,8},{10,11... | collective-permute-start | bytes 1572872 | tf_op jit(solution)/shard_map/ppermute | solution.py:42
  102.4 4.3 %collective-permute-start.14 = (bf16[256,512]{1,0:T(8,128)(2,1)}, bf16[256,512]{1,0:T(8,128)(2,1)}, u32[]{:S(2)}, u32[]{:S(2)}) collective-permute-start(bf16[256,512]{1,0:T(8,128)(2,1)} %get-tuple-element.286), channel_id=1, source_target_pairs={{0,1},{1,0},{2,3},{3,2},{4,5},{5,4},{6,7},{7,6},{8,9},{9,8},{10,11... | collective-permute-start | bytes 786440 | tf_op jit(solution)/shard_map/ppermute | solution.py:42
  123.5 55.2 %collective-permute-start.16 = (bf16[8,560,256]{2,1,0:T(8,128)(2,1)}, bf16[8,560,256]{2,1,0:T(8,128)(2,1)}, u32[]{:S(2)}, u32[]{:S(2)}) collective-permute-start(bf16[8,560,256]{2,1,0:T(8,128)(2,1)} %get-tuple-element.109), channel_id=1, source_target_pairs={{0,4},{1,5},{2,6},{3,7},{4,0},{5,1},{6,2},{7,3},{8,12},{9,13},{10,... | collective-permute-start | bytes 6881288 | tf_op jit(solution)/shard_map/ppermute | solution.py:42
  128.2 39.5 %collective-permute-start.10 = (bf16[256,4096]{1,0:T(8,128)(2,1)}, bf16[256,4096]{1,0:T(8,128)(2,1)S(1)}, u32[]{:S(2)}, u32[]{:S(2)}) collective-permute-start(bf16[256,4096]{1,0:T(8,128)(2,1)} %pad_maximum_fusion.refs_0_), channel_id=1, source_target_pairs={{0,1},{1,0},{2,3},{3,2},{4,5},{5,4},{6,7},{7,6},{8,9},{9,8},{10,11... | collective-permute-start | bytes 6291464 | tf_op jit(solution)/shard_map/ppermute | solution.py:42
  128.2 47.0 %collective-permute-start.15 = (bf16[8,496,256]{2,1,0:T(8,128)(2,1)}, bf16[8,496,256]{2,1,0:T(8,128)(2,1)}, u32[]{:S(2)}, u32[]{:S(2)}) collective-permute-start(bf16[8,496,256]{2,1,0:T(8,128)(2,1)} %get-tuple-element.99.refs_1_), channel_id=1, source_target_pairs={{0,2},{1,3},{2,0},{3,1},{4,6},{5,7},{6,4},{7,5},{8,10},{9,11},{10,... | collective-permute-start | bytes 6094856 | tf_op jit(solution)/shard_map/ppermute | solution.py:42
  148.1 19.6 %copy-start.58 = (f32[256,1024]{1,0:T(8,128)}, f32[256,1024]{1,0:T(8,128)S(1)}, u32[]{:S(2)}) copy-start(f32[256,1024]{1,0:T(8,128)S(1)} %get-tuple-element.130.refs_10_) | copy-start | bytes 3145732
  148.1 19.6 %collective-permute-start.17 = (bf16[256,1536]{1,0:T(8,128)(2,1)}, bf16[256,1536]{1,0:T(8,128)(2,1)S(1)}, u32[]{:S(2)}, u32[]{:S(2)}) collective-permute-start(bf16[256,1536]{1,0:T(8,128)(2,1)} %get-tuple-element.110), channel_id=1, source_target_pairs={{0,1},{1,0},{2,3},{3,2},{4,5},{5,4},{6,7},{7,6},{8,9},{9,8},{10,11... | collective-permute-start | bytes 2359304 | tf_op jit(solution)/shard_map/ppermute | solution.py:42
  148.6 38.2 %collective-permute-start.22 = (bf16[8,128,512]{2,1,0:T(8,128)(2,1)}, bf16[8,128,512]{2,1,0:T(8,128)(2,1)}, u32[]{:S(2)}, u32[]{:S(2)}) collective-permute-start(bf16[8,128,512]{2,1,0:T(8,128)(2,1)} %get-tuple-element.119), channel_id=1, source_target_pairs={{0,1},{1,0},{2,3},{3,2},{4,5},{5,4},{6,7},{7,6},{8,9},{9,8},{10,11... | collective-permute-start | bytes 3145736 | tf_op jit(solution)/shard_map/ppermute | solution.py:42
  148.6 30.0 %copy-start.54 = (bf16[8,496,256]{2,1,0:T(8,128)(2,1)S(1)}, bf16[8,496,256]{2,1,0:T(8,128)(2,1)}, u32[]{:S(2)}) copy-start(bf16[8,496,256]{2,1,0:T(8,128)(2,1)} %copy-done.53) | copy-start | bytes 6094852
  167.7 46.2 %copy-start.48 = (bf16[8,256,512]{2,1,0:T(8,128)(2,1)}, bf16[8,256,512]{2,1,0:T(8,128)(2,1)S(1)}, u32[]{:S(2)}) copy-start(bf16[8,256,512]{2,1,0:T(8,128)(2,1)S(1)} %get-tuple-element.112) | copy-start | bytes 6291460
  167.7 20.9 %copy-start.20 = (bf16[256,4096]{1,0:T(8,128)(2,1)}, bf16[256,4096]{1,0:T(8,128)(2,1)S(1)}, u32[]{:S(2)}) copy-start(bf16[256,4096]{1,0:T(8,128)(2,1)S(1)} %collective-permute-done.10.refs_3_.refs_1_) | copy-start | bytes 6291460
  178.7 35.2 %collective-permute-start.19 = (bf16[8,256,512]{2,1,0:T(8,128)(2,1)}, bf16[8,256,512]{2,1,0:T(8,128)(2,1)S(1)}, u32[]{:S(2)}, u32[]{:S(2)}) collective-permute-start(bf16[8,256,512]{2,1,0:T(8,128)(2,1)} %get-tuple-element.113), channel_id=1, source_target_pairs={{0,1},{1,0},{2,3},{3,2},{4,5},{5,4},{6,7},{7,6},{8,9},{9,8},{10,11... | collective-permute-start | bytes 6291464 | tf_op jit(solution)/shard_map/ppermute | solution.py:42
  183.7 25.3 %collective-permute-start.20 = (bf16[4,496,256]{2,1,0:T(8,128)(2,1)}, bf16[4,496,256]{2,1,0:T(8,128)(2,1)}, u32[]{:S(2)}, u32[]{:S(2)}) collective-permute-start(bf16[4,496,256]{2,1,0:T(8,128)(2,1)} %get-tuple-element.116), channel_id=1, source_target_pairs={{0,4},{1,5},{2,6},{3,7},{4,0},{5,1},{6,2},{7,3},{8,12},{9,13},{10,... | collective-permute-start | bytes 3047432 | tf_op jit(solution)/shard_map/ppermute | solution.py:42
  185.5 27.4 %collective-permute-start.21 = (bf16[4,560,256]{2,1,0:T(8,128)(2,1)S(1)}, bf16[4,560,256]{2,1,0:T(8,128)(2,1)S(1)}, u32[]{:S(2)}, u32[]{:S(2)}) collective-permute-start(bf16[4,560,256]{2,1,0:T(8,128)(2,1)S(1)} %get-tuple-element.117), channel_id=1, source_target_pairs={{0,2},{1,3},{2,0},{3,1},{4,6},{5,7},{6,4},{7,5},{8,10},{9,11},{10,... | collective-permute-start | bytes 3440648 | tf_op jit(solution)/shard_map/ppermute | solution.py:42
  188.3 27.5 %collective-permute-start.18 = (bf16[256,512]{1,0:T(8,128)(2,1)S(1)}, bf16[256,512]{1,0:T(8,128)(2,1)S(1)}, u32[]{:S(2)}, u32[]{:S(2)}) collective-permute-start(bf16[256,512]{1,0:T(8,128)(2,1)S(1)} %get-tuple-element.284), channel_id=1, source_target_pairs={{0,1},{1,0},{2,3},{3,2},{4,5},{5,4},{6,7},{7,6},{8,9},{9,8},{10,11... | collective-permute-start | bytes 786440 | tf_op jit(solution)/shard_map/ppermute | solution.py:42
  191.5 22.3 %copy-start.64 = (bf16[8,192,256]{2,1,0:T(8,128)(2,1)}, bf16[8,192,256]{2,1,0:T(8,128)(2,1)S(1)}, u32[]{:S(2)}) copy-start(bf16[8,192,256]{2,1,0:T(8,128)(2,1)S(1)} %get-tuple-element.146) | copy-start | bytes 2359300
  191.5 22.3 %copy-start.66 = (bf16[8,192,256]{2,1,0:T(8,128)(2,1)}, bf16[8,192,256]{2,1,0:T(8,128)(2,1)S(1)}, u32[]{:S(2)}) copy-start(bf16[8,192,256]{2,1,0:T(8,128)(2,1)S(1)} %get-tuple-element.147) | copy-start | bytes 2359300
  191.5 22.3 %copy-start.76 = (bf16[8,192,256]{2,1,0:T(8,128)(2,1)}, bf16[8,192,256]{2,1,0:T(8,128)(2,1)S(1)}, u32[]{:S(2)}) copy-start(bf16[8,192,256]{2,1,0:T(8,128)(2,1)S(1)} %get-tuple-element.138) | copy-start | bytes 2359300
  191.6 22.3 %copy-start.78 = (bf16[8,192,256]{2,1,0:T(8,128)(2,1)}, bf16[8,192,256]{2,1,0:T(8,128)(2,1)S(1)}, u32[]{:S(2)}) copy-start(bf16[8,192,256]{2,1,0:T(8,128)(2,1)S(1)} %get-tuple-element.139) | copy-start | bytes 2359300
  216.5 9.3 %collective-permute-start.27 = (bf16[2,128,512]{2,1,0:T(8,128)(2,1)S(1)}, bf16[2,128,512]{2,1,0:T(8,128)(2,1)}, u32[]{:S(2)}, u32[]{:S(2)}) collective-permute-start(bf16[2,128,512]{2,1,0:T(8,128)(2,1)S(1)} %get-tuple-element.125), channel_id=1, source_target_pairs={{0,2},{1,3},{2,0},{3,1},{4,6},{5,7},{6,4},{7,5},{8,10},{9,11},{10,... | collective-permute-start | bytes 786440 | tf_op jit(solution)/shard_map/ppermute | solution.py:42
  216.8 13.0 %collective-permute-start.28 = (bf16[2,128,512]{2,1,0:T(8,128)(2,1)S(1)}, bf16[2,128,512]{2,1,0:T(8,128)(2,1)}, u32[]{:S(2)}, u32[]{:S(2)}) collective-permute-start(bf16[2,128,512]{2,1,0:T(8,128)(2,1)S(1)} %get-tuple-element.126), channel_id=1, source_target_pairs={{0,4},{1,5},{2,6},{3,7},{4,0},{5,1},{6,2},{7,3},{8,12},{9,13},{10,... | collective-permute-start | bytes 786440 | tf_op jit(solution)/shard_map/ppermute | solution.py:42
  217.1 15.1 %collective-permute-start.29 = (bf16[2,128,512]{2,1,0:T(8,128)(2,1)S(1)}, bf16[2,128,512]{2,1,0:T(8,128)(2,1)}, u32[]{:S(2)}, u32[]{:S(2)}) collective-permute-start(bf16[2,128,512]{2,1,0:T(8,128)(2,1)S(1)} %get-tuple-element.127), channel_id=1, source_target_pairs={{0,6},{1,7},{2,4},{3,5},{4,2},{5,3},{6,0},{7,1},{8,14},{9,15},{10,... | collective-permute-start | bytes 786440 | tf_op jit(solution)/shard_map/ppermute | solution.py:42
  221.1 33.7 %collective-permute-start.30 = (bf16[2,1056,256]{2,1,0:T(8,128)(2,1)}, bf16[2,1056,256]{2,1,0:T(8,128)(2,1)S(1)}, u32[]{:S(2)}, u32[]{:S(2)}) collective-permute-start(bf16[2,1056,256]{2,1,0:T(8,128)(2,1)} %pad_maximum_fusion.2), channel_id=1, source_target_pairs={{0,8},{8,0},{16,24},{24,16},{1,9},{9,1},{17,25},{25,17},{2,10},{10... | collective-permute-start | bytes 3244040 | tf_op jit(solution)/shard_map/ppermute | solution.py:42
  222.6 20.1 %collective-permute-start.23 = (bf16[2,256,512]{2,1,0:T(8,128)(2,1)}, bf16[2,256,512]{2,1,0:T(8,128)(2,1)}, u32[]{:S(2)}, u32[]{:S(2)}) collective-permute-start(bf16[2,256,512]{2,1,0:T(8,128)(2,1)} %get-tuple-element.122), channel_id=1, source_target_pairs={{0,2},{1,3},{2,0},{3,1},{4,6},{5,7},{6,4},{7,5},{8,10},{9,11},{10,... | collective-permute-start | bytes 1572872 | tf_op jit(solution)/shard_map/ppermute | solution.py:42
  225.8 26.8 %collective-permute-start.24 = (bf16[2,256,512]{2,1,0:T(8,128)(2,1)}, bf16[2,256,512]{2,1,0:T(8,128)(2,1)}, u32[]{:S(2)}, u32[]{:S(2)}) collective-permute-start(bf16[2,256,512]{2,1,0:T(8,128)(2,1)} %get-tuple-element.123), channel_id=1, source_target_pairs={{0,4},{1,5},{2,6},{3,7},{4,0},{5,1},{6,2},{7,3},{8,12},{9,13},{10,... | collective-permute-start | bytes 1572872 | tf_op jit(solution)/shard_map/ppermute | solution.py:42
  229.8 22.9 %collective-permute-start.25 = (bf16[2,256,512]{2,1,0:T(8,128)(2,1)}, bf16[2,256,512]{2,1,0:T(8,128)(2,1)}, u32[]{:S(2)}, u32[]{:S(2)}) collective-permute-start(bf16[2,256,512]{2,1,0:T(8,128)(2,1)} %get-tuple-element.124), channel_id=1, source_target_pairs={{0,6},{1,7},{2,4},{3,5},{4,2},{5,3},{6,0},{7,1},{8,14},{9,15},{10,... | collective-permute-start | bytes 1572872 | tf_op jit(solution)/shard_map/ppermute | solution.py:42
  232.2 25.4 %collective-permute-start.26 = (bf16[128,1024]{1,0:T(8,128)(2,1)S(1)}, bf16[128,1024]{1,0:T(8,128)(2,1)S(1)}, u32[]{:S(2)}, u32[]{:S(2)}) collective-permute-start(bf16[128,1024]{1,0:T(8,128)(2,1)S(1)} %copy-done.43), channel_id=1, source_target_pairs={{0,1},{1,0},{2,3},{3,2},{4,5},{5,4},{6,7},{7,6},{8,9},{9,8},{10,11... | collective-permute-start | bytes 786440 | tf_op jit(solution)/shard_map/ppermute | solution.py:42
  242.7 21.2 %collective-permute-start.32 = (bf16[128,512]{1,0:T(8,128)(2,1)S(1)}, bf16[128,512]{1,0:T(8,128)(2,1)S(1)}, u32[]{:S(2)}, u32[]{:S(2)}) collective-permute-start(bf16[128,512]{1,0:T(8,128)(2,1)S(1)} %get-tuple-element.308.refs_9_), channel_id=1, source_target_pairs={{0,1},{1,0},{2,3},{3,2},{4,5},{5,4},{6,7},{7,6},{8,9},{9,8},{10,11... | collective-permute-start | bytes 393224 | tf_op jit(solution)/shard_map/ppermute | solution.py:42
  254.7 7.3 %collective-permute-start.31 = (bf16[256,512]{1,0:T(8,128)(2,1)S(1)}, bf16[256,512]{1,0:T(8,128)(2,1)S(1)}, u32[]{:S(2)}, u32[]{:S(2)}) collective-permute-start(bf16[256,512]{1,0:T(8,128)(2,1)S(1)} %get-tuple-element.282.refs_5_), channel_id=1, source_target_pairs={{0,1},{1,0},{2,3},{3,2},{4,5},{5,4},{6,7},{7,6},{8,9},{9,8},{10,11... | collective-permute-start | bytes 786440 | tf_op jit(solution)/shard_map/ppermute | solution.py:42
  255.0 27.2 %collective-permute-start.38 = (bf16[1,1056,256]{2,1,0:T(8,128)(2,1)S(1)}, bf16[1,1056,256]{2,1,0:T(8,128)(2,1)S(1)}, u32[]{:S(2)}, u32[]{:S(2)}) collective-permute-start(bf16[1,1056,256]{2,1,0:T(8,128)(2,1)S(1)} %fusion.1), channel_id=1, source_target_pairs={{0,16},{8,24},{16,0},{24,8},{1,17},{9,25},{17,1},{25,9},{2,18},{10... | collective-permute-start | bytes 1622024 | tf_op jit(solution)/shard_map/ppermute | solution.py:42
  263.6 4.0 %collective-permute-start.33 = (f32[28,128]{1,0:T(8,128)S(1)}, f32[28,128]{1,0:T(8,128)S(1)}, u32[]{:S(2)}, u32[]{:S(2)}) collective-permute-start(f32[28,128]{1,0:T(8,128)S(1)} %maximum_bitcast_fusion), channel_id=1, source_target_pairs={{0,1},{1,0},{2,3},{3,2},{4,5},{5,4},{6,7},{7,6},{8,9},{9,8},{10,11... | collective-permute-start | bytes 43016 | tf_op jit(solution)/shard_map/ppermute | solution.py:42
  264.4 36.8 %collective-permute-start.34 = (bf16[8,192,256]{2,1,0:T(8,128)(2,1)S(1)}, bf16[8,192,256]{2,1,0:T(8,128)(2,1)S(1)}, u32[]{:S(2)}, u32[]{:S(2)}) collective-permute-start(bf16[8,192,256]{2,1,0:T(8,128)(2,1)S(1)} %get-tuple-element.129.refs_1_), channel_id=1, source_target_pairs={{0,2},{1,3},{2,0},{3,1},{4,6},{5,7},{6,4},{7,5},{8,10},{9,11},{10,... | collective-permute-start | bytes 2359304 | tf_op jit(solution)/shard_map/ppermute | solution.py:42
  265.9 20.4 %collective-permute-start.37 = (bf16[8,192,256]{2,1,0:T(8,128)(2,1)S(1)}, bf16[8,192,256]{2,1,0:T(8,128)(2,1)S(1)}, u32[]{:S(2)}, u32[]{:S(2)}) collective-permute-start(bf16[8,192,256]{2,1,0:T(8,128)(2,1)S(1)} %copy-done.79), channel_id=1, source_target_pairs={{0,4},{1,5},{2,6},{3,7},{4,0},{5,1},{6,2},{7,3},{8,12},{9,13},{10,... | collective-permute-start | bytes 2359304 | tf_op jit(solution)/shard_map/ppermute | solution.py:42
  266.3 34.8 %collective-permute-start.36 = (bf16[8,192,256]{2,1,0:T(8,128)(2,1)S(1)}, bf16[8,192,256]{2,1,0:T(8,128)(2,1)S(1)}, u32[]{:S(2)}, u32[]{:S(2)}) collective-permute-start(bf16[8,192,256]{2,1,0:T(8,128)(2,1)S(1)} %copy-done.77), channel_id=1, source_target_pairs={{0,2},{1,3},{2,0},{3,1},{4,6},{5,7},{6,4},{7,5},{8,10},{9,11},{10,... | collective-permute-start | bytes 2359304 | tf_op jit(solution)/shard_map/ppermute | solution.py:42
  267.6 34.5 %collective-permute-start.35 = (bf16[8,192,256]{2,1,0:T(8,128)(2,1)S(1)}, bf16[8,192,256]{2,1,0:T(8,128)(2,1)S(1)}, u32[]{:S(2)}, u32[]{:S(2)}) collective-permute-start(bf16[8,192,256]{2,1,0:T(8,128)(2,1)S(1)} %get-tuple-element.136), channel_id=1, source_target_pairs={{0,4},{1,5},{2,6},{3,7},{4,0},{5,1},{6,2},{7,3},{8,12},{9,13},{10,... | collective-permute-start | bytes 2359304 | tf_op jit(solution)/shard_map/ppermute | solution.py:42
  282.5 18.5 %copy-start.65 = (bf16[8,192,256]{2,1,0:T(8,128)(2,1)S(1)}, bf16[8,192,256]{2,1,0:T(8,128)(2,1)}, u32[]{:S(2)}) copy-start(bf16[8,192,256]{2,1,0:T(8,128)(2,1)} %copy-done.64) | copy-start | bytes 2359300
  302.2 12.1 %collective-permute-start.42 = (bf16[4,192,256]{2,1,0:T(8,128)(2,1)S(1)}, bf16[4,192,256]{2,1,0:T(8,128)(2,1)S(1)}, u32[]{:S(2)}, u32[]{:S(2)}) collective-permute-start(bf16[4,192,256]{2,1,0:T(8,128)(2,1)S(1)} %get-tuple-element.148), channel_id=1, source_target_pairs={{0,4},{1,5},{2,6},{3,7},{4,0},{5,1},{6,2},{7,3},{8,12},{9,13},{10,... | collective-permute-start | bytes 1179656 | tf_op jit(solution)/shard_map/ppermute | solution.py:42
  302.6 12.1 %collective-permute-start.43 = (bf16[4,192,256]{2,1,0:T(8,128)(2,1)S(1)}, bf16[4,192,256]{2,1,0:T(8,128)(2,1)S(1)}, u32[]{:S(2)}, u32[]{:S(2)}) collective-permute-start(bf16[4,192,256]{2,1,0:T(8,128)(2,1)S(1)} %get-tuple-element.149), channel_id=1, source_target_pairs={{0,2},{1,3},{2,0},{3,1},{4,6},{5,7},{6,4},{7,5},{8,10},{9,11},{10,... | collective-permute-start | bytes 1179656 | tf_op jit(solution)/shard_map/ppermute | solution.py:42
  304.0 4.1 %collective-permute-start.39 = (f32[28,128]{1,0:T(8,128)S(1)}, f32[28,128]{1,0:T(8,128)S(1)}, u32[]{:S(2)}, u32[]{:S(2)}) collective-permute-start(f32[28,128]{1,0:T(8,128)S(1)} %fusion.14), channel_id=1, source_target_pairs={{0,8},{8,0},{16,24},{24,16},{1,9},{9,1},{17,25},{25,17},{2,10},{10... | collective-permute-start | bytes 43016 | tf_op jit(solution)/shard_map/ppermute | solution.py:42
  305.7 15.1 %collective-permute-start.40 = (bf16[4,192,256]{2,1,0:T(8,128)(2,1)S(1)}, bf16[4,192,256]{2,1,0:T(8,128)(2,1)S(1)}, u32[]{:S(2)}, u32[]{:S(2)}) collective-permute-start(bf16[4,192,256]{2,1,0:T(8,128)(2,1)S(1)} %get-tuple-element.144), channel_id=1, source_target_pairs={{0,4},{1,5},{2,6},{3,7},{4,0},{5,1},{6,2},{7,3},{8,12},{9,13},{10,... | collective-permute-start | bytes 1179656 | tf_op jit(solution)/shard_map/ppermute | solution.py:42
  306.6 14.4 %collective-permute-start.41 = (bf16[4,192,256]{2,1,0:T(8,128)(2,1)S(1)}, bf16[4,192,256]{2,1,0:T(8,128)(2,1)S(1)}, u32[]{:S(2)}, u32[]{:S(2)}) collective-permute-start(bf16[4,192,256]{2,1,0:T(8,128)(2,1)S(1)} %get-tuple-element.145), channel_id=1, source_target_pairs={{0,2},{1,3},{2,0},{3,1},{4,6},{5,7},{6,4},{7,5},{8,10},{9,11},{10,... | collective-permute-start | bytes 1179656 | tf_op jit(solution)/shard_map/ppermute | solution.py:42
  321.4 17.9 %collective-permute-start.47 = (bf16[2,768,256]{2,1,0:T(8,128)(2,1)S(1)}, bf16[2,768,256]{2,1,0:T(8,128)(2,1)S(1)}, u32[]{:S(2)}, u32[]{:S(2)}) collective-permute-start(bf16[2,768,256]{2,1,0:T(8,128)(2,1)S(1)} %pad_maximum_fusion.5), channel_id=1, source_target_pairs={{0,8},{8,0},{16,24},{24,16},{1,9},{9,1},{17,25},{25,17},{2,10},{10... | collective-permute-start | bytes 2359304 | tf_op jit(solution)/shard_map/ppermute | solution.py:42
  323.3 17.1 %copy-start.83 = (bf16[1024,512]{1,0:T(8,128)(2,1)S(1)}, bf16[1024,512]{1,0:T(8,128)(2,1)}, u32[]{:S(2)}) copy-start(bf16[1024,512]{1,0:T(8,128)(2,1)} %param.34) | copy-start | bytes 3145732
  323.3 21.7 %collective-permute-start.50 = (bf16[528,256]{1,0:T(8,128)(2,1)S(1)}, bf16[528,256]{1,0:T(8,128)(2,1)S(1)}, u32[]{:S(2)}, u32[]{:S(2)}) collective-permute-start(bf16[528,256]{1,0:T(8,128)(2,1)S(1)} %select_convert_fusion), channel_id=1, source_target_pairs={{0,1},{1,0},{2,3},{3,2},{4,5},{5,4},{6,7},{7,6},{8,9},{9,8},{10,11... | collective-permute-start | bytes 811016 | tf_op jit(solution)/shard_map/ppermute | solution.py:42
  323.4 20.4 %collective-permute-start.44 = (f32[28,128]{1,0:T(8,128)S(1)}, f32[28,128]{1,0:T(8,128)S(1)}, u32[]{:S(2)}, u32[]{:S(2)}) collective-permute-start(f32[28,128]{1,0:T(8,128)S(1)} %add.233), channel_id=1, source_target_pairs={{0,16},{8,24},{16,0},{24,8},{1,17},{9,25},{17,1},{25,9},{2,18},{10... | collective-permute-start | bytes 43016 | tf_op jit(solution)/shard_map/ppermute | solution.py:42
  339.4 17.5 %collective-permute-start.48 = (bf16[1,768,256]{2,1,0:T(8,128)(2,1)S(1)}, bf16[1,768,256]{2,1,0:T(8,128)(2,1)S(1)}, u32[]{:S(2)}, u32[]{:S(2)}) collective-permute-start(bf16[1,768,256]{2,1,0:T(8,128)(2,1)S(1)} %slice_add_fusion.9), channel_id=1, source_target_pairs={{0,16},{8,24},{16,0},{24,8},{1,17},{9,25},{17,1},{25,9},{2,18},{10... | collective-permute-start | bytes 1179656 | tf_op jit(solution)/shard_map/ppermute | solution.py:42
  343.8 3.8 %collective-permute-start.45 = (f32[28,128]{1,0:T(8,128)S(1)}, f32[28,128]{1,0:T(8,128)S(1)}, u32[]{:S(2)}, u32[]{:S(2)}) collective-permute-start(f32[28,128]{1,0:T(8,128)S(1)} %add.238), channel_id=1, source_target_pairs={{0,2},{1,3},{2,0},{3,1},{4,6},{5,7},{6,4},{7,5},{8,10},{9,11},{10,... | collective-permute-start | bytes 43016 | tf_op jit(solution)/shard_map/ppermute | solution.py:42
  347.6 3.7 %collective-permute-start.46 = (f32[28,128]{1,0:T(8,128)S(1)}, f32[28,128]{1,0:T(8,128)S(1)}, u32[]{:S(2)}, u32[]{:S(2)}) collective-permute-start(f32[28,128]{1,0:T(8,128)S(1)} %add.239), channel_id=1, source_target_pairs={{0,4},{1,5},{2,6},{3,7},{4,0},{5,1},{6,2},{7,3},{8,12},{9,13},{10,... | collective-permute-start | bytes 43016 | tf_op jit(solution)/shard_map/ppermute | solution.py:42
  357.5 1.5 collective-permute-start.49
  (80 other events, 368.9 us)

commit v4 on v3

--- a/solution.py
+++ b/solution.py
@@ -93,6 +93,10 @@
             filled[stack] += rchip
 
 
+def block_whole(array):
+    return pl.BlockSpec(array.shape, lambda i: (0,) * len(array.shape))
+
+
 def group_grads(arrays, tasks, after=()):
     chips = lax.axis_size("seq") // 2
     orders = [grad_order(False), grad_order(True)]
@@ -107,22 +111,22 @@
         for stack, lane in tiles:
             depth[stack] += rows // blocks
     me = jnp.stack([lax.axis_index("dp"), lax.axis_index("seq") // 2]).astype(jnp.int32)
-    vmem = pl.BlockSpec(memory_space=pltpu.VMEM)
     most = max(t[2] for t in full)
     shapes = [jax.ShapeDtypeStruct((blocks // 2, depth[i // 2], TILE), bf16) for i in range(4)]
     total = arrays[0].dtype.itemsize * sum(a.size for a in arrays)
     return pl.pallas_call(
         functools.partial(grads_kernel, chips, orders, full, len(arrays), len(arrays) + len(after)),
+        grid=(1,),
         in_specs=[pl.BlockSpec(memory_space=pltpu.SMEM)]
-        + [vmem] * len(arrays)
+        + [block_whole(a) for a in arrays]
         + [pl.BlockSpec(memory_space=pl.ANY)] * len(after),
-        out_specs=[vmem] * 4,
+        out_specs=[block_whole(a) for a in shapes],
         scratch_shapes=[
             pltpu.VMEM((most, max(2 * t[1] for t in full)), bf16),
             pltpu.VMEM((blocks, most // blocks, TILE), f32),
         ],
         out_shape=shapes,
-        compiler_params=pltpu.CompilerParams(vmem_limit_bytes=44 * 1024 * 1024),
+        compiler_params=pltpu.CompilerParams(vmem_limit_bytes=60 * 1024 * 1024),
         cost_estimate=LIGHT,
     )(me, *arrays, *after)
 
@@ -168,37 +172,57 @@
             self.start()
             self.add()
 
-    def finish(self):
-        if self.got is not None:
-            self.add()
+    def last(self):
         while self.level < len(self.orders[0]):
+            if self.got is not None:
+                self.add()
             self.start()
-            self.add()
-        return self.keep[0][0]
-
-
-def swap_rows(parts):
-    lows, highs = [], []
-    for part in parts:
-        half = part.shape[1] // 2
-        lows.append(part[:, :half].reshape(-1, TILE))
-        highs.append(part[:, half:].reshape(-1, TILE))
-    low = jnp.concatenate(lows, axis=0)
-    high = jnp.concatenate(highs, axis=0)
-    mine, other = core_halves(low, high)
-    got = exchange(other.astype(bf16), "seq", 1).astype(f32)
-    first, second = core_halves(mine, got)
-    done = []
+        return self.keep[0], self.got[0]
+
+
+def split_kernel(tiles, core_ref, keep, got, mine, other):
+    first = core_ref[0] == 0
     start = 0
-    for part in parts:
-        tiles, half = part.shape[0], part.shape[1] // 2
-        pair = []
-        for whole in (first, second):
-            piece = whole[start : start + tiles * half].reshape(tiles, half, TILE)
-            pair.append(jnp.transpose(piece, (1, 0, 2)).reshape(half, tiles * TILE))
-        done.append(tuple(pair))
-        start += tiles * half
-    return done
+    for row, rows in tiles:
+        half = rows // 2
+        value = keep[0, row : row + rows].astype(f32) + got[0, row : row + rows].astype(f32)
+        low, high = value[:half], value[half:]
+        mine[start : start + half] = jnp.where(first, low, high)
+        other[start : start + half] = jnp.where(first, high, low).astype(bf16)
+        start += half
+
+
+def place_kernel(weights, core_ref, mine, got, *outs):
+    first = core_ref[0] == 0
+    for tiles, half, (left, shift_left), (right, shift_right) in weights:
+        for i, row in enumerate(tiles):
+            own, swapped = mine[row : row + half], got[row : row + half].astype(f32)
+            outs[left][:, shift_left + i * TILE : shift_left + (i + 1) * TILE] = jnp.where(first, own, swapped)
+            outs[right][:, shift_right + i * TILE : shift_right + (i + 1) * TILE] = jnp.where(first, swapped, own)
+
+
+def finish_rows(core, keep, got, tiles, weights, after=()):
+    starts, total = [], 0
+    listed = []
+    for rows in tiles:
+        listed.append((2 * total, rows))
+        starts.append(total)
+        total += rows // 2
+    mine, other = whole_call(
+        functools.partial(split_kernel, listed), [((total, TILE), f32), ((total, TILE), bf16)], keep, got, core=core, after=after
+    )
+    arrived = exchange(other, "seq", 1)
+    shapes, plan = [], []
+    for places, joined in weights:
+        half, columns = tiles[places[0]] // 2, len(places) * TILE
+        rows = [starts[p] for p in places]
+        if joined:
+            plan.append((rows, half, (len(shapes), 0), (len(shapes), columns)))
+            shapes.append(((half, 2 * columns), f32))
+        else:
+            plan.append((rows, half, (len(shapes), 0), (len(shapes) + 1, 0)))
+            shapes += [((half, columns), f32)] * 2
+    return whole_call(functools.partial(place_kernel, plan), shapes, mine, arrived, core=core)
 
 
 def core_halves(left, right):
@@ -255,7 +279,7 @@
     for value in arrived:
         total = total + value.astype(f32)
     total = total.astype(bf16)
-    return total[0], total[1], exchange(total[1], "seq", 1)
+    return total[0], total[1]
 
 
 def sum_over(value, steps):
@@ -542,7 +566,7 @@
             jax.ShapeDtypeStruct((steps, BATCH * seqs, 2 * tokens), f32),
         ],
         compiler_params=pltpu.CompilerParams(vmem_limit_bytes=40 * 1024 * 1024),
-        cost_estimate=LIGHT,
+        cost_estimate=pl.CostEstimate(flops=4096 * pairs, bytes_accessed=8 * query.size, transcendentals=pairs),
     )(info, *([line] if biased else []), query, *arrays, *arrays)
 
 
@@ -673,7 +697,9 @@
         ],
         scratch_shapes=[pltpu.VMEM((tokens, width), f32)] * 3,
         compiler_params=pltpu.CompilerParams(vmem_limit_bytes=60 * 1024 * 1024),
-        cost_estimate=LIGHT,
+        cost_estimate=pl.CostEstimate(
+            flops=12 * tokens * width * units, bytes_accessed=6 * width * units, transcendentals=tokens * units
+        ),
     )(core, *after, first, mixed, out_weight, live, gain.reshape(1, -1), grad_low, gate_weight, up_weight, down_weight)
 
 
@@ -712,7 +738,7 @@
     gain_grad[...] = gained
 
 
-def whole_call(kernel, shapes, *arrays, core=None, after=()):
+def whole_call(kernel, shapes, *arrays, core=None, after=(), stream=False):
     vmem = pl.BlockSpec(memory_space=pltpu.VMEM)
     scalars = [] if core is None else [core]
     skip, lead = len(after), len(scalars)
@@ -720,14 +746,19 @@
     def body(*refs):
         kernel(*refs[:lead], *refs[lead + skip :])
 
+    grid, spec, limit = {}, lambda array: vmem, 32
+    if stream:
+        grid, spec, limit = {"grid": (1,)}, block_whole, 60
+    outs = [jax.ShapeDtypeStruct(*shape) for shape in shapes]
     return pl.pallas_call(
         body,
+        **grid,
         in_specs=[pl.BlockSpec(memory_space=pltpu.SMEM)] * lead
         + [pl.BlockSpec(memory_space=pl.ANY)] * skip
-        + [vmem] * len(arrays),
-        out_specs=[vmem] * len(shapes),
-        out_shape=[jax.ShapeDtypeStruct(*shape) for shape in shapes],
-        compiler_params=pltpu.CompilerParams(vmem_limit_bytes=32 * 1024 * 1024),
+        + [spec(a) for a in arrays],
+        out_specs=[spec(a) for a in outs],
+        out_shape=outs,
+        compiler_params=pltpu.CompilerParams(vmem_limit_bytes=limit * 1024 * 1024),
         cost_estimate=LIGHT,
     )(*scalars, *after, *arrays)
 
@@ -791,12 +822,15 @@
     gathered = gather_finish(held_kv)
     held_memory = gather_start(tie([memory_kv], held_kv[1:])[0])
     query = mm(normed_self, self_query).astype(bf16)
-
     bucket_match = distance_bucket[:, None] == jnp.arange(buckets, dtype=jnp.int32)[None, :]
     bucket_onehot = bucket_match.astype(f32)
     line = jnp.dot(bias_table.T, bucket_onehot.T, precision=highest, preferred_element_type=f32)
     line = jnp.concatenate([jnp.full((line.shape[0], 2 * tokens), negative, f32), line], axis=1)
     line = line.reshape(GROUPS // BATCH, -1, length + 2 * tokens)
+    live_rows = live.astype(f32)
+    low_own, low_other = core_halves(*cut(grad_low))
+    low_pair = exchange(low_other, "seq", 1)
+    mem_pair = exchange(mem, "seq", 1)
 
     self_mixed, self_logsum = attend(query, gathered, self_info, seqs, line)
     recalled = gather_finish(held_memory[:1] + tie(held_memory[1:], [self_mixed]))
@@ -809,25 +843,23 @@
         self_out,
         cross_gain.reshape(1, -1),
         cross_query,
+        stream=True,
     )
     cross_mixed, cross_logsum = attend(recall_query, recalled, cross_info, seqs, None)
     core = (me % 2).astype(jnp.int32).reshape(1)
-    shared = jnp.concatenate([normed_self, self_mixed, normed_cross, cross_mixed], axis=1)
     normed_feed, hidden, gu_own, gu_other, outputs, second_grad, cross_mixed_grad, feed_gain_grad = feed_forward(
         core,
         first,
         cross_mixed,
         cross_out,
-        live.astype(f32),
+        live_rows,
         feed_gain,
         grad_low,
         gate_weight,
         up_weight,
         down_weight,
-        [shared],
-    )
-    low_own, low_pair = pair_grad(*cut(grad_low))
-    mem_pair = exchange(mem, "seq", 1)
+        [],
+    )
     feed_pair = exchange(normed_feed, "seq", 1)
     hidden_pair = exchange(hidden, "seq", 1)
     gu_pair = exchange(gu_other, "seq", 1)
@@ -865,6 +897,7 @@
         query, self_mixed, self_mixed_grad, self_logsum, gathered, self_info, seqs, line
     )
     grads_pair = exchange(grads_other, "seq", 1)
+    shared = jnp.concatenate(tie([normed_self, self_mixed, normed_cross, cross_mixed], before), axis=1)
     shared = exchange(shared, "seq", 1)
 
     memory_parts = scatter_start(memory_kept, memory_rest)
@@ -872,6 +905,7 @@
     key_parts = scatter_start(kept, rest)
     feed_chain.add()
     feed_second = feed_chain.start([kept])
+    memory_sent = scatter_send(memory_parts[:1] + tie(memory_parts[1:], [kept]))
     query_own, query_other = core_halves(*cut(query_grad))
     query_pair = exchange(query_other, "seq", 1)
     two = [(0, 0), (1, TILE)]
@@ -888,21 +922,18 @@
     )
     line_grad = line_grad.reshape(-1, line_grad.shape[2])[:, 2 * tokens :]
     table_grad = jnp.dot(line_grad, bucket_onehot, precision=highest, preferred_element_type=f32).T
-    arrived = feed_second + memory_parts[1:] + key_parts[1:] + [query_pair, out_chain.send[0]]
+    arrived = feed_second + key_parts[1:] + [query_pair, out_chain.send[0]]
 
     key_sent = scatter_send(key_parts[:1] + tie(key_parts[1:], arrived))
-    memory_sent = scatter_send(memory_parts[:1] + tie(memory_parts[1:], arrived))
+    out_first = out_chain.start(arrived)
     feed_chain.add()
     feed_chain.to_dp()
     feed_chain = Chain.merged([feed_chain])
     feed_z = feed_chain.start(arrived)
-    key_half, key_half_pair, key_other = scatter_finish(key_parts[0], key_sent)
-    memory_half, memory_half_pair, memory_other = scatter_finish(memory_parts[0], memory_sent)
-    arrived = key_sent + memory_sent + feed_z
-
-    out_first = out_chain.start(arrived)
-    feed_chain.add()
-    feed_z = feed_chain.start(arrived)
+    key_half, key_half_pair = scatter_finish(key_parts[0], key_sent)
+    memory_half, memory_half_pair = scatter_finish(memory_parts[0], memory_sent)
+    arrived = key_sent + memory_sent
+
     in_chain = Chain.of(
         group_grads(
             [normed_self, shared, query_own, query_pair, key_half, key_half_pair, mem, mem_pair, memory_half, memory_half_pair],
@@ -915,6 +946,9 @@
         )
     )
     in_first = in_chain.start()
+    key_other, memory_other = [
+        exchange(v, "seq", 1) for v in tie([key_half_pair, memory_half_pair], in_chain.send[:1])
+    ]
     memory_key_low, memory_value_low = core_halves(memory_half, memory_other)
     memory_grad = mm_t(memory_key_low, cross_key) + mm_t(memory_value_low, cross_value)
     input_grad, self_gain_grad = whole_call(
@@ -936,64 +970,71 @@
         [v.reshape(-1) for v in (self_gain_grad, cross_gain_grad, feed_gain_grad, table_grad)]
     ).reshape(-1, 128)
     small = sum_over(small, [("seq", 1)])
-    arrived = in_first + out_first + feed_z + [small]
+    out_chain.add()
+    out_second = out_chain.start(arrived + in_chain.send[:1])
+    feed_chain.add()
+    feed_z = feed_chain.start(arrived)
+    arrived = in_first + out_second + feed_z + [small]
 
     dp_bits, seq_bits = bits_of(lax.axis_size("dp"), 1), bits_of(lax.axis_size("seq"), 2)
-    small = sum_over(tie([small], arrived)[0], [("dp", bit) for bit in dp_bits[:1]])
+    small = sum_over(tie([small], arrived)[0], [("dp", bit) for bit in dp_bits])
     in_chain.add()
+    in_second = in_chain.start(arrived)
     out_chain.add()
-    in_second = in_chain.start(arrived)
-    out_second = out_chain.start(arrived)
-    feed_chain.add()
-    arrived = in_second + out_second + [small]
-
+    out_chain.to_dp()
+    out_chain = Chain.merged([out_chain])
+    out_z = out_chain.start(arrived)
+    arrived = in_second + out_z
+
+    in_chain.add()
+    in_chain.to_dp()
+    in_chain = Chain.merged([in_chain])
+    in_z = in_chain.start(arrived)
     out_chain.add()
-    in_chain.add()
-    out_chain.to_dp()
-    in_chain.to_dp()
-    last_chain = Chain.merged([out_chain, in_chain])
-    last_z = last_chain.start(arrived)
-    small = sum_over(tie([small], arrived)[0], [("dp", bit) for bit in dp_bits[1:]])
-    small = sum_over(small, [("seq", bit) for bit in seq_bits]).reshape(-1)
-    last_chain.add()
+    out_z = out_chain.start(arrived)
+    small = sum_over(tie([small], arrived)[0], [("seq", bit) for bit in seq_bits]).reshape(-1)
 
     blocks = 2 ** len(grad_order(False))
     narrow, broad = width // blocks, hidden_cols // blocks
-    piece = feed_chain.finish()
-    middle = broad + cutting * narrow
-    gate_up = jnp.concatenate([piece[broad:middle], piece[middle + broad :]], axis=0)
-    down = jnp.concatenate([piece[:broad], piece[middle : middle + broad]], axis=0)
-    (gate_out, up_out), down_out = swap_rows(
-        [gate_up.reshape(tiles, narrow, TILE), down.reshape(2, broad, TILE)]
-    )
-    piece = last_chain.finish().reshape(-1, narrow, TILE)
-    outs, ins = piece[:6].reshape(2, 3, narrow, TILE), piece[6:].reshape(2, 3, narrow, TILE)
-    cross_out_out, cross_query_out, self_out_out, cross_kv_out, self_query_out, self_kv_out = swap_rows(
-        [outs[:, i] for i in range(3)] + [ins[:, i] for i in range(3)]
-    )
-
-    def joined(pair):
-        return jnp.concatenate(pair, axis=1)
+    keep, got = feed_chain.last()
+    gate_out, up_out, down_out = finish_rows(
+        core,
+        keep,
+        got,
+        [broad] + [narrow] * cutting + [broad] + [narrow] * (tiles - cutting),
+        [
+            ([1 + j for j in range(cutting)] + [2 + j for j in range(cutting, tiles)], False),
+            ([0, 1 + cutting], True),
+        ],
+    )
+    keep, got = out_chain.last()
+    cross_out_out, cross_query_out, self_out_out = finish_rows(
+        core, keep, got, [narrow] * 6, [([0, 3], True), ([1, 4], True), ([2, 5], True)]
+    )
+    keep, got = in_chain.last()
+    cross_key_out, cross_value_out, self_query_out, self_key_out, self_value_out = finish_rows(
+        core, keep, got, [narrow] * 6, [([0, 3], False), ([1, 4], True), ([2, 5], False)]
+    )
 
     return (
         unflat(outputs),
         unflat(input_grad),
         unflat(memory_grad),
         small[:width],
-        joined(self_query_out),
-        self_kv_out[0],
-        self_kv_out[1],
-        joined(self_out_out),
+        self_query_out,
+        self_key_out,
+        self_value_out,
+        self_out_out,
         small[3 * width :].reshape(buckets, -1),
         small[width : 2 * width],
-        joined(cross_query_out),
-        cross_kv_out[0],
-        cross_kv_out[1],
-        joined(cross_out_out),
+        cross_query_out,
+        cross_key_out,
+        cross_value_out,
+        cross_out_out,
         small[2 * width : 3 * width],
         gate_out,
         up_out,
-        joined(down_out),
+        down_out,
     )
 
 

time: 369 us -> 349 us (0.946)
  waiting for transfers between devices: 153 us -> 129 us
  Pallas kernels: 90.4 us -> 103 us
  local copies, waits for them, and re-layouts: 39.5 us -> 27.8 us
    ppermute x51 -> x54, waiting for transfers between devices: 153 us -> 129 us  [exchange(): return lax.ppermute(value, axis, [(i, i ^ bit) for i in range(size)])]
    unnamed x198 -> x184, local copies, waits for them, and re-layouts: 25.7 us -> 16.4 us
    pallas_call x3, Pallas kernels: 17.9 us -> 24.7 us  [group_grads(): pl.pallas_call(functools.partial(grads_kernel, chips, orders, full, len(a...]
    pallas_call x3 -> x9, Pallas kernels: 5.85 us -> 12 us  [whole_call(): pl.pallas_call(body, **grid, in_specs=[pl.BlockSpec(memory_space=pltpu.SM...]
    add x2 -> x6, other arithmetic: 0.24 us -> 4.65 us  [add(): self.send = [k[half:] + g[half:] for k, g in zip(self.keep, got)]]
    reshape x16 -> x0, local copies, waits for them, and re-layouts: 4.13 us -> none  [swap_rows(): pair.append(jnp.transpose(piece, (1, 0, 2)).reshape(half, tiles * TILE))]
    ppermute x51 -> x54, starting transfers between devices: 43.5 us -> 42.1 us  [exchange(): return lax.ppermute(value, axis, [(i, i ^ bit) for i in range(size)])]
    add x12 -> x9, other arithmetic: 8.57 us -> 10 us  [add(): self.keep = [k[:half] + g[:half] for k, g in zip(self.keep, got)]]
  transfers between devices with their start and end apart: 51 -> 54, of which waited for: 25 -> 22; matrix products, arithmetic and copies ran while one was open for 10% -> 13% of each run, Pallas kernels for 14% -> 18%
where the time goes in v4:
time: 349 us; the launch traced here: 344 us
  waiting for transfers between devices  129 us (37%)
  Pallas kernels  103 us (30%)
  starting transfers between devices  42.1 us (12%)
  other arithmetic  35.1 us (10%)
  local copies, waits for them, and re-layouts  27.8 us (8%)
  matrix products  4.17 us (1%)
    ppermute x54, waiting for transfers between devices, exchange(): return lax.ppermute(value, axis, [(i, i ^ bit) for i in range(size)])  129 us
    ppermute x54, starting transfers between devices, exchange(): return lax.ppermute(value, axis, [(i, i ^ bit) for i in range(size)])  42.1 us
    pallas_call x2, Pallas kernels, attend_back(): pl.pallas_call(functools.partial(back_kernel, biased, seqs, tokens, count...  29.2 us
    pallas_call x3, Pallas kernels, group_grads(): pl.pallas_call(functools.partial(grads_kernel, chips, orders, full, len(a...  24.7 us
    pallas_call x1, Pallas kernels, feed_forward(): pl.pallas_call(body, grid=(units // TILE,), in_specs=[pl.BlockSpec(memory...  21.8 us
    unnamed x184, local copies, waits for them, and re-layouts  16.4 us
    pallas_call x2, Pallas kernels, attend(): pl.pallas_call(functools.partial(attend_kernel, biased, seqs, tokens, cou...  15.5 us
    pallas_call x9, Pallas kernels, whole_call(): pl.pallas_call(body, **grid, in_specs=[pl.BlockSpec(memory_space=pltpu.SM...  12 us
  transfers between devices with their start and end apart: 54, of which 22 were waited for; matrix products, arithmetic and copies ran while one was open for 13% of the time, Pallas kernels for 18%

profile of v4, /device:TPU:0, one launch (start us, length us, event | category | flops | bytes accessed | tf_op | source)
XLA Modules:
  0.0 343.9 jit_solution(1719316029593853580)
XLA Ops:
  0.7 1.8 multiply_reduce_fusion
  6.3 2.6 collective-permute-start.1
  8.9 1.5 collective-permute-start.3
  11.5 10.2 %collective-permute-done.1.refs_5_.refs_13_.refs_8_.refs_16_ = bf16[256,1024]{1,0:T(8,128)(2,1)S(1)} collective-permute-done((bf16[256,1024]{1,0:T(8,128)(2,1)S(1)}, bf16[256,1024]{1,0:T(8,128)(2,1)S(1)}, u32[]{:S(2)}, u32[]{:S(2)}) %collective-permute-start.1) | collective-permute-done | bytes 524320 | tf_op jit(solution)/shard_map/ppermute | solution.py:42
  21.6 12.3 %collective-permute-done.3.refs_9_.refs_17_.refs_12_.refs_20_ = bf16[256,1024]{1,0:T(8,128)(2,1)S(1)} collective-permute-done((bf16[256,1024]{1,0:T(8,128)(2,1)S(1)}, bf16[256,1024]{1,0:T(8,128)(2,1)S(1)}, u32[]{:S(2)}, u32[]{:S(2)}) %collective-permute-start.3) | collective-permute-done | bytes 524320 | tf_op jit(solution)/shard_map/ppermute | solution.py:42
  34.0 1.4 collective-permute-done.2.refs_7_.refs_15_.refs_10_.refs_18_
  40.7 1.6 collective-permute-start.6
  42.8 1.5 collective-permute-start.8
  44.3 8.8 %shard_map.340 = (bf16[256,1024]{1,0:T(8,128)(2,1)S(1)}, f32[2,8,256]{2,1,0:T(8,128)S(1)}) custom-call(s32[3]{0:T(128)S(1)} %pad_add_fusion.refs_0_, f32[2,8,1280]{2,1,0:T(8,128)S(1)} %pad_bitcast_fusion.refs_1_, bf16[256,1024]{1,0:T(8,128)(2,1)S(1)} %convolution_convert_fusion.refs_2_, ...), custom_call_target="tpu_custom_call" | custom-call | flops 17179869184 | bytes 2097152 | tf_op jit(solution)/shard_map/pallas_call | solution.py:549
  54.0 2.6 collective-permute-done.7.refs_6_.refs_14_.refs_10_.refs_18_
  59.8 2.0 copy.76
  61.7 2.0 bitcast_select_fusion.refs_5_
  63.7 4.9 %shard_map.341 = (f32[256,1024]{1,0:T(8,128)}, bf16[256,1024]{1,0:T(8,128)(2,1)}, bf16[256,1024]{1,0:T(8,128)(2,1)}) custom-call(bf16[256,1024]{1,0:T(8,128)(2,1)} %bitcast.78, bf16[256,1024]{1,0:T(8,128)(2,1)} %copy-done.5, bf16[1024,1024]{1,0:T(8,128)(2,1)} %refs_6_.4, f32[1,1024]{1,0:T(1,128)} %bitcast.86, bf16[1024,1024]{1,0:T(8,128)(2,1)} %refs_2_.5), custom_call_target="tpu_custom_call" | custom-call | flops 1 | bytes 1 | tf_op jit(solution)/shard_map/pallas_call | solution.py:753
  70.6 6.7 %shard_map.342 = (bf16[256,1024]{1,0:T(8,128)(2,1)S(1)}, f32[2,8,256]{2,1,0:T(8,128)S(1)}) custom-call(s32[3]{0:T(128)S(1)} %pad_add_fusion.1.refs_0_, bf16[256,1024]{1,0:T(8,128)(2,1)S(1)} %copy-done.50, bf16[128,1024]{1,0:T(8,128)(2,1)} %pad_maximum_fusion.8.refs_2_.refs_10_.refs_6_.refs_14_, ...), custom_call_target="tpu_custom_call" | custom-call | flops 8589934592 | bytes 2097152 | tf_op jit(solution)/shard_map/pallas_call | solution.py:549
  78.1 21.8 %shard_map.343 = (bf16[256,1024]{1,0:T(8,128)(2,1)}, bf16[256,2816]{1,0:T(8,128)(2,1)}, bf16[256,2816]{1,0:T(8,128)(2,1)}, bf16[256,2816]{1,0:T(8,128)(2,1)}, bf...) custom-call(s32[1]{0:T(128)} %bitcast.core_ref.refs_0_, ...), custom_call_target="tpu_custom_call" | custom-call | flops 8858370048 | bytes 17301504 | tf_op jit(solution)/shard_map/pallas_call | solution.py:673
  100.6 1.9 broadcast_select_fusion.2
  103.5 3.2 collective-permute-done.13.refs_7_
  106.8 12.1 %shard_map.344 = (bf16[8,496,256]{2,1,0:T(8,128)(2,1)}, bf16[8,496,256]{2,1,0:T(8,128)(2,1)}, bf16[8,560,256]{2,1,0:T(8,128)(2,1)}, bf16[8,560,256]{2,1,0:T(8,128)(2,1)}) custom-call(s32[2]{0:T(128)} %pad_add_fusion.2.me_ref, bf16[256,1024]{1,0:T(8,128)(2,1)} %get-tuple-element.120.refs_0_, bf16[256,1024]{1,0:T(8,128)(2,1)} %collective-permute-done.10.refs_1_, ...), custom_call_target="tpu_custom_call" | custom-call | flops 1 | bytes 1 | tf_op jit(solution)/shard_map/pallas_call | solution.py:117
  118.9 3.0 collective-permute-start.16
  122.0 2.9 pad_maximum_fusion
  126.0 10.3 %shard_map.345 = (bf16[256,1024]{1,0:T(8,128)(2,1)S(1)}, bf16[8,128,512]{2,1,0:T(8,128)(2,1)S(1)}, bf16[8,128,512]{2,1,0:T(8,128)(2,1)}) custom-call(s32[3]{0:T(128)S(1)} %pad_add_fusion.1.refs_0_, bf16[8,496,256]{2,1,0:T(8,128)(2,1)S(1)} %copy-done.40, bf16[256,1024]{1,0:T(8,128)(2,1)S(1)} %copy-done.51, bf16[256,1024]{1,0:T(8,128)(2,1)S(1)} %copy-done.21, ...), custom_call_target="tpu_custom_call" | custom-call | flops 1 | bytes 1 | tf_op jit(solution)/shard_map/pallas_call | solution.py:598
  136.3 1.8 shard_map.346
  139.6 19.0 %shard_map.347 = (bf16[256,1024]{1,0:T(8,128)(2,1)S(1)}, bf16[8,256,512]{2,1,0:T(8,128)(2,1)S(1)}, bf16[8,256,512]{2,1,0:T(8,128)(2,1)}, f32[2,8,1280]{2,1,0:T(8,128)S(1)}) custom-call(s32[3]{0:T(128)S(1)} %pad_add_fusion.refs_0_, f32[2,8,1280]{2,1,0:T(8,128)S(1)} %pad_bitcast_fusion.refs_1_, bf16[256,1024]{1,0:T(8,128)(2,1)S(1)} %copy-done.49, ...), custom_call_target="tpu_custom_call" | custom-call | flops 1 | bytes 1 | tf_op jit(solution)/shard_map/pallas_call | solution.py:598
  158.6 12.9 %collective-permute-done.15 = bf16[8,496,256]{2,1,0:T(8,128)(2,1)} collective-permute-done((bf16[8,496,256]{2,1,0:T(8,128)(2,1)S(1)}, bf16[8,496,256]{2,1,0:T(8,128)(2,1)}, u32[]{:S(2)}, u32[]{:S(2)}) %collective-permute-start.15) | collective-permute-done | bytes 2031648 | tf_op jit(solution)/shard_map/ppermute | solution.py:42
  172.4 2.8 slice_add_fusion.2
  175.3 2.8 slice_add_fusion
  178.1 1.7 collective-permute-start.20
  181.4 3.1 collective-permute-start.27
  184.5 6.6 %collective-permute-done.29.refs_15_ = bf16[2,128,512]{2,1,0:T(8,128)(2,1)S(1)} collective-permute-done((bf16[2,128,512]{2,1,0:T(8,128)(2,1)S(1)}, bf16[2,128,512]{2,1,0:T(8,128)(2,1)S(1)}, u32[]{:S(2)}, u32[]{:S(2)}) %collective-permute-start.29) | collective-permute-done | bytes 262176 | tf_op jit(solution)/shard_map/ppermute | solution.py:42
  192.0 6.3 %shard_map.348 = (bf16[8,192,256]{2,1,0:T(8,128)(2,1)}, bf16[8,192,256]{2,1,0:T(8,128)(2,1)}, bf16[8,192,256]{2,1,0:T(8,128)(2,1)}, bf16[8,192,256]{2,1,0:T(8,128)(2,1)}) custom-call(s32[2]{0:T(128)} %pad_add_fusion.2.me_ref, bf16[256,1024]{1,0:T(8,128)(2,1)} %copy-done.20, bf16[256,1024]{1,0:T(8,128)(2,1)} %get-tuple-element.127.refs_1_, ...), custom_call_target="tpu_custom_call" | custom-call | flops 1 | bytes 1 | tf_op jit(solution)/shard_map/pallas_call | solution.py:117
  198.3 16.1 %collective-permute-done.28.refs_14_ = bf16[2,128,512]{2,1,0:T(8,128)(2,1)S(1)} collective-permute-done((bf16[2,128,512]{2,1,0:T(8,128)(2,1)}, bf16[2,128,512]{2,1,0:T(8,128)(2,1)S(1)}, u32[]{:S(2)}, u32[]{:S(2)}) %collective-permute-start.28) | collective-permute-done | bytes 262176 | tf_op jit(solution)/shard_map/ppermute | solution.py:42
  215.2 1.4 add_convert_fusion.4
  217.3 2.2 slice_add_fusion.7
  219.5 1.8 add_convert_fusion.1
  221.4 1.8 collective-permute-start.23
  223.2 1.7 collective-permute-start.22
  224.9 2.2 slice_add_fusion.4
  228.5 8.6 %collective-permute-done.24.refs_12_ = bf16[2,256,512]{2,1,0:T(8,128)(2,1)S(1)} collective-permute-done((bf16[2,256,512]{2,1,0:T(8,128)(2,1)S(1)}, bf16[2,256,512]{2,1,0:T(8,128)(2,1)S(1)}, u32[]{:S(2)}, u32[]{:S(2)}) %collective-permute-start.24) | collective-permute-done | bytes 524320 | tf_op jit(solution)/shard_map/ppermute | solution.py:42
  237.1 1.7 collective-permute-start.36
  238.8 8.6 %collective-permute-done.23.refs_11_ = bf16[2,256,512]{2,1,0:T(8,128)(2,1)S(1)} collective-permute-done((bf16[2,256,512]{2,1,0:T(8,128)(2,1)S(1)}, bf16[2,256,512]{2,1,0:T(8,128)(2,1)S(1)}, u32[]{:S(2)}, u32[]{:S(2)}) %collective-permute-start.23) | collective-permute-done | bytes 524320 | tf_op jit(solution)/shard_map/ppermute | solution.py:42
  247.4 1.8 collective-permute-start.39
  249.2 1.6 add_convert_fusion
  252.4 6.2 %shard_map.349 = (bf16[8,192,256]{2,1,0:T(8,128)(2,1)}, bf16[8,192,256]{2,1,0:T(8,128)(2,1)}, bf16[8,192,256]{2,1,0:T(8,128)(2,1)}, bf16[8,192,256]{2,1,0:T(8,128)(2,1)}) custom-call(s32[2]{0:T(128)} %pad_add_fusion.2.me_ref, bf16[256,1024]{1,0:T(8,128)(2,1)} %copy-done.57, bf16[256,4096]{1,0:T(8,128)(2,1)} %collective-permute-done.14.refs_3_.refs_1_, ...), custom_call_target="tpu_custom_call" | custom-call | flops 1 | bytes 1 | tf_op jit(solution)/shard_map/pallas_call | solution.py:117
  258.6 1.3 copy.90
  263.2 1.6 copy-done.37
  264.8 1.2 copy-done.42
  267.2 2.6 shard_map.350
  270.9 1.3 slice_add_fusion.12
  274.6 1.6 slice_add_fusion.6
  276.2 2.8 collective-permute-start.40
  279.0 2.9 collective-permute-done.33
  282.0 8.2 %collective-permute-done.34 = bf16[8,192,256]{2,1,0:T(8,128)(2,1)S(1)} collective-permute-done((bf16[8,192,256]{2,1,0:T(8,128)(2,1)S(1)}, bf16[8,192,256]{2,1,0:T(8,128)(2,1)S(1)}, u32[]{:S(2)}, u32[]{:S(2)}) %collective-permute-start.34) | collective-permute-done | bytes 786464 | tf_op jit(solution)/shard_map/ppermute | solution.py:42
  290.3 7.7 %collective-permute-done.37 = bf16[4,192,256]{2,1,0:T(8,128)(2,1)S(1)} collective-permute-done((bf16[4,192,256]{2,1,0:T(8,128)(2,1)S(1)}, bf16[4,192,256]{2,1,0:T(8,128)(2,1)S(1)}, u32[]{:S(2)}, u32[]{:S(2)}) %collective-permute-start.37) | collective-permute-done | bytes 393248 | tf_op jit(solution)/shard_map/ppermute | solution.py:42
  298.0 5.0 %collective-permute-done.40.refs_2_ = bf16[1,1056,256]{2,1,0:T(8,128)(2,1)S(1)} collective-permute-done((bf16[1,1056,256]{2,1,0:T(8,128)(2,1)S(1)}, bf16[1,1056,256]{2,1,0:T(8,128)(2,1)S(1)}, u32[]{:S(2)}, u32[]{:S(2)}) %collective-permute-start.40) | collective-permute-done | bytes 540704 | tf_op jit(solution)/shard_map/ppermute | solution.py:42
  304.2 1.6 collective-permute-start.43
  305.9 2.1 collective-permute-start.45
  308.0 1.9 collective-permute-done.41
  311.0 3.1 collective-permute-done.44
  314.9 2.2 collective-permute-done.45
  317.1 1.6 collective-permute-start.48
  320.9 2.4 collective-permute-done.46
  323.8 6.3 %collective-permute-done.48 = bf16[2,384,256]{2,1,0:T(8,128)(2,1)S(1)} collective-permute-done((bf16[2,384,256]{2,1,0:T(8,128)(2,1)S(1)}, bf16[2,384,256]{2,1,0:T(8,128)(2,1)S(1)}, u32[]{:S(2)}, u32[]{:S(2)}) %collective-permute-start.48) | collective-permute-done | bytes 393248 | tf_op jit(solution)/shard_map/ppermute | solution.py:42
  331.9 1.8 copy.88
  334.9 5.7 %collective-permute-done.49.refs_2_ = bf16[1,384,256]{2,1,0:T(8,128)(2,1)S(1)} collective-permute-done((bf16[1,384,256]{2,1,0:T(8,128)(2,1)S(1)}, bf16[1,384,256]{2,1,0:T(8,128)(2,1)S(1)}, u32[]{:S(2)}, u32[]{:S(2)}) %collective-permute-start.49) | collective-permute-done | bytes 196640 | tf_op jit(solution)/shard_map/ppermute | solution.py:42
  (318 shorter events, 49.4 us)
Async XLA Ops:
  0.7 37.4 %copy-start = (bf16[1024,512]{1,0:T(8,128)(2,1)S(1)}, bf16[1024,512]{1,0:T(8,128)(2,1)}, u32[]{:S(2)}) copy-start(bf16[1024,512]{1,0:T(8,128)(2,1)} %param.35) | copy-start | bytes 3145732
  5.8 38.5 %copy-start.7 = (bf16[256,1024]{1,0:T(8,128)(2,1)}, bf16[256,1024]{1,0:T(8,128)(2,1)S(1)}, u32[]{:S(2)}) copy-start(bf16[256,1024]{1,0:T(8,128)(2,1)S(1)} %pad_maximum_fusion.5.refs_3_.refs_11_.refs_6_.refs_14_) | copy-start | bytes 1572868
  5.8 38.5 %collective-permute-start = (bf16[256,1024]{1,0:T(8,128)(2,1)S(1)}, bf16[256,1024]{1,0:T(8,128)(2,1)}, u32[]{:S(2)}, u32[]{:S(2)}) collective-permute-start(bf16[256,1024]{1,0:T(8,128)(2,1)S(1)} %pad_maximum_fusion.5.refs_3_.refs_11_.refs_6_.refs_14_), channel_id=1, source_target_pairs={{0,1},{1,0},{2,3},{3,2},{4,5},{5,4},{6,7},{7,6},{8,9},{9,8},{10,11... | collective-permute-start | bytes 1572872 | tf_op jit(solution)/shard_map/ppermute | solution.py:42
  6.3 15.3 %collective-permute-start.1 = (bf16[256,1024]{1,0:T(8,128)(2,1)S(1)}, bf16[256,1024]{1,0:T(8,128)(2,1)S(1)}, u32[]{:S(2)}, u32[]{:S(2)}) collective-permute-start(bf16[256,1024]{1,0:T(8,128)(2,1)S(1)} %pad_maximum_fusion.5.refs_3_.refs_11_.refs_6_.refs_14_), channel_id=1, source_target_pairs={{0,2},{1,3},{2,0},{3,1},{4,6},{5,7},{6,4},{7,5},{8,10},{9,11},{10,... | collective-permute-start | bytes 1572872 | tf_op jit(solution)/shard_map/ppermute | solution.py:42
  8.9 25.1 %collective-permute-start.3 = (bf16[256,1024]{1,0:T(8,128)(2,1)S(1)}, bf16[256,1024]{1,0:T(8,128)(2,1)S(1)}, u32[]{:S(2)}, u32[]{:S(2)}) collective-permute-start(bf16[256,1024]{1,0:T(8,128)(2,1)S(1)} %pad_maximum_fusion.5.refs_3_.refs_11_.refs_6_.refs_14_), channel_id=1, source_target_pairs={{0,6},{1,7},{2,4},{3,5},{4,2},{5,3},{6,0},{7,1},{8,14},{9,15},{10,... | collective-permute-start | bytes 1572872 | tf_op jit(solution)/shard_map/ppermute | solution.py:42
  10.4 24.9 %collective-permute-start.2 = (bf16[256,1024]{1,0:T(8,128)(2,1)S(1)}, bf16[256,1024]{1,0:T(8,128)(2,1)S(1)}, u32[]{:S(2)}, u32[]{:S(2)}) collective-permute-start(bf16[256,1024]{1,0:T(8,128)(2,1)S(1)} %pad_maximum_fusion.5.refs_3_.refs_11_.refs_6_.refs_14_), channel_id=1, source_target_pairs={{0,4},{1,5},{2,6},{3,7},{4,0},{5,1},{6,2},{7,3},{8,12},{9,13},{10,... | collective-permute-start | bytes 1572872 | tf_op jit(solution)/shard_map/ppermute | solution.py:42
  11.3 26.6 %copy-start.72 = (bf16[2,64,1024]{2,1,0:T(8,128)(2,1)S(1)}, bf16[2,64,1024]{2,1,0:T(8,128)(2,1)}, u32[]{:S(2)}) copy-start(bf16[2,64,1024]{2,1,0:T(8,128)(2,1)} %copy.75) | copy-start | bytes 786436
  11.5 27.0 %copy-start.59 = (bf16[1024,512]{1,0:T(8,128)(2,1)S(1)}, bf16[1024,512]{1,0:T(8,128)(2,1)}, u32[]{:S(2)}) copy-start(bf16[1024,512]{1,0:T(8,128)(2,1)} %param.34) | copy-start | bytes 3145732
  37.9 6.4 %collective-permute-start.4 = (bf16[256,3072]{1,0:T(8,128)(2,1)S(1)}, bf16[256,3072]{1,0:T(8,128)(2,1)S(1)}, u32[]{:S(2)}, u32[]{:S(2)}) collective-permute-start(bf16[256,3072]{1,0:T(8,128)(2,1)S(1)} %pad_maximum_fusion.1), channel_id=1, source_target_pairs={{0,1},{1,0},{2,3},{3,2},{4,5},{5,4},{6,7},{7,6},{8,9},{9,8},{10,11... | collective-permute-start | bytes 4718600 | tf_op jit(solution)/shard_map/ppermute | solution.py:42
  40.7 13.2 %collective-permute-start.6 = (bf16[128,1024]{1,0:T(8,128)(2,1)}, bf16[128,1024]{1,0:T(8,128)(2,1)S(1)}, u32[]{:S(2)}, u32[]{:S(2)}) collective-permute-start(bf16[128,1024]{1,0:T(8,128)(2,1)} %pad_maximum_fusion.8.refs_2_.refs_10_.refs_6_.refs_14_), channel_id=1, source_target_pairs={{0,2},{1,3},{2,0},{3,1},{4,6},{5,7},{6,4},{7,5},{8,10},{9,11},{10,... | collective-permute-start | bytes 786440 | tf_op jit(solution)/shard_map/ppermute | solution.py:42
  42.3 14.3 %collective-permute-start.7 = (bf16[128,1024]{1,0:T(8,128)(2,1)}, bf16[128,1024]{1,0:T(8,128)(2,1)S(1)}, u32[]{:S(2)}, u32[]{:S(2)}) collective-permute-start(bf16[128,1024]{1,0:T(8,128)(2,1)} %pad_maximum_fusion.8.refs_2_.refs_10_.refs_6_.refs_14_), channel_id=1, source_target_pairs={{0,4},{1,5},{2,6},{3,7},{4,0},{5,1},{6,2},{7,3},{8,12},{9,13},{10,... | collective-permute-start | bytes 786440 | tf_op jit(solution)/shard_map/ppermute | solution.py:42
  42.8 13.8 %collective-permute-start.8 = (bf16[128,1024]{1,0:T(8,128)(2,1)}, bf16[128,1024]{1,0:T(8,128)(2,1)S(1)}, u32[]{:S(2)}, u32[]{:S(2)}) collective-permute-start(bf16[128,1024]{1,0:T(8,128)(2,1)} %pad_maximum_fusion.8.refs_2_.refs_10_.refs_6_.refs_14_), channel_id=1, source_target_pairs={{0,6},{1,7},{2,4},{3,5},{4,2},{5,3},{6,0},{7,1},{8,14},{9,15},{10,... | collective-permute-start | bytes 786440 | tf_op jit(solution)/shard_map/ppermute | solution.py:42
  58.3 10.3 %collective-permute-start.9 = (bf16[128,3072]{1,0:T(8,128)(2,1)}, bf16[128,3072]{1,0:T(8,128)(2,1)S(1)}, u32[]{:S(2)}, u32[]{:S(2)}) collective-permute-start(bf16[128,3072]{1,0:T(8,128)(2,1)} %pad_maximum_fusion.3), channel_id=1, source_target_pairs={{0,1},{1,0},{2,3},{3,2},{4,5},{5,4},{6,7},{7,6},{8,9},{9,8},{10,11... | collective-permute-start | bytes 2359304 | tf_op jit(solution)/shard_map/ppermute | solution.py:42
  58.4 10.2 %collective-permute-start.5 = (bf16[128,1024]{1,0:T(8,128)(2,1)}, bf16[128,1024]{1,0:T(8,128)(2,1)}, u32[]{:S(2)}, u32[]{:S(2)}) collective-permute-start(bf16[128,1024]{1,0:T(8,128)(2,1)} %pad_maximum_fusion.8.refs_2_.refs_10_.refs_6_.refs_14_), channel_id=1, source_target_pairs={{0,1},{1,0},{2,3},{3,2},{4,5},{5,4},{6,7},{7,6},{8,9},{9,8},{10,11... | collective-permute-start | bytes 786440 | tf_op jit(solution)/shard_map/ppermute | solution.py:42
  99.9 6.8 %collective-permute-start.11 = (bf16[256,2816]{1,0:T(8,128)(2,1)}, bf16[256,2816]{1,0:T(8,128)(2,1)}, u32[]{:S(2)}, u32[]{:S(2)}) collective-permute-start(bf16[256,2816]{1,0:T(8,128)(2,1)} %get-tuple-element.122), channel_id=1, source_target_pairs={{0,1},{1,0},{2,3},{3,2},{4,5},{5,4},{6,7},{7,6},{8,9},{9,8},{10,11... | collective-permute-start | bytes 4325384 | tf_op jit(solution)/shard_map/ppermute | solution.py:42
  100.0 6.7 %collective-permute-start.12 = (bf16[256,2816]{1,0:T(8,128)(2,1)}, bf16[256,2816]{1,0:T(8,128)(2,1)}, u32[]{:S(2)}, u32[]{:S(2)}) collective-permute-start(bf16[256,2816]{1,0:T(8,128)(2,1)} %get-tuple-element.123.refs_4_), channel_id=1, source_target_pairs={{0,1},{1,0},{2,3},{3,2},{4,5},{5,4},{6,7},{7,6},{8,9},{9,8},{10,11... | collective-permute-start | bytes 4325384 | tf_op jit(solution)/shard_map/ppermute | solution.py:42
  100.5 6.2 %collective-permute-start.10 = (bf16[256,1024]{1,0:T(8,128)(2,1)}, bf16[256,1024]{1,0:T(8,128)(2,1)}, u32[]{:S(2)}, u32[]{:S(2)}) collective-permute-start(bf16[256,1024]{1,0:T(8,128)(2,1)} %get-tuple-element.120.refs_0_), channel_id=1, source_target_pairs={{0,1},{1,0},{2,3},{3,2},{4,5},{5,4},{6,7},{7,6},{8,9},{9,8},{10,11... | collective-permute-start | bytes 1572872 | tf_op jit(solution)/shard_map/ppermute | solution.py:42
  102.5 4.3 %collective-permute-start.13 = (bf16[256,512]{1,0:T(8,128)(2,1)}, bf16[256,512]{1,0:T(8,128)(2,1)}, u32[]{:S(2)}, u32[]{:S(2)}) collective-permute-start(bf16[256,512]{1,0:T(8,128)(2,1)} %get-tuple-element.314), channel_id=1, source_target_pairs={{0,1},{1,0},{2,3},{3,2},{4,5},{5,4},{6,7},{7,6},{8,9},{9,8},{10,11... | collective-permute-start | bytes 786440 | tf_op jit(solution)/shard_map/ppermute | solution.py:42
  118.9 53.5 %collective-permute-start.16 = (bf16[8,560,256]{2,1,0:T(8,128)(2,1)}, bf16[8,560,256]{2,1,0:T(8,128)(2,1)}, u32[]{:S(2)}, u32[]{:S(2)}) collective-permute-start(bf16[8,560,256]{2,1,0:T(8,128)(2,1)} %get-tuple-element.138), channel_id=1, source_target_pairs={{0,4},{1,5},{2,6},{3,7},{4,0},{5,1},{6,2},{7,3},{8,12},{9,13},{10,... | collective-permute-start | bytes 6881288 | tf_op jit(solution)/shard_map/ppermute | solution.py:42
  124.8 46.8 %collective-permute-start.14 = (bf16[256,4096]{1,0:T(8,128)(2,1)}, bf16[256,4096]{1,0:T(8,128)(2,1)}, u32[]{:S(2)}, u32[]{:S(2)}) collective-permute-start(bf16[256,4096]{1,0:T(8,128)(2,1)} %pad_maximum_fusion), channel_id=1, source_target_pairs={{0,1},{1,0},{2,3},{3,2},{4,5},{5,4},{6,7},{7,6},{8,9},{9,8},{10,11... | collective-permute-start | bytes 6291464 | tf_op jit(solution)/shard_map/ppermute | solution.py:42
  124.8 46.7 %collective-permute-start.15 = (bf16[8,496,256]{2,1,0:T(8,128)(2,1)S(1)}, bf16[8,496,256]{2,1,0:T(8,128)(2,1)}, u32[]{:S(2)}, u32[]{:S(2)}) collective-permute-start(bf16[8,496,256]{2,1,0:T(8,128)(2,1)S(1)} %copy-done.40), channel_id=1, source_target_pairs={{0,2},{1,3},{2,0},{3,1},{4,6},{5,7},{6,4},{7,5},{8,10},{9,11},{10,... | collective-permute-start | bytes 6094856 | tf_op jit(solution)/shard_map/ppermute | solution.py:42
  136.2 43.7 %copy-start.45 = (bf16[8,128,512]{2,1,0:T(8,128)(2,1)}, bf16[8,128,512]{2,1,0:T(8,128)(2,1)S(1)}, u32[]{:S(2)}) copy-start(bf16[8,128,512]{2,1,0:T(8,128)(2,1)S(1)} %get-tuple-element.152) | copy-start | bytes 3145732
  139.1 19.5 %copy-start.41 = (f32[256,1024]{1,0:T(8,128)}, f32[256,1024]{1,0:T(8,128)S(1)}, u32[]{:S(2)}) copy-start(f32[256,1024]{1,0:T(8,128)S(1)} %get-tuple-element.159.refs_10_) | copy-start | bytes 3145732
  139.1 19.6 %collective-permute-start.17 = (bf16[256,1536]{1,0:T(8,128)(2,1)S(1)}, bf16[256,1536]{1,0:T(8,128)(2,1)S(1)}, u32[]{:S(2)}, u32[]{:S(2)}) collective-permute-start(bf16[256,1536]{1,0:T(8,128)(2,1)S(1)} %get-tuple-element.139), channel_id=1, source_target_pairs={{0,1},{1,0},{2,3},{3,2},{4,5},{5,4},{6,7},{7,6},{8,9},{9,8},{10,11... | collective-permute-start | bytes 2359304 | tf_op jit(solution)/shard_map/ppermute | solution.py:42
  139.6 40.3 %collective-permute-start.26 = (bf16[8,128,512]{2,1,0:T(8,128)(2,1)}, bf16[8,128,512]{2,1,0:T(8,128)(2,1)S(1)}, u32[]{:S(2)}, u32[]{:S(2)}) collective-permute-start(bf16[8,128,512]{2,1,0:T(8,128)(2,1)} %get-tuple-element.153), channel_id=1, source_target_pairs={{0,1},{1,0},{2,3},{3,2},{4,5},{5,4},{6,7},{7,6},{8,9},{9,8},{10,11... | collective-permute-start | bytes 3145736 | tf_op jit(solution)/shard_map/ppermute | solution.py:42
  139.6 32.8 %copy-start.70 = (bf16[8,496,256]{2,1,0:T(8,128)(2,1)S(1)}, bf16[8,496,256]{2,1,0:T(8,128)(2,1)}, u32[]{:S(2)}) copy-start(bf16[8,496,256]{2,1,0:T(8,128)(2,1)} %get-tuple-element.143) | copy-start | bytes 6094852
  158.6 32.5 %copy-start.18 = (bf16[256,1024]{1,0:T(8,128)(2,1)}, bf16[256,1024]{1,0:T(8,128)(2,1)S(1)}, u32[]{:S(2)}) copy-start(bf16[256,1024]{1,0:T(8,128)(2,1)S(1)} %get-tuple-element.140.refs_6_.refs_2_) | copy-start | bytes 1572868
  172.4 47.0 %collective-permute-start.19 = (bf16[8,256,512]{2,1,0:T(8,128)(2,1)}, bf16[8,256,512]{2,1,0:T(8,128)(2,1)}, u32[]{:S(2)}, u32[]{:S(2)}) collective-permute-start(bf16[8,256,512]{2,1,0:T(8,128)(2,1)} %get-tuple-element.142), channel_id=1, source_target_pairs={{0,1},{1,0},{2,3},{3,2},{4,5},{5,4},{6,7},{7,6},{8,9},{9,8},{10,11... | collective-permute-start | bytes 6291464 | tf_op jit(solution)/shard_map/ppermute | solution.py:42
  178.1 39.1 %collective-permute-start.20 = (bf16[4,496,256]{2,1,0:T(8,128)(2,1)}, bf16[4,496,256]{2,1,0:T(8,128)(2,1)}, u32[]{:S(2)}, u32[]{:S(2)}) collective-permute-start(bf16[4,496,256]{2,1,0:T(8,128)(2,1)} %get-tuple-element.145), channel_id=1, source_target_pairs={{0,4},{1,5},{2,6},{3,7},{4,0},{5,1},{6,2},{7,3},{8,12},{9,13},{10,... | collective-permute-start | bytes 3047432 | tf_op jit(solution)/shard_map/ppermute | solution.py:42
  181.0 10.1 %collective-permute-start.29 = (bf16[2,128,512]{2,1,0:T(8,128)(2,1)S(1)}, bf16[2,128,512]{2,1,0:T(8,128)(2,1)S(1)}, u32[]{:S(2)}, u32[]{:S(2)}) collective-permute-start(bf16[2,128,512]{2,1,0:T(8,128)(2,1)S(1)} %get-tuple-element.156), channel_id=1, source_target_pairs={{0,6},{1,7},{2,4},{3,5},{4,2},{5,3},{6,0},{7,1},{8,14},{9,15},{10,... | collective-permute-start | bytes 786440 | tf_op jit(solution)/shard_map/ppermute | solution.py:42
  181.1 33.3 %collective-permute-start.28 = (bf16[2,128,512]{2,1,0:T(8,128)(2,1)}, bf16[2,128,512]{2,1,0:T(8,128)(2,1)S(1)}, u32[]{:S(2)}, u32[]{:S(2)}) collective-permute-start(bf16[2,128,512]{2,1,0:T(8,128)(2,1)} %get-tuple-element.155), channel_id=1, source_target_pairs={{0,4},{1,5},{2,6},{3,7},{4,0},{5,1},{6,2},{7,3},{8,12},{9,13},{10,... | collective-permute-start | bytes 786440 | tf_op jit(solution)/shard_map/ppermute | solution.py:42
  181.4 33.1 %collective-permute-start.27 = (bf16[2,128,512]{2,1,0:T(8,128)(2,1)}, bf16[2,128,512]{2,1,0:T(8,128)(2,1)}, u32[]{:S(2)}, u32[]{:S(2)}) collective-permute-start(bf16[2,128,512]{2,1,0:T(8,128)(2,1)} %get-tuple-element.154), channel_id=1, source_target_pairs={{0,2},{1,3},{2,0},{3,1},{4,6},{5,7},{6,4},{7,5},{8,10},{9,11},{10,... | collective-permute-start | bytes 786440 | tf_op jit(solution)/shard_map/ppermute | solution.py:42
  191.1 24.1 %copy-start.73 = (bf16[2,128,512]{2,1,0:T(8,128)(2,1)}, bf16[2,128,512]{2,1,0:T(8,128)(2,1)S(1)}, u32[]{:S(2)}) copy-start(bf16[2,128,512]{2,1,0:T(8,128)(2,1)S(1)} %collective-permute-done.29.refs_15_) | copy-start | bytes 786436
  191.1 30.2 %collective-permute-start.21 = (bf16[4,560,256]{2,1,0:T(8,128)(2,1)}, bf16[4,560,256]{2,1,0:T(8,128)(2,1)}, u32[]{:S(2)}, u32[]{:S(2)}) collective-permute-start(bf16[4,560,256]{2,1,0:T(8,128)(2,1)} %get-tuple-element.146), channel_id=1, source_target_pairs={{0,2},{1,3},{2,0},{3,1},{4,6},{5,7},{6,4},{7,5},{8,10},{9,11},{10,... | collective-permute-start | bytes 3440648 | tf_op jit(solution)/shard_map/ppermute | solution.py:42
  192.0 22.4 %copy-start.62 = (bf16[128,1024]{1,0:T(8,128)(2,1)S(1)}, bf16[128,1024]{1,0:T(8,128)(2,1)}, u32[]{:S(2)}) copy-start(bf16[128,1024]{1,0:T(8,128)(2,1)} %copy-done.61) | copy-start | bytes 786436
  214.4 37.2 %collective-permute-start.25 = (bf16[128,1024]{1,0:T(8,128)(2,1)S(1)}, bf16[128,1024]{1,0:T(8,128)(2,1)S(1)}, u32[]{:S(2)}, u32[]{:S(2)}) collective-permute-start(bf16[128,1024]{1,0:T(8,128)(2,1)S(1)} %copy-done.62), channel_id=1, source_target_pairs={{0,1},{1,0},{2,3},{3,2},{4,5},{5,4},{6,7},{7,6},{8,9},{9,8},{10,11... | collective-permute-start | bytes 786440 | tf_op jit(solution)/shard_map/ppermute | solution.py:42
  215.2 6.1 %collective-permute-start.18 = (bf16[256,512]{1,0:T(8,128)(2,1)}, bf16[256,512]{1,0:T(8,128)(2,1)S(1)}, u32[]{:S(2)}, u32[]{:S(2)}) collective-permute-start(bf16[256,512]{1,0:T(8,128)(2,1)} %get-tuple-element.312), channel_id=1, source_target_pairs={{0,1},{1,0},{2,3},{3,2},{4,5},{5,4},{6,7},{7,6},{8,9},{9,8},{10,11... | collective-permute-start | bytes 786440 | tf_op jit(solution)/shard_map/ppermute | solution.py:42
  221.3 15.7 %collective-permute-start.24 = (bf16[2,256,512]{2,1,0:T(8,128)(2,1)S(1)}, bf16[2,256,512]{2,1,0:T(8,128)(2,1)S(1)}, u32[]{:S(2)}, u32[]{:S(2)}) collective-permute-start(bf16[2,256,512]{2,1,0:T(8,128)(2,1)S(1)} %get-tuple-element.151), channel_id=1, source_target_pairs={{0,6},{1,7},{2,4},{3,5},{4,2},{5,3},{6,0},{7,1},{8,14},{9,15},{10,... | collective-permute-start | bytes 1572872 | tf_op jit(solution)/shard_map/ppermute | solution.py:42
  221.4 26.0 %collective-permute-start.23 = (bf16[2,256,512]{2,1,0:T(8,128)(2,1)S(1)}, bf16[2,256,512]{2,1,0:T(8,128)(2,1)S(1)}, u32[]{:S(2)}, u32[]{:S(2)}) collective-permute-start(bf16[2,256,512]{2,1,0:T(8,128)(2,1)S(1)} %get-tuple-element.150), channel_id=1, source_target_pairs={{0,4},{1,5},{2,6},{3,7},{4,0},{5,1},{6,2},{7,3},{8,12},{9,13},{10,... | collective-permute-start | bytes 1572872 | tf_op jit(solution)/shard_map/ppermute | solution.py:42
  223.2 26.0 %collective-permute-start.22 = (bf16[2,256,512]{2,1,0:T(8,128)(2,1)S(1)}, bf16[2,256,512]{2,1,0:T(8,128)(2,1)S(1)}, u32[]{:S(2)}, u32[]{:S(2)}) collective-permute-start(bf16[2,256,512]{2,1,0:T(8,128)(2,1)S(1)} %get-tuple-element.149), channel_id=1, source_target_pairs={{0,2},{1,3},{2,0},{3,1},{4,6},{5,7},{6,4},{7,5},{8,10},{9,11},{10,... | collective-permute-start | bytes 1572872 | tf_op jit(solution)/shard_map/ppermute | solution.py:42
  228.1 41.6 %collective-permute-start.35 = (bf16[8,192,256]{2,1,0:T(8,128)(2,1)}, bf16[8,192,256]{2,1,0:T(8,128)(2,1)}, u32[]{:S(2)}, u32[]{:S(2)}) collective-permute-start(bf16[8,192,256]{2,1,0:T(8,128)(2,1)} %get-tuple-element.169), channel_id=1, source_target_pairs={{0,2},{1,3},{2,0},{3,1},{4,6},{5,7},{6,4},{7,5},{8,10},{9,11},{10,... | collective-permute-start | bytes 2359304 | tf_op jit(solution)/shard_map/ppermute | solution.py:42
  237.1 35.2 %collective-permute-start.36 = (bf16[8,192,256]{2,1,0:T(8,128)(2,1)}, bf16[8,192,256]{2,1,0:T(8,128)(2,1)}, u32[]{:S(2)}, u32[]{:S(2)}) collective-permute-start(bf16[8,192,256]{2,1,0:T(8,128)(2,1)} %get-tuple-element.171), channel_id=1, source_target_pairs={{0,4},{1,5},{2,6},{3,7},{4,0},{5,1},{6,2},{7,3},{8,12},{9,13},{10,... | collective-permute-start | bytes 2359304 | tf_op jit(solution)/shard_map/ppermute | solution.py:42
  247.4 26.1 %collective-permute-start.39 = (bf16[2,1056,256]{2,1,0:T(8,128)(2,1)}, bf16[2,1056,256]{2,1,0:T(8,128)(2,1)}, u32[]{:S(2)}, u32[]{:S(2)}) collective-permute-start(bf16[2,1056,256]{2,1,0:T(8,128)(2,1)} %pad_maximum_fusion.2), channel_id=1, source_target_pairs={{0,8},{8,0},{16,24},{24,16},{1,9},{9,1},{17,25},{25,17},{2,10},{10... | collective-permute-start | bytes 3244040 | tf_op jit(solution)/shard_map/ppermute | solution.py:42
  258.6 3.1 collective-permute-start.30
  260.7 21.2 %collective-permute-start.33 = (bf16[8,192,256]{2,1,0:T(8,128)(2,1)}, bf16[8,192,256]{2,1,0:T(8,128)(2,1)S(1)}, u32[]{:S(2)}, u32[]{:S(2)}) collective-permute-start(bf16[8,192,256]{2,1,0:T(8,128)(2,1)} %get-tuple-element.157.refs_1_), channel_id=1, source_target_pairs={{0,2},{1,3},{2,0},{3,1},{4,6},{5,7},{6,4},{7,5},{8,10},{9,11},{10,... | collective-permute-start | bytes 2359304 | tf_op jit(solution)/shard_map/ppermute | solution.py:42
  261.7 57.0 %collective-permute-start.31 = (bf16[128,512]{1,0:T(8,128)(2,1)}, bf16[128,512]{1,0:T(8,128)(2,1)S(1)}, u32[]{:S(2)}, u32[]{:S(2)}) collective-permute-start(bf16[128,512]{1,0:T(8,128)(2,1)} %get-tuple-element.161.refs_9_), channel_id=1, source_target_pairs={{0,1},{1,0},{2,3},{3,2},{4,5},{5,4},{6,7},{7,6},{8,9},{9,8},{10,11... | collective-permute-start | bytes 393224 | tf_op jit(solution)/shard_map/ppermute | solution.py:42
  269.8 20.4 %collective-permute-start.34 = (bf16[8,192,256]{2,1,0:T(8,128)(2,1)S(1)}, bf16[8,192,256]{2,1,0:T(8,128)(2,1)S(1)}, u32[]{:S(2)}, u32[]{:S(2)}) collective-permute-start(bf16[8,192,256]{2,1,0:T(8,128)(2,1)S(1)} %copy-done.87), channel_id=1, source_target_pairs={{0,4},{1,5},{2,6},{3,7},{4,0},{5,1},{6,2},{7,3},{8,12},{9,13},{10,... | collective-permute-start | bytes 2359304 | tf_op jit(solution)/shard_map/ppermute | solution.py:42
  272.2 4.0 %collective-permute-start.32 = (f32[28,128]{1,0:T(8,128)S(1)}, f32[28,128]{1,0:T(8,128)S(1)}, u32[]{:S(2)}, u32[]{:S(2)}) collective-permute-start(f32[28,128]{1,0:T(8,128)S(1)} %maximum_bitcast_fusion), channel_id=1, source_target_pairs={{0,1},{1,0},{2,3},{3,2},{4,5},{5,4},{6,7},{7,6},{8,9},{9,8},{10,11... | collective-permute-start | bytes 43016 | tf_op jit(solution)/shard_map/ppermute | solution.py:42
  273.5 24.5 %collective-permute-start.37 = (bf16[4,192,256]{2,1,0:T(8,128)(2,1)S(1)}, bf16[4,192,256]{2,1,0:T(8,128)(2,1)S(1)}, u32[]{:S(2)}, u32[]{:S(2)}) collective-permute-start(bf16[4,192,256]{2,1,0:T(8,128)(2,1)S(1)} %get-tuple-element.172), channel_id=1, source_target_pairs={{0,4},{1,5},{2,6},{3,7},{4,0},{5,1},{6,2},{7,3},{8,12},{9,13},{10,... | collective-permute-start | bytes 1179656 | tf_op jit(solution)/shard_map/ppermute | solution.py:42
  276.2 26.8 %collective-permute-start.40 = (bf16[1,1056,256]{2,1,0:T(8,128)(2,1)S(1)}, bf16[1,1056,256]{2,1,0:T(8,128)(2,1)S(1)}, u32[]{:S(2)}, u32[]{:S(2)}) collective-permute-start(bf16[1,1056,256]{2,1,0:T(8,128)(2,1)S(1)} %get-tuple-element.175), channel_id=1, source_target_pairs={{0,16},{8,24},{16,0},{24,8},{1,17},{9,25},{17,1},{25,9},{2,18},{10... | collective-permute-start | bytes 1622024 | tf_op jit(solution)/shard_map/ppermute | solution.py:42
  281.9 16.1 %collective-permute-start.38 = (bf16[4,192,256]{2,1,0:T(8,128)(2,1)S(1)}, bf16[4,192,256]{2,1,0:T(8,128)(2,1)S(1)}, u32[]{:S(2)}, u32[]{:S(2)}) collective-permute-start(bf16[4,192,256]{2,1,0:T(8,128)(2,1)S(1)} %get-tuple-element.173), channel_id=1, source_target_pairs={{0,2},{1,3},{2,0},{3,1},{4,6},{5,7},{6,4},{7,5},{8,10},{9,11},{10,... | collective-permute-start | bytes 1179656 | tf_op jit(solution)/shard_map/ppermute | solution.py:42
  303.0 11.1 %collective-permute-start.44 = (bf16[4,192,256]{2,1,0:T(8,128)(2,1)S(1)}, bf16[4,192,256]{2,1,0:T(8,128)(2,1)S(1)}, u32[]{:S(2)}, u32[]{:S(2)}) collective-permute-start(bf16[4,192,256]{2,1,0:T(8,128)(2,1)S(1)} %get-tuple-element.180), channel_id=1, source_target_pairs={{0,2},{1,3},{2,0},{3,1},{4,6},{5,7},{6,4},{7,5},{8,10},{9,11},{10,... | collective-permute-start | bytes 1179656 | tf_op jit(solution)/shard_map/ppermute | solution.py:42
  304.2 10.6 %collective-permute-start.43 = (bf16[4,192,256]{2,1,0:T(8,128)(2,1)S(1)}, bf16[4,192,256]{2,1,0:T(8,128)(2,1)S(1)}, u32[]{:S(2)}, u32[]{:S(2)}) collective-permute-start(bf16[4,192,256]{2,1,0:T(8,128)(2,1)S(1)} %get-tuple-element.179), channel_id=1, source_target_pairs={{0,4},{1,5},{2,6},{3,7},{4,0},{5,1},{6,2},{7,3},{8,12},{9,13},{10,... | collective-permute-start | bytes 1179656 | tf_op jit(solution)/shard_map/ppermute | solution.py:42
  305.8 4.0 %collective-permute-start.41 = (f32[28,128]{1,0:T(8,128)S(1)}, f32[28,128]{1,0:T(8,128)S(1)}, u32[]{:S(2)}, u32[]{:S(2)}) collective-permute-start(f32[28,128]{1,0:T(8,128)S(1)} %fusion.17), channel_id=1, source_target_pairs={{0,8},{8,0},{16,24},{24,16},{1,9},{9,1},{17,25},{25,17},{2,10},{10... | collective-permute-start | bytes 43016 | tf_op jit(solution)/shard_map/ppermute | solution.py:42
  305.9 11.2 %collective-permute-start.45 = (bf16[2,384,256]{2,1,0:T(8,128)(2,1)S(1)}, bf16[2,384,256]{2,1,0:T(8,128)(2,1)S(1)}, u32[]{:S(2)}, u32[]{:S(2)}) collective-permute-start(bf16[2,384,256]{2,1,0:T(8,128)(2,1)S(1)} %pad_maximum_fusion.6), channel_id=1, source_target_pairs={{0,8},{8,0},{16,24},{24,16},{1,9},{9,1},{17,25},{25,17},{2,10},{10... | collective-permute-start | bytes 1179656 | tf_op jit(solution)/shard_map/ppermute | solution.py:42
  309.9 9.6 %collective-permute-start.42 = (f32[28,128]{1,0:T(8,128)S(1)}, f32[28,128]{1,0:T(8,128)S(1)}, u32[]{:S(2)}, u32[]{:S(2)}) collective-permute-start(f32[28,128]{1,0:T(8,128)S(1)} %add.231), channel_id=1, source_target_pairs={{0,16},{8,24},{16,0},{24,8},{1,17},{9,25},{17,1},{25,9},{2,18},{10... | collective-permute-start | bytes 43016 | tf_op jit(solution)/shard_map/ppermute | solution.py:42
  317.1 12.9 %collective-permute-start.48 = (bf16[2,384,256]{2,1,0:T(8,128)(2,1)S(1)}, bf16[2,384,256]{2,1,0:T(8,128)(2,1)S(1)}, u32[]{:S(2)}, u32[]{:S(2)}) collective-permute-start(bf16[2,384,256]{2,1,0:T(8,128)(2,1)S(1)} %pad_maximum_fusion.7), channel_id=1, source_target_pairs={{0,8},{8,0},{16,24},{24,16},{1,9},{9,1},{17,25},{25,17},{2,10},{10... | collective-permute-start | bytes 1179656 | tf_op jit(solution)/shard_map/ppermute | solution.py:42
  319.4 14.3 %collective-permute-start.53 = (bf16[528,256]{1,0:T(8,128)(2,1)S(1)}, bf16[528,256]{1,0:T(8,128)(2,1)S(1)}, u32[]{:S(2)}, u32[]{:S(2)}) collective-permute-start(bf16[528,256]{1,0:T(8,128)(2,1)S(1)} %get-tuple-element.198), channel_id=1, source_target_pairs={{0,1},{1,0},{2,3},{3,2},{4,5},{5,4},{6,7},{7,6},{8,9},{9,8},{10,11... | collective-permute-start | bytes 811016 | tf_op jit(solution)/shard_map/ppermute | solution.py:42
  319.5 3.8 %collective-permute-start.46 = (f32[28,128]{1,0:T(8,128)S(1)}, f32[28,128]{1,0:T(8,128)S(1)}, u32[]{:S(2)}, u32[]{:S(2)}) collective-permute-start(f32[28,128]{1,0:T(8,128)S(1)} %add.232), channel_id=1, source_target_pairs={{0,2},{1,3},{2,0},{3,1},{4,6},{5,7},{6,4},{7,5},{8,10},{9,11},{10,... | collective-permute-start | bytes 43016 | tf_op jit(solution)/shard_map/ppermute | solution.py:42
  320.0 14.7 %collective-permute-start.51 = (bf16[1,384,256]{2,1,0:T(8,128)(2,1)S(1)}, bf16[1,384,256]{2,1,0:T(8,128)(2,1)S(1)}, u32[]{:S(2)}, u32[]{:S(2)}) collective-permute-start(bf16[1,384,256]{2,1,0:T(8,128)(2,1)S(1)} %get-tuple-element.189), channel_id=1, source_target_pairs={{0,16},{8,24},{16,0},{24,8},{1,17},{9,25},{17,1},{25,9},{2,18},{10... | collective-permute-start | bytes 589832 | tf_op jit(solution)/shard_map/ppermute | solution.py:42
  323.3 11.4 %collective-permute-start.47 = (f32[28,128]{1,0:T(8,128)S(1)}, f32[28,128]{1,0:T(8,128)S(1)}, u32[]{:S(2)}, u32[]{:S(2)}) collective-permute-start(f32[28,128]{1,0:T(8,128)S(1)} %add.239), channel_id=1, source_target_pairs={{0,4},{1,5},{2,6},{3,7},{4,0},{5,1},{6,2},{7,3},{8,12},{9,13},{10,... | collective-permute-start | bytes 43016 | tf_op jit(solution)/shard_map/ppermute | solution.py:42
  330.1 10.5 %collective-permute-start.49 = (bf16[1,384,256]{2,1,0:T(8,128)(2,1)S(1)}, bf16[1,384,256]{2,1,0:T(8,128)(2,1)S(1)}, u32[]{:S(2)}, u32[]{:S(2)}) collective-permute-start(bf16[1,384,256]{2,1,0:T(8,128)(2,1)S(1)} %get-tuple-element.304), channel_id=1, source_target_pairs={{0,16},{8,24},{16,0},{24,8},{1,17},{9,25},{17,1},{25,9},{2,18},{10... | collective-permute-start | bytes 589832 | tf_op jit(solution)/shard_map/ppermute | solution.py:42
  334.8 7.3 %collective-permute-start.52 = (bf16[192,256]{1,0:T(8,128)(2,1)S(1)}, bf16[192,256]{1,0:T(8,128)(2,1)S(1)}, u32[]{:S(2)}, u32[]{:S(2)}) collective-permute-start(bf16[192,256]{1,0:T(8,128)(2,1)S(1)} %get-tuple-element.191), channel_id=1, source_target_pairs={{0,1},{1,0},{2,3},{3,2},{4,5},{5,4},{6,7},{7,6},{8,9},{9,8},{10,11... | collective-permute-start | bytes 294920 | tf_op jit(solution)/shard_map/ppermute | solution.py:42
  340.7 2.2 collective-permute-start.50
  (81 other events, 441.9 us)

commit v5 on v4

--- a/solution.py
+++ b/solution.py
@@ -858,7 +858,7 @@
         gate_weight,
         up_weight,
         down_weight,
-        [],
+        [low_pair],
     )
     feed_pair = exchange(normed_feed, "seq", 1)
     hidden_pair = exchange(hidden, "seq", 1)
@@ -905,7 +905,6 @@
     key_parts = scatter_start(kept, rest)
     feed_chain.add()
     feed_second = feed_chain.start([kept])
-    memory_sent = scatter_send(memory_parts[:1] + tie(memory_parts[1:], [kept]))
     query_own, query_other = core_halves(*cut(query_grad))
     query_pair = exchange(query_other, "seq", 1)
     two = [(0, 0), (1, TILE)]
@@ -922,9 +921,13 @@
     )
     line_grad = line_grad.reshape(-1, line_grad.shape[2])[:, 2 * tokens :]
     table_grad = jnp.dot(line_grad, bucket_onehot, precision=highest, preferred_element_type=f32).T
-    arrived = feed_second + key_parts[1:] + [query_pair, out_chain.send[0]]
-
-    key_sent = scatter_send(key_parts[:1] + tie(key_parts[1:], arrived))
+    arrived = feed_second + key_parts[1:] + memory_parts[1:] + [query_pair, out_chain.send[0]]
+
+    joint = [jnp.concatenate(pair, axis=1) for pair in zip(key_parts[1:], memory_parts[1:])]
+    joint_sent = scatter_send(key_parts[:1] + tie(joint, arrived))
+    cut_at = key_parts[0].shape[1]
+    key_sent = [v[:, :cut_at] for v in joint_sent]
+    memory_sent = [v[:, cut_at:] for v in joint_sent]
     out_first = out_chain.start(arrived)
     feed_chain.add()
     feed_chain.to_dp()
@@ -932,7 +935,9 @@
     feed_z = feed_chain.start(arrived)
     key_half, key_half_pair = scatter_finish(key_parts[0], key_sent)
     memory_half, memory_half_pair = scatter_finish(memory_parts[0], memory_sent)
-    arrived = key_sent + memory_sent
+    arrived = joint_sent + feed_z
+    feed_chain.add()
+    feed_z = feed_chain.start(arrived)
 
     in_chain = Chain.of(
         group_grads(
@@ -964,7 +969,7 @@
         self_gain.reshape(1, -1),
         first_grad,
         core=core,
-        after=[in_chain.send[0]],
+        after=[in_chain.send[0]] + feed_z,
     )
     small = jnp.concatenate(
         [v.reshape(-1) for v in (self_gain_grad, cross_gain_grad, feed_gain_grad, table_grad)]
@@ -972,9 +977,7 @@
     small = sum_over(small, [("seq", 1)])
     out_chain.add()
     out_second = out_chain.start(arrived + in_chain.send[:1])
-    feed_chain.add()
-    feed_z = feed_chain.start(arrived)
-    arrived = in_first + out_second + feed_z + [small]
+    arrived = in_first + out_second + [small]
 
     dp_bits, seq_bits = bits_of(lax.axis_size("dp"), 1), bits_of(lax.axis_size("seq"), 2)
     small = sum_over(tie([small], arrived)[0], [("dp", bit) for bit in dp_bits])

time: 349 us -> 341 us (0.977)
  waiting for transfers between devices: 129 us -> 120 us
  starting transfers between devices: 42.1 us -> 45.9 us
    ppermute x54 -> x51, waiting for transfers between devices: 129 us -> 120 us  [exchange(): return lax.ppermute(value, axis, [(i, i ^ bit) for i in range(size)])]
    add x9 -> x11, other arithmetic: 10 us -> 15.7 us  [add(): self.keep = [k[:half] + g[:half] for k, g in zip(self.keep, got)]]
    add x6 -> x4, other arithmetic: 4.65 us -> 0.29 us  [add(): self.send = [k[half:] + g[half:] for k, g in zip(self.keep, got)]]
    ppermute x54 -> x51, starting transfers between devices: 42.1 us -> 45.9 us  [exchange(): return lax.ppermute(value, axis, [(i, i ^ bit) for i in range(size)])]
    unnamed x184 -> x180, local copies, waits for them, and re-layouts: 16.4 us -> 14.7 us
  transfers between devices with their start and end apart: 54 -> 51, of which waited for: 22 -> 22; matrix products, arithmetic and copies ran while one was open for 13% -> 14% of each run, Pallas kernels for 18% -> 20%
where the time goes in v5:
time: 341 us; the launch traced here: 336 us
  waiting for transfers between devices  120 us (35%)
  Pallas kernels  102 us (30%)
  starting transfers between devices  45.9 us (13%)
  other arithmetic  35.9 us (11%)
  local copies, waits for them, and re-layouts  26.2 us (8%)
  matrix products  4.15 us (1%)
    ppermute x51, waiting for transfers between devices, exchange(): return lax.ppermute(value, axis, [(i, i ^ bit) for i in range(size)])  120 us
    ppermute x51, starting transfers between devices, exchange(): return lax.ppermute(value, axis, [(i, i ^ bit) for i in range(size)])  45.9 us
    pallas_call x2, Pallas kernels, attend_back(): pl.pallas_call(functools.partial(back_kernel, biased, seqs, tokens, count...  29.2 us
    pallas_call x3, Pallas kernels, group_grads(): pl.pallas_call(functools.partial(grads_kernel, chips, orders, full, len(a...  24.6 us
    pallas_call x1, Pallas kernels, feed_forward(): pl.pallas_call(body, grid=(units // TILE,), in_specs=[pl.BlockSpec(memory...  21.8 us
    add x11, other arithmetic, add(): self.keep = [k[:half] + g[:half] for k, g in zip(self.keep, got)]  15.7 us
    pallas_call x2, Pallas kernels, attend(): pl.pallas_call(functools.partial(attend_kernel, biased, seqs, tokens, cou...  15.5 us
    unnamed x180, local copies, waits for them, and re-layouts  14.7 us
  transfers between devices with their start and end apart: 51, of which 22 were waited for; matrix products, arithmetic and copies ran while one was open for 14% of the time, Pallas kernels for 20%

profile of v5, /device:TPU:0, one launch (start us, length us, event | category | flops | bytes accessed | tf_op | source)
XLA Modules:
  0.0 336.2 jit_solution(8582977536622158177)
XLA Ops:
  0.7 1.8 multiply_reduce_fusion
  5.8 3.0 collective-permute-start.2
  8.8 1.5 collective-permute-start.3
  10.5 1.7 copy.76
  12.2 1.1 copy.73
  14.6 7.0 %collective-permute-done.2.refs_5_.refs_13_.refs_8_.refs_16_ = bf16[256,1024]{1,0:T(8,128)(2,1)S(1)} collective-permute-done((bf16[256,1024]{1,0:T(8,128)(2,1)S(1)}, bf16[256,1024]{1,0:T(8,128)(2,1)S(1)}, u32[]{:S(2)}, u32[]{:S(2)}) %collective-permute-start.2) | collective-permute-done | bytes 524320 | tf_op jit(solution)/shard_map/ppermute | solution.py:42
  21.6 11.9 %collective-permute-done.3.refs_7_.refs_15_.refs_10_.refs_18_ = bf16[256,1024]{1,0:T(8,128)(2,1)S(1)} collective-permute-done((bf16[256,1024]{1,0:T(8,128)(2,1)S(1)}, bf16[256,1024]{1,0:T(8,128)(2,1)S(1)}, u32[]{:S(2)}, u32[]{:S(2)}) %collective-permute-start.3) | collective-permute-done | bytes 524320 | tf_op jit(solution)/shard_map/ppermute | solution.py:42
  38.4 1.3 collective-permute-start.7
  40.5 1.4 collective-permute-start.9
  42.0 8.8 %shard_map.340 = (bf16[256,1024]{1,0:T(8,128)(2,1)S(1)}, f32[2,8,256]{2,1,0:T(8,128)S(1)}) custom-call(s32[3]{0:T(128)S(1)} %pad_add_fusion.refs_0_, f32[2,8,1280]{2,1,0:T(8,128)S(1)} %pad_bitcast_fusion.refs_1_, bf16[256,1024]{1,0:T(8,128)(2,1)S(1)} %convolution_convert_fusion.refs_2_, ...), custom_call_target="tpu_custom_call" | custom-call | flops 17179869184 | bytes 2097152 | tf_op jit(solution)/shard_map/pallas_call | solution.py:549
  51.8 1.6 collective-permute-done.9.refs_8_.refs_16_.refs_12_.refs_20_
  57.0 4.9 %shard_map.341 = (f32[256,1024]{1,0:T(8,128)}, bf16[256,1024]{1,0:T(8,128)(2,1)}, bf16[256,1024]{1,0:T(8,128)(2,1)}) custom-call(bf16[256,1024]{1,0:T(8,128)(2,1)} %bitcast.78, bf16[256,1024]{1,0:T(8,128)(2,1)} %copy-done.3, bf16[1024,1024]{1,0:T(8,128)(2,1)} %refs_6_.2, f32[1,1024]{1,0:T(1,128)} %bitcast.86, bf16[1024,1024]{1,0:T(8,128)(2,1)} %refs_2_.3), custom_call_target="tpu_custom_call" | custom-call | flops 1 | bytes 1 | tf_op jit(solution)/shard_map/pallas_call | solution.py:753
  64.8 6.7 %shard_map.342 = (bf16[256,1024]{1,0:T(8,128)(2,1)S(1)}, f32[2,8,256]{2,1,0:T(8,128)S(1)}) custom-call(s32[3]{0:T(128)S(1)} %pad_add_fusion.1.refs_0_, bf16[256,1024]{1,0:T(8,128)(2,1)S(1)} %copy-done.53, bf16[128,1024]{1,0:T(8,128)(2,1)S(1)} %copy-done.27, bf16[128,1024]{1,0:T(8,128)(2,1)} %collective-permute-done.6.refs_3_.refs_11_.refs_7_.refs_15_, ...), custom_call_target="tpu_custom_call" | custom-call | flops 8589934592 | bytes 2097152 | tf_op jit(solution)/shard_map/pallas_call | solution.py:549
  72.3 21.8 %shard_map.343 = (bf16[256,1024]{1,0:T(8,128)(2,1)}, bf16[256,2816]{1,0:T(8,128)(2,1)}, bf16[256,2816]{1,0:T(8,128)(2,1)}, bf16[256,2816]{1,0:T(8,128)(2,1)}, bf...) custom-call(s32[1]{0:T(128)} %bitcast.core_ref.refs_0_, ...), custom_call_target="tpu_custom_call" | custom-call | flops 8858370048 | bytes 17301504 | tf_op jit(solution)/shard_map/pallas_call | solution.py:673
  95.8 4.9 %collective-permute-done.11.refs_1_ = bf16[256,1024]{1,0:T(8,128)(2,1)} collective-permute-done((bf16[256,1024]{1,0:T(8,128)(2,1)}, bf16[256,1024]{1,0:T(8,128)(2,1)}, u32[]{:S(2)}, u32[]{:S(2)}) %collective-permute-start.11) | collective-permute-done | bytes 524320 | tf_op jit(solution)/shard_map/ppermute | solution.py:42
  100.7 12.1 %shard_map.344 = (bf16[8,496,256]{2,1,0:T(8,128)(2,1)}, bf16[8,496,256]{2,1,0:T(8,128)(2,1)}, bf16[8,560,256]{2,1,0:T(8,128)(2,1)}, bf16[8,560,256]{2,1,0:T(8,128)(2,1)}) custom-call(s32[2]{0:T(128)} %pad_add_fusion.2.me_ref, bf16[256,1024]{1,0:T(8,128)(2,1)} %get-tuple-element.117.refs_0_, bf16[256,1024]{1,0:T(8,128)(2,1)} %collective-permute-done.11.refs_1_, ...), custom_call_target="tpu_custom_call" | custom-call | flops 1 | bytes 1 | tf_op jit(solution)/shard_map/pallas_call | solution.py:117
  112.9 4.3 %collective-permute-start.16 = (bf16[8,560,256]{2,1,0:T(8,128)(2,1)}, bf16[8,560,256]{2,1,0:T(8,128)(2,1)}, u32[]{:S(2)}, u32[]{:S(2)}) collective-permute-start(bf16[8,560,256]{2,1,0:T(8,128)(2,1)} %get-tuple-element.135), channel_id=1, source_target_pairs={{0,4},{1,5},{2,6},{3,7},{4,0},{5,1},{6,2},{7,3},{8,12},{9,13},{10,... | collective-permute-start | bytes 6881288 | tf_op jit(solution)/shard_map/ppermute | solution.py:42
  117.2 3.0 pad_maximum_fusion
  121.4 10.2 %shard_map.345 = (bf16[256,1024]{1,0:T(8,128)(2,1)S(1)}, bf16[8,128,512]{2,1,0:T(8,128)(2,1)S(1)}, bf16[8,128,512]{2,1,0:T(8,128)(2,1)}) custom-call(s32[3]{0:T(128)S(1)} %pad_add_fusion.1.refs_0_, bf16[8,496,256]{2,1,0:T(8,128)(2,1)S(1)} %copy-done.43, bf16[256,1024]{1,0:T(8,128)(2,1)S(1)} %copy-done.54, bf16[256,1024]{1,0:T(8,128)(2,1)S(1)} %copy-done.19, ...), custom_call_target="tpu_custom_call" | custom-call | flops 1 | bytes 1 | tf_op jit(solution)/shard_map/pallas_call | solution.py:598
  131.7 1.8 shard_map.346
  135.1 19.0 %shard_map.347 = (bf16[256,1024]{1,0:T(8,128)(2,1)S(1)}, bf16[8,256,512]{2,1,0:T(8,128)(2,1)S(1)}, bf16[8,256,512]{2,1,0:T(8,128)(2,1)}, f32[2,8,1280]{2,1,0:T(8,128)S(1)}) custom-call(s32[3]{0:T(128)S(1)} %pad_add_fusion.refs_0_, f32[2,8,1280]{2,1,0:T(8,128)S(1)} %pad_bitcast_fusion.refs_1_, bf16[256,1024]{1,0:T(8,128)(2,1)S(1)} %copy-done.52, ...), custom_call_target="tpu_custom_call" | custom-call | flops 1 | bytes 1 | tf_op jit(solution)/shard_map/pallas_call | solution.py:598
  154.1 12.9 %collective-permute-done.15 = bf16[8,496,256]{2,1,0:T(8,128)(2,1)} collective-permute-done((bf16[8,496,256]{2,1,0:T(8,128)(2,1)S(1)}, bf16[8,496,256]{2,1,0:T(8,128)(2,1)}, u32[]{:S(2)}, u32[]{:S(2)}) %collective-permute-start.15) | collective-permute-done | bytes 2031648 | tf_op jit(solution)/shard_map/ppermute | solution.py:42
  167.8 2.8 slice_add_fusion.2
  170.7 2.9 slice_add_fusion
  173.6 1.7 collective-permute-start.21
  177.5 6.3 %shard_map.348 = (bf16[8,192,256]{2,1,0:T(8,128)(2,1)}, bf16[8,192,256]{2,1,0:T(8,128)(2,1)}, bf16[8,192,256]{2,1,0:T(8,128)(2,1)}, bf16[8,192,256]{2,1,0:T(8,128)(2,1)}) custom-call(s32[2]{0:T(128)} %pad_add_fusion.2.me_ref, bf16[256,1024]{1,0:T(8,128)(2,1)} %copy-done.18, bf16[256,1024]{1,0:T(8,128)(2,1)} %get-tuple-element.124.refs_1_, ...), custom_call_target="tpu_custom_call" | custom-call | flops 1 | bytes 1 | tf_op jit(solution)/shard_map/pallas_call | solution.py:117
  183.8 15.0 %collective-permute-done.21 = bf16[4,496,256]{2,1,0:T(8,128)(2,1)} collective-permute-done((bf16[4,496,256]{2,1,0:T(8,128)(2,1)}, bf16[4,496,256]{2,1,0:T(8,128)(2,1)}, u32[]{:S(2)}, u32[]{:S(2)}) %collective-permute-start.21) | collective-permute-done | bytes 1015840 | tf_op jit(solution)/shard_map/ppermute | solution.py:42
  198.7 2.1 slice_add_fusion.7
  200.8 2.0 collective-permute-done.22
  202.8 2.4 slice_add_fusion.4
  205.2 1.8 add_convert_fusion.1
  208.1 1.3 pad_maximum_fusion.4
  210.0 2.9 collective-permute-start.25
  214.0 1.6 collective-permute-start.27
  215.6 1.3 copy.90
  217.6 12.7 %collective-permute-done.23.refs_10_ = bf16[2,384,512]{2,1,0:T(8,128)(2,1)} collective-permute-done((bf16[2,384,512]{2,1,0:T(8,128)(2,1)}, bf16[2,384,512]{2,1,0:T(8,128)(2,1)}, u32[]{:S(2)}, u32[]{:S(2)}) %collective-permute-start.23) | collective-permute-done | bytes 786464 | tf_op jit(solution)/shard_map/ppermute | solution.py:42
  230.6 15.2 %collective-permute-done.24.refs_11_ = bf16[2,384,512]{2,1,0:T(8,128)(2,1)} collective-permute-done((bf16[2,384,512]{2,1,0:T(8,128)(2,1)}, bf16[2,384,512]{2,1,0:T(8,128)(2,1)}, u32[]{:S(2)}, u32[]{:S(2)}) %collective-permute-start.24) | collective-permute-done | bytes 786464 | tf_op jit(solution)/shard_map/ppermute | solution.py:42
  245.7 2.8 collective-permute-start.34
  248.5 1.4 add_convert_fusion.4
  250.0 2.0 add_convert_fusion
  252.0 2.4 slice_add_fusion.6
  254.3 2.6 collective-permute-start.28
  258.5 6.2 %shard_map.349 = (bf16[8,192,256]{2,1,0:T(8,128)(2,1)}, bf16[8,192,256]{2,1,0:T(8,128)(2,1)}, bf16[8,192,256]{2,1,0:T(8,128)(2,1)}, bf16[8,192,256]{2,1,0:T(8,128)(2,1)}) custom-call(s32[2]{0:T(128)} %pad_add_fusion.2.me_ref, bf16[256,1024]{1,0:T(8,128)(2,1)} %copy-done.60, bf16[256,4096]{1,0:T(8,128)(2,1)} %collective-permute-done.14.refs_3_.refs_1_, ...), custom_call_target="tpu_custom_call" | custom-call | flops 1 | bytes 1 | tf_op jit(solution)/shard_map/pallas_call | solution.py:117
  265.0 1.6 slice_add_fusion.11
  266.9 9.6 %collective-permute-done.28.refs_2_ = bf16[1,1056,256]{2,1,0:T(8,128)(2,1)S(1)} collective-permute-done((bf16[1,1056,256]{2,1,0:T(8,128)(2,1)}, bf16[1,1056,256]{2,1,0:T(8,128)(2,1)S(1)}, u32[]{:S(2)}, u32[]{:S(2)}) %collective-permute-start.28) | collective-permute-done | bytes 540704 | tf_op jit(solution)/shard_map/ppermute | solution.py:42
  276.5 1.6 copy-done.42
  278.1 1.2 copy-done.48
  280.4 1.5 shard_map.350
  282.1 1.3 slice_add_fusion.12
  283.5 1.8 collective-permute-start.36
  286.5 8.4 %collective-permute-done.36 = bf16[4,192,256]{2,1,0:T(8,128)(2,1)S(1)} collective-permute-done((bf16[4,192,256]{2,1,0:T(8,128)(2,1)S(1)}, bf16[4,192,256]{2,1,0:T(8,128)(2,1)S(1)}, u32[]{:S(2)}, u32[]{:S(2)}) %collective-permute-start.36) | collective-permute-done | bytes 393248 | tf_op jit(solution)/shard_map/ppermute | solution.py:42
  294.9 1.5 collective-permute-done.37
  298.7 1.3 collective-permute-start.42
  300.0 1.8 collective-permute-done.38
  301.9 2.0 collective-permute-start.39
  303.9 2.8 collective-permute-done.40
  307.2 1.9 collective-permute-done.42
  312.3 2.6 collective-permute-start.48
  314.9 1.5 collective-permute-start.44
  316.4 4.4 %collective-permute-done.45 = bf16[2,384,256]{2,1,0:T(8,128)(2,1)S(1)} collective-permute-done((bf16[2,384,256]{2,1,0:T(8,128)(2,1)S(1)}, bf16[2,384,256]{2,1,0:T(8,128)(2,1)S(1)}, u32[]{:S(2)}, u32[]{:S(2)}) %collective-permute-start.45) | collective-permute-done | bytes 393248 | tf_op jit(solution)/shard_map/ppermute | solution.py:42
  321.0 3.1 collective-permute-start.46
  324.5 1.2 copy.89
  325.7 1.8 copy.88
  329.6 3.3 collective-permute-done.46.refs_2_
  (310 shorter events, 45.9 us)
Async XLA Ops:
  0.7 35.4 %copy-start = (bf16[1024,512]{1,0:T(8,128)(2,1)S(1)}, bf16[1024,512]{1,0:T(8,128)(2,1)}, u32[]{:S(2)}) copy-start(bf16[1024,512]{1,0:T(8,128)(2,1)} %param.35) | copy-start | bytes 3145732
  5.8 36.2 %copy-start.7 = (bf16[256,1024]{1,0:T(8,128)(2,1)}, bf16[256,1024]{1,0:T(8,128)(2,1)S(1)}, u32[]{:S(2)}) copy-start(bf16[256,1024]{1,0:T(8,128)(2,1)S(1)} %pad_maximum_fusion.8.refs_3_.refs_11_.refs_6_.refs_14_) | copy-start | bytes 1572868
  5.8 15.8 %collective-permute-start.2 = (bf16[256,1024]{1,0:T(8,128)(2,1)S(1)}, bf16[256,1024]{1,0:T(8,128)(2,1)S(1)}, u32[]{:S(2)}, u32[]{:S(2)}) collective-permute-start(bf16[256,1024]{1,0:T(8,128)(2,1)S(1)} %pad_maximum_fusion.8.refs_3_.refs_11_.refs_6_.refs_14_), channel_id=1, source_target_pairs={{0,2},{1,3},{2,0},{3,1},{4,6},{5,7},{6,4},{7,5},{8,10},{9,11},{10,... | collective-permute-start | bytes 1572872 | tf_op jit(solution)/shard_map/ppermute | solution.py:42
  8.8 24.6 %collective-permute-start.3 = (bf16[256,1024]{1,0:T(8,128)(2,1)S(1)}, bf16[256,1024]{1,0:T(8,128)(2,1)S(1)}, u32[]{:S(2)}, u32[]{:S(2)}) collective-permute-start(bf16[256,1024]{1,0:T(8,128)(2,1)S(1)} %pad_maximum_fusion.8.refs_3_.refs_11_.refs_6_.refs_14_), channel_id=1, source_target_pairs={{0,4},{1,5},{2,6},{3,7},{4,0},{5,1},{6,2},{7,3},{8,12},{9,13},{10,... | collective-permute-start | bytes 1572872 | tf_op jit(solution)/shard_map/ppermute | solution.py:42
  10.3 23.1 %collective-permute-start.4 = (bf16[256,1024]{1,0:T(8,128)(2,1)S(1)}, bf16[256,1024]{1,0:T(8,128)(2,1)S(1)}, u32[]{:S(2)}, u32[]{:S(2)}) collective-permute-start(bf16[256,1024]{1,0:T(8,128)(2,1)S(1)} %pad_maximum_fusion.8.refs_3_.refs_11_.refs_6_.refs_14_), channel_id=1, source_target_pairs={{0,6},{1,7},{2,4},{3,5},{4,2},{5,3},{6,0},{7,1},{8,14},{9,15},{10,... | collective-permute-start | bytes 1572872 | tf_op jit(solution)/shard_map/ppermute | solution.py:42
  10.4 31.6 %collective-permute-start.1 = (bf16[256,1024]{1,0:T(8,128)(2,1)S(1)}, bf16[256,1024]{1,0:T(8,128)(2,1)}, u32[]{:S(2)}, u32[]{:S(2)}) collective-permute-start(bf16[256,1024]{1,0:T(8,128)(2,1)S(1)} %pad_maximum_fusion.8.refs_3_.refs_11_.refs_6_.refs_14_), channel_id=1, source_target_pairs={{0,1},{1,0},{2,3},{3,2},{4,5},{5,4},{6,7},{7,6},{8,9},{9,8},{10,11... | collective-permute-start | bytes 1572872 | tf_op jit(solution)/shard_map/ppermute | solution.py:42
  14.5 21.8 %copy-start.65 = (bf16[128,1024]{1,0:T(8,128)(2,1)}, bf16[128,1024]{1,0:T(8,128)(2,1)S(1)}, u32[]{:S(2)}) copy-start(bf16[128,1024]{1,0:T(8,128)(2,1)S(1)} %bitcast_select_fusion.1.refs_6_) | copy-start | bytes 786436
  14.6 21.8 %copy-start.63 = (bf16[1024,512]{1,0:T(8,128)(2,1)S(1)}, bf16[1024,512]{1,0:T(8,128)(2,1)}, u32[]{:S(2)}) copy-start(bf16[1024,512]{1,0:T(8,128)(2,1)} %param.34) | copy-start | bytes 3145732
  36.0 6.0 %collective-permute-start.5 = (bf16[256,3072]{1,0:T(8,128)(2,1)S(1)}, bf16[256,3072]{1,0:T(8,128)(2,1)S(1)}, u32[]{:S(2)}, u32[]{:S(2)}) collective-permute-start(bf16[256,3072]{1,0:T(8,128)(2,1)S(1)} %pad_maximum_fusion.1), channel_id=1, source_target_pairs={{0,1},{1,0},{2,3},{3,2},{4,5},{5,4},{6,7},{7,6},{8,9},{9,8},{10,11... | collective-permute-start | bytes 4718600 | tf_op jit(solution)/shard_map/ppermute | solution.py:42
  38.4 12.4 %collective-permute-start.7 = (bf16[128,1024]{1,0:T(8,128)(2,1)S(1)}, bf16[128,1024]{1,0:T(8,128)(2,1)S(1)}, u32[]{:S(2)}, u32[]{:S(2)}) collective-permute-start(bf16[128,1024]{1,0:T(8,128)(2,1)S(1)} %pad_maximum_fusion.11.refs_2_.refs_10_.refs_6_.refs_14_), channel_id=1, source_target_pairs={{0,2},{1,3},{2,0},{3,1},{4,6},{5,7},{6,4},{7,5},{8,10},{9,11},{10,... | collective-permute-start | bytes 786440 | tf_op jit(solution)/shard_map/ppermute | solution.py:42
  39.7 12.1 %collective-permute-start.8 = (bf16[128,1024]{1,0:T(8,128)(2,1)S(1)}, bf16[128,1024]{1,0:T(8,128)(2,1)S(1)}, u32[]{:S(2)}, u32[]{:S(2)}) collective-permute-start(bf16[128,1024]{1,0:T(8,128)(2,1)S(1)} %pad_maximum_fusion.11.refs_2_.refs_10_.refs_6_.refs_14_), channel_id=1, source_target_pairs={{0,4},{1,5},{2,6},{3,7},{4,0},{5,1},{6,2},{7,3},{8,12},{9,13},{10,... | collective-permute-start | bytes 786440 | tf_op jit(solution)/shard_map/ppermute | solution.py:42
  40.5 12.9 %collective-permute-start.9 = (bf16[128,1024]{1,0:T(8,128)(2,1)S(1)}, bf16[128,1024]{1,0:T(8,128)(2,1)S(1)}, u32[]{:S(2)}, u32[]{:S(2)}) collective-permute-start(bf16[128,1024]{1,0:T(8,128)(2,1)S(1)} %pad_maximum_fusion.11.refs_2_.refs_10_.refs_6_.refs_14_), channel_id=1, source_target_pairs={{0,6},{1,7},{2,4},{3,5},{4,2},{5,3},{6,0},{7,1},{8,14},{9,15},{10,... | collective-permute-start | bytes 786440 | tf_op jit(solution)/shard_map/ppermute | solution.py:42
  54.4 7.4 %collective-permute-start.10 = (bf16[128,3072]{1,0:T(8,128)(2,1)}, bf16[128,3072]{1,0:T(8,128)(2,1)S(1)}, u32[]{:S(2)}, u32[]{:S(2)}) collective-permute-start(bf16[128,3072]{1,0:T(8,128)(2,1)} %pad_maximum_fusion.3), channel_id=1, source_target_pairs={{0,1},{1,0},{2,3},{3,2},{4,5},{5,4},{6,7},{7,6},{8,9},{9,8},{10,11... | collective-permute-start | bytes 2359304 | tf_op jit(solution)/shard_map/ppermute | solution.py:42
  55.5 16.8 %collective-permute-start = (bf16[256,512]{1,0:T(8,128)(2,1)}, bf16[256,512]{1,0:T(8,128)(2,1)}, u32[]{:S(2)}, u32[]{:S(2)}) collective-permute-start(bf16[256,512]{1,0:T(8,128)(2,1)} %get-tuple-element.309), channel_id=1, source_target_pairs={{0,1},{1,0},{2,3},{3,2},{4,5},{5,4},{6,7},{7,6},{8,9},{9,8},{10,11... | collective-permute-start | bytes 786440 | tf_op jit(solution)/shard_map/ppermute | solution.py:42
  56.8 5.0 %collective-permute-start.6 = (bf16[128,1024]{1,0:T(8,128)(2,1)}, bf16[128,1024]{1,0:T(8,128)(2,1)}, u32[]{:S(2)}, u32[]{:S(2)}) collective-permute-start(bf16[128,1024]{1,0:T(8,128)(2,1)} %copy-done.26), channel_id=1, source_target_pairs={{0,1},{1,0},{2,3},{3,2},{4,5},{5,4},{6,7},{7,6},{8,9},{9,8},{10,11... | collective-permute-start | bytes 786440 | tf_op jit(solution)/shard_map/ppermute | solution.py:42
  94.2 6.6 %collective-permute-start.12 = (bf16[256,2816]{1,0:T(8,128)(2,1)}, bf16[256,2816]{1,0:T(8,128)(2,1)}, u32[]{:S(2)}, u32[]{:S(2)}) collective-permute-start(bf16[256,2816]{1,0:T(8,128)(2,1)} %get-tuple-element.119), channel_id=1, source_target_pairs={{0,1},{1,0},{2,3},{3,2},{4,5},{5,4},{6,7},{7,6},{8,9},{9,8},{10,11... | collective-permute-start | bytes 4325384 | tf_op jit(solution)/shard_map/ppermute | solution.py:42
  94.7 6.0 %collective-permute-start.13 = (bf16[256,2816]{1,0:T(8,128)(2,1)}, bf16[256,2816]{1,0:T(8,128)(2,1)}, u32[]{:S(2)}, u32[]{:S(2)}) collective-permute-start(bf16[256,2816]{1,0:T(8,128)(2,1)} %get-tuple-element.120.refs_4_), channel_id=1, source_target_pairs={{0,1},{1,0},{2,3},{3,2},{4,5},{5,4},{6,7},{7,6},{8,9},{9,8},{10,11... | collective-permute-start | bytes 4325384 | tf_op jit(solution)/shard_map/ppermute | solution.py:42
  94.8 5.9 %collective-permute-start.11 = (bf16[256,1024]{1,0:T(8,128)(2,1)}, bf16[256,1024]{1,0:T(8,128)(2,1)}, u32[]{:S(2)}, u32[]{:S(2)}) collective-permute-start(bf16[256,1024]{1,0:T(8,128)(2,1)} %get-tuple-element.117.refs_0_), channel_id=1, source_target_pairs={{0,1},{1,0},{2,3},{3,2},{4,5},{5,4},{6,7},{7,6},{8,9},{9,8},{10,11... | collective-permute-start | bytes 1572872 | tf_op jit(solution)/shard_map/ppermute | solution.py:42
  112.9 55.0 %collective-permute-start.16 = (bf16[8,560,256]{2,1,0:T(8,128)(2,1)}, bf16[8,560,256]{2,1,0:T(8,128)(2,1)}, u32[]{:S(2)}, u32[]{:S(2)}) collective-permute-start(bf16[8,560,256]{2,1,0:T(8,128)(2,1)} %get-tuple-element.135), channel_id=1, source_target_pairs={{0,4},{1,5},{2,6},{3,7},{4,0},{5,1},{6,2},{7,3},{8,12},{9,13},{10,... | collective-permute-start | bytes 6881288 | tf_op jit(solution)/shard_map/ppermute | solution.py:42
  120.2 46.8 %collective-permute-start.14 = (bf16[256,4096]{1,0:T(8,128)(2,1)}, bf16[256,4096]{1,0:T(8,128)(2,1)}, u32[]{:S(2)}, u32[]{:S(2)}) collective-permute-start(bf16[256,4096]{1,0:T(8,128)(2,1)} %pad_maximum_fusion), channel_id=1, source_target_pairs={{0,1},{1,0},{2,3},{3,2},{4,5},{5,4},{6,7},{7,6},{8,9},{9,8},{10,11... | collective-permute-start | bytes 6291464 | tf_op jit(solution)/shard_map/ppermute | solution.py:42
  120.3 46.7 %collective-permute-start.15 = (bf16[8,496,256]{2,1,0:T(8,128)(2,1)S(1)}, bf16[8,496,256]{2,1,0:T(8,128)(2,1)}, u32[]{:S(2)}, u32[]{:S(2)}) collective-permute-start(bf16[8,496,256]{2,1,0:T(8,128)(2,1)S(1)} %copy-done.43), channel_id=1, source_target_pairs={{0,2},{1,3},{2,0},{3,1},{4,6},{5,7},{6,4},{7,5},{8,10},{9,11},{10,... | collective-permute-start | bytes 6094856 | tf_op jit(solution)/shard_map/ppermute | solution.py:42
  131.6 43.7 %copy-start.46 = (bf16[8,128,512]{2,1,0:T(8,128)(2,1)}, bf16[8,128,512]{2,1,0:T(8,128)(2,1)S(1)}, u32[]{:S(2)}) copy-start(bf16[8,128,512]{2,1,0:T(8,128)(2,1)S(1)} %get-tuple-element.140) | copy-start | bytes 3145732
  134.5 19.5 %copy-start.49 = (bf16[256,1536]{1,0:T(8,128)(2,1)}, bf16[256,1536]{1,0:T(8,128)(2,1)S(1)}, u32[]{:S(2)}) copy-start(bf16[256,1536]{1,0:T(8,128)(2,1)S(1)} %get-tuple-element.146.refs_4_) | copy-start | bytes 2359300
  134.5 19.6 %collective-permute-start.17 = (bf16[256,1536]{1,0:T(8,128)(2,1)S(1)}, bf16[256,1536]{1,0:T(8,128)(2,1)S(1)}, u32[]{:S(2)}, u32[]{:S(2)}) collective-permute-start(bf16[256,1536]{1,0:T(8,128)(2,1)S(1)} %get-tuple-element.136), channel_id=1, source_target_pairs={{0,1},{1,0},{2,3},{3,2},{4,5},{5,4},{6,7},{7,6},{8,9},{9,8},{10,11... | collective-permute-start | bytes 2359304 | tf_op jit(solution)/shard_map/ppermute | solution.py:42
  134.9 40.4 %collective-permute-start.20 = (bf16[8,128,512]{2,1,0:T(8,128)(2,1)}, bf16[8,128,512]{2,1,0:T(8,128)(2,1)S(1)}, u32[]{:S(2)}, u32[]{:S(2)}) collective-permute-start(bf16[8,128,512]{2,1,0:T(8,128)(2,1)} %get-tuple-element.141), channel_id=1, source_target_pairs={{0,1},{1,0},{2,3},{3,2},{4,5},{5,4},{6,7},{7,6},{8,9},{9,8},{10,11... | collective-permute-start | bytes 3145736 | tf_op jit(solution)/shard_map/ppermute | solution.py:42
  135.1 32.8 %copy-start.72 = (bf16[8,496,256]{2,1,0:T(8,128)(2,1)S(1)}, bf16[8,496,256]{2,1,0:T(8,128)(2,1)}, u32[]{:S(2)}) copy-start(bf16[8,496,256]{2,1,0:T(8,128)(2,1)} %get-tuple-element.142) | copy-start | bytes 6094852
  154.1 16.6 %copy-start.39 = (bf16[8,256,512]{2,1,0:T(8,128)(2,1)}, bf16[8,256,512]{2,1,0:T(8,128)(2,1)S(1)}, u32[]{:S(2)}) copy-start(bf16[8,256,512]{2,1,0:T(8,128)(2,1)S(1)} %get-tuple-element.138) | copy-start | bytes 6291460
  154.1 16.6 %copy-start.58 = (f32[2,8,1280]{2,1,0:T(8,128)}, f32[2,8,1280]{2,1,0:T(8,128)S(1)}, u32[]{:S(2)}) copy-start(f32[2,8,1280]{2,1,0:T(8,128)S(1)} %get-tuple-element.161) | copy-start | bytes 245764
  154.1 22.4 %copy-start.20 = (bf16[256,1024]{1,0:T(8,128)(2,1)}, bf16[256,1024]{1,0:T(8,128)(2,1)S(1)}, u32[]{:S(2)}) copy-start(bf16[256,1024]{1,0:T(8,128)(2,1)S(1)} %get-tuple-element.137.refs_6_.refs_3_) | copy-start | bytes 1572868
  154.1 16.6 %copy-start.81 = (bf16[256,1536]{1,0:T(8,128)(2,1)}, bf16[256,1536]{1,0:T(8,128)(2,1)S(1)}, u32[]{:S(2)}) copy-start(bf16[256,1536]{1,0:T(8,128)(2,1)S(1)} %collective-permute-done.17.refs_5_) | copy-start | bytes 2359300
  167.8 37.4 %collective-permute-start.19 = (bf16[8,256,512]{2,1,0:T(8,128)(2,1)}, bf16[8,256,512]{2,1,0:T(8,128)(2,1)}, u32[]{:S(2)}, u32[]{:S(2)}) collective-permute-start(bf16[8,256,512]{2,1,0:T(8,128)(2,1)} %get-tuple-element.139), channel_id=1, source_target_pairs={{0,1},{1,0},{2,3},{3,2},{4,5},{5,4},{6,7},{7,6},{8,9},{9,8},{10,11... | collective-permute-start | bytes 6291464 | tf_op jit(solution)/shard_map/ppermute | solution.py:42
  173.6 25.2 %collective-permute-start.21 = (bf16[4,496,256]{2,1,0:T(8,128)(2,1)}, bf16[4,496,256]{2,1,0:T(8,128)(2,1)}, u32[]{:S(2)}, u32[]{:S(2)}) collective-permute-start(bf16[4,496,256]{2,1,0:T(8,128)(2,1)} %get-tuple-element.144), channel_id=1, source_target_pairs={{0,4},{1,5},{2,6},{3,7},{4,0},{5,1},{6,2},{7,3},{8,12},{9,13},{10,... | collective-permute-start | bytes 3047432 | tf_op jit(solution)/shard_map/ppermute | solution.py:42
  175.3 27.5 %collective-permute-start.22 = (bf16[4,560,256]{2,1,0:T(8,128)(2,1)S(1)}, bf16[4,560,256]{2,1,0:T(8,128)(2,1)}, u32[]{:S(2)}, u32[]{:S(2)}) collective-permute-start(bf16[4,560,256]{2,1,0:T(8,128)(2,1)S(1)} %get-tuple-element.145), channel_id=1, source_target_pairs={{0,2},{1,3},{2,0},{3,1},{4,6},{5,7},{6,4},{7,5},{8,10},{9,11},{10,... | collective-permute-start | bytes 3440648 | tf_op jit(solution)/shard_map/ppermute | solution.py:42
  177.3 32.1 %collective-permute-start.18 = (bf16[256,512]{1,0:T(8,128)(2,1)}, bf16[256,512]{1,0:T(8,128)(2,1)}, u32[]{:S(2)}, u32[]{:S(2)}) collective-permute-start(bf16[256,512]{1,0:T(8,128)(2,1)} %get-tuple-element.306), channel_id=1, source_target_pairs={{0,1},{1,0},{2,3},{3,2},{4,5},{5,4},{6,7},{7,6},{8,9},{9,8},{10,11... | collective-permute-start | bytes 786440 | tf_op jit(solution)/shard_map/ppermute | solution.py:42
  183.8 19.0 %copy-start.62 = (bf16[4,560,256]{2,1,0:T(8,128)(2,1)S(1)}, bf16[4,560,256]{2,1,0:T(8,128)(2,1)}, u32[]{:S(2)}) copy-start(bf16[4,560,256]{2,1,0:T(8,128)(2,1)} %get-tuple-element.268) | copy-start | bytes 3440644
  209.4 20.9 %collective-permute-start.23 = (bf16[2,384,512]{2,1,0:T(8,128)(2,1)}, bf16[2,384,512]{2,1,0:T(8,128)(2,1)}, u32[]{:S(2)}, u32[]{:S(2)}) collective-permute-start(bf16[2,384,512]{2,1,0:T(8,128)(2,1)} %get-tuple-element.148), channel_id=1, source_target_pairs={{0,2},{1,3},{2,0},{3,1},{4,6},{5,7},{6,4},{7,5},{8,10},{9,11},{10,... | collective-permute-start | bytes 2359304 | tf_op jit(solution)/shard_map/ppermute | solution.py:42
  209.8 36.0 %collective-permute-start.24 = (bf16[2,384,512]{2,1,0:T(8,128)(2,1)}, bf16[2,384,512]{2,1,0:T(8,128)(2,1)}, u32[]{:S(2)}, u32[]{:S(2)}) collective-permute-start(bf16[2,384,512]{2,1,0:T(8,128)(2,1)} %get-tuple-element.149), channel_id=1, source_target_pairs={{0,4},{1,5},{2,6},{3,7},{4,0},{5,1},{6,2},{7,3},{8,12},{9,13},{10,... | collective-permute-start | bytes 2359304 | tf_op jit(solution)/shard_map/ppermute | solution.py:42
  210.0 38.5 %collective-permute-start.25 = (bf16[2,384,512]{2,1,0:T(8,128)(2,1)}, bf16[2,384,512]{2,1,0:T(8,128)(2,1)}, u32[]{:S(2)}, u32[]{:S(2)}) collective-permute-start(bf16[2,384,512]{2,1,0:T(8,128)(2,1)} %pad_maximum_fusion.6), channel_id=1, source_target_pairs={{0,6},{1,7},{2,4},{3,5},{4,2},{5,3},{6,0},{7,1},{8,14},{9,15},{10,... | collective-permute-start | bytes 2359304 | tf_op jit(solution)/shard_map/ppermute | solution.py:42
  214.0 37.9 %collective-permute-start.27 = (bf16[2,1056,256]{2,1,0:T(8,128)(2,1)}, bf16[2,1056,256]{2,1,0:T(8,128)(2,1)}, u32[]{:S(2)}, u32[]{:S(2)}) collective-permute-start(bf16[2,1056,256]{2,1,0:T(8,128)(2,1)} %pad_maximum_fusion.2), channel_id=1, source_target_pairs={{0,8},{8,0},{16,24},{24,16},{1,9},{9,1},{17,25},{25,17},{2,10},{10... | collective-permute-start | bytes 3244040 | tf_op jit(solution)/shard_map/ppermute | solution.py:42
  215.6 42.9 %collective-permute-start.26 = (bf16[128,1024]{1,0:T(8,128)(2,1)S(1)}, bf16[128,1024]{1,0:T(8,128)(2,1)}, u32[]{:S(2)}, u32[]{:S(2)}) collective-permute-start(bf16[128,1024]{1,0:T(8,128)(2,1)S(1)} %copy-done.66), channel_id=1, source_target_pairs={{0,1},{1,0},{2,3},{3,2},{4,5},{5,4},{6,7},{7,6},{8,9},{9,8},{10,11... | collective-permute-start | bytes 786440 | tf_op jit(solution)/shard_map/ppermute | solution.py:42
  230.3 34.7 %collective-permute-start.35 = (bf16[8,192,256]{2,1,0:T(8,128)(2,1)}, bf16[8,192,256]{2,1,0:T(8,128)(2,1)}, u32[]{:S(2)}, u32[]{:S(2)}) collective-permute-start(bf16[8,192,256]{2,1,0:T(8,128)(2,1)} %get-tuple-element.167), channel_id=1, source_target_pairs={{0,4},{1,5},{2,6},{3,7},{4,0},{5,1},{6,2},{7,3},{8,12},{9,13},{10,... | collective-permute-start | bytes 2359304 | tf_op jit(solution)/shard_map/ppermute | solution.py:42
  245.7 36.3 %collective-permute-start.34 = (bf16[8,192,256]{2,1,0:T(8,128)(2,1)}, bf16[8,192,256]{2,1,0:T(8,128)(2,1)}, u32[]{:S(2)}, u32[]{:S(2)}) collective-permute-start(bf16[8,192,256]{2,1,0:T(8,128)(2,1)} %get-tuple-element.165), channel_id=1, source_target_pairs={{0,2},{1,3},{2,0},{3,1},{4,6},{5,7},{6,4},{7,5},{8,10},{9,11},{10,... | collective-permute-start | bytes 2359304 | tf_op jit(solution)/shard_map/ppermute | solution.py:42
  254.3 22.1 %collective-permute-start.28 = (bf16[1,1056,256]{2,1,0:T(8,128)(2,1)}, bf16[1,1056,256]{2,1,0:T(8,128)(2,1)S(1)}, u32[]{:S(2)}, u32[]{:S(2)}) collective-permute-start(bf16[1,1056,256]{2,1,0:T(8,128)(2,1)} %get-tuple-element.153), channel_id=1, source_target_pairs={{0,16},{8,24},{16,0},{24,8},{1,17},{9,25},{17,1},{25,9},{2,18},{10... | collective-permute-start | bytes 1622024 | tf_op jit(solution)/shard_map/ppermute | solution.py:42
  258.5 18.0 %copy-start.25 = (bf16[1024,512]{1,0:T(8,128)(2,1)S(1)}, bf16[1024,512]{1,0:T(8,128)(2,1)}, u32[]{:S(2)}) copy-start(bf16[1024,512]{1,0:T(8,128)(2,1)} %refs_7_.3) | copy-start | bytes 3145732
  264.7 2.2 collective-permute-start.29
  264.8 21.5 %collective-permute-start.33 = (bf16[8,192,256]{2,1,0:T(8,128)(2,1)}, bf16[8,192,256]{2,1,0:T(8,128)(2,1)S(1)}, u32[]{:S(2)}, u32[]{:S(2)}) collective-permute-start(bf16[8,192,256]{2,1,0:T(8,128)(2,1)} %get-tuple-element.162), channel_id=1, source_target_pairs={{0,4},{1,5},{2,6},{3,7},{4,0},{5,1},{6,2},{7,3},{8,12},{9,13},{10,... | collective-permute-start | bytes 2359304 | tf_op jit(solution)/shard_map/ppermute | solution.py:42
  266.6 19.9 %collective-permute-start.32 = (bf16[8,192,256]{2,1,0:T(8,128)(2,1)}, bf16[8,192,256]{2,1,0:T(8,128)(2,1)S(1)}, u32[]{:S(2)}, u32[]{:S(2)}) collective-permute-start(bf16[8,192,256]{2,1,0:T(8,128)(2,1)} %get-tuple-element.152.refs_1_), channel_id=1, source_target_pairs={{0,2},{1,3},{2,0},{3,1},{4,6},{5,7},{6,4},{7,5},{8,10},{9,11},{10,... | collective-permute-start | bytes 2359304 | tf_op jit(solution)/shard_map/ppermute | solution.py:42
  282.0 4.2 %collective-permute-start.31 = (f32[28,128]{1,0:T(8,128)S(1)}, f32[28,128]{1,0:T(8,128)S(1)}, u32[]{:S(2)}, u32[]{:S(2)}) collective-permute-start(f32[28,128]{1,0:T(8,128)S(1)} %maximum_bitcast_fusion), channel_id=1, source_target_pairs={{0,1},{1,0},{2,3},{3,2},{4,5},{5,4},{6,7},{7,6},{8,9},{9,8},{10,11... | collective-permute-start | bytes 43016 | tf_op jit(solution)/shard_map/ppermute | solution.py:42
  283.5 11.5 %collective-permute-start.36 = (bf16[4,192,256]{2,1,0:T(8,128)(2,1)S(1)}, bf16[4,192,256]{2,1,0:T(8,128)(2,1)S(1)}, u32[]{:S(2)}, u32[]{:S(2)}) collective-permute-start(bf16[4,192,256]{2,1,0:T(8,128)(2,1)S(1)} %get-tuple-element.168), channel_id=1, source_target_pairs={{0,4},{1,5},{2,6},{3,7},{4,0},{5,1},{6,2},{7,3},{8,12},{9,13},{10,... | collective-permute-start | bytes 1179656 | tf_op jit(solution)/shard_map/ppermute | solution.py:42
  285.3 11.1 %collective-permute-start.37 = (bf16[4,192,256]{2,1,0:T(8,128)(2,1)S(1)}, bf16[4,192,256]{2,1,0:T(8,128)(2,1)S(1)}, u32[]{:S(2)}, u32[]{:S(2)}) collective-permute-start(bf16[4,192,256]{2,1,0:T(8,128)(2,1)S(1)} %get-tuple-element.169), channel_id=1, source_target_pairs={{0,2},{1,3},{2,0},{3,1},{4,6},{5,7},{6,4},{7,5},{8,10},{9,11},{10,... | collective-permute-start | bytes 1179656 | tf_op jit(solution)/shard_map/ppermute | solution.py:42
  286.2 23.8 %collective-permute-start.30 = (bf16[128,512]{1,0:T(8,128)(2,1)S(1)}, bf16[128,512]{1,0:T(8,128)(2,1)S(1)}, u32[]{:S(2)}, u32[]{:S(2)}) collective-permute-start(bf16[128,512]{1,0:T(8,128)(2,1)S(1)} %copy-done.82), channel_id=1, source_target_pairs={{0,1},{1,0},{2,3},{3,2},{4,5},{5,4},{6,7},{7,6},{8,9},{9,8},{10,11... | collective-permute-start | bytes 393224 | tf_op jit(solution)/shard_map/ppermute | solution.py:42
  296.4 10.3 %collective-permute-start.40 = (bf16[4,192,256]{2,1,0:T(8,128)(2,1)S(1)}, bf16[4,192,256]{2,1,0:T(8,128)(2,1)S(1)}, u32[]{:S(2)}, u32[]{:S(2)}) collective-permute-start(bf16[4,192,256]{2,1,0:T(8,128)(2,1)S(1)} %get-tuple-element.173), channel_id=1, source_target_pairs={{0,4},{1,5},{2,6},{3,7},{4,0},{5,1},{6,2},{7,3},{8,12},{9,13},{10,... | collective-permute-start | bytes 1179656 | tf_op jit(solution)/shard_map/ppermute | solution.py:42
  296.8 10.3 %collective-permute-start.41 = (bf16[4,192,256]{2,1,0:T(8,128)(2,1)S(1)}, bf16[4,192,256]{2,1,0:T(8,128)(2,1)S(1)}, u32[]{:S(2)}, u32[]{:S(2)}) collective-permute-start(bf16[4,192,256]{2,1,0:T(8,128)(2,1)S(1)} %get-tuple-element.174), channel_id=1, source_target_pairs={{0,2},{1,3},{2,0},{3,1},{4,6},{5,7},{6,4},{7,5},{8,10},{9,11},{10,... | collective-permute-start | bytes 1179656 | tf_op jit(solution)/shard_map/ppermute | solution.py:42
  297.8 4.0 %collective-permute-start.38 = (f32[28,128]{1,0:T(8,128)S(1)}, f32[28,128]{1,0:T(8,128)S(1)}, u32[]{:S(2)}, u32[]{:S(2)}) collective-permute-start(f32[28,128]{1,0:T(8,128)S(1)} %fusion.17), channel_id=1, source_target_pairs={{0,8},{8,0},{16,24},{24,16},{1,9},{9,1},{17,25},{25,17},{2,10},{10... | collective-permute-start | bytes 43016 | tf_op jit(solution)/shard_map/ppermute | solution.py:42
  298.7 10.3 %collective-permute-start.42 = (bf16[2,384,256]{2,1,0:T(8,128)(2,1)S(1)}, bf16[2,384,256]{2,1,0:T(8,128)(2,1)S(1)}, u32[]{:S(2)}, u32[]{:S(2)}) collective-permute-start(bf16[2,384,256]{2,1,0:T(8,128)(2,1)S(1)} %pad_maximum_fusion.9), channel_id=1, source_target_pairs={{0,8},{8,0},{16,24},{24,16},{1,9},{9,1},{17,25},{25,17},{2,10},{10... | collective-permute-start | bytes 1179656 | tf_op jit(solution)/shard_map/ppermute | solution.py:42
  301.9 9.1 %collective-permute-start.39 = (f32[28,128]{1,0:T(8,128)S(1)}, f32[28,128]{1,0:T(8,128)S(1)}, u32[]{:S(2)}, u32[]{:S(2)}) collective-permute-start(f32[28,128]{1,0:T(8,128)S(1)} %add.231), channel_id=1, source_target_pairs={{0,16},{8,24},{16,0},{24,8},{1,17},{9,25},{17,1},{25,9},{2,18},{10... | collective-permute-start | bytes 43016 | tf_op jit(solution)/shard_map/ppermute | solution.py:42
  309.0 11.9 %collective-permute-start.45 = (bf16[2,384,256]{2,1,0:T(8,128)(2,1)S(1)}, bf16[2,384,256]{2,1,0:T(8,128)(2,1)S(1)}, u32[]{:S(2)}, u32[]{:S(2)}) collective-permute-start(bf16[2,384,256]{2,1,0:T(8,128)(2,1)S(1)} %pad_maximum_fusion.10), channel_id=1, source_target_pairs={{0,8},{8,0},{16,24},{24,16},{1,9},{9,1},{17,25},{25,17},{2,10},{10... | collective-permute-start | bytes 1179656 | tf_op jit(solution)/shard_map/ppermute | solution.py:42
  310.9 16.6 %collective-permute-start.50 = (bf16[528,256]{1,0:T(8,128)(2,1)S(1)}, bf16[528,256]{1,0:T(8,128)(2,1)S(1)}, u32[]{:S(2)}, u32[]{:S(2)}) collective-permute-start(bf16[528,256]{1,0:T(8,128)(2,1)S(1)} %get-tuple-element.192), channel_id=1, source_target_pairs={{0,1},{1,0},{2,3},{3,2},{4,5},{5,4},{6,7},{7,6},{8,9},{9,8},{10,11... | collective-permute-start | bytes 811016 | tf_op jit(solution)/shard_map/ppermute | solution.py:42
  311.0 3.9 %collective-permute-start.43 = (f32[28,128]{1,0:T(8,128)S(1)}, f32[28,128]{1,0:T(8,128)S(1)}, u32[]{:S(2)}, u32[]{:S(2)}) collective-permute-start(f32[28,128]{1,0:T(8,128)S(1)} %add.232), channel_id=1, source_target_pairs={{0,2},{1,3},{2,0},{3,1},{4,6},{5,7},{6,4},{7,5},{8,10},{9,11},{10,... | collective-permute-start | bytes 43016 | tf_op jit(solution)/shard_map/ppermute | solution.py:42
  312.3 17.2 %collective-permute-start.48 = (bf16[1,384,256]{2,1,0:T(8,128)(2,1)S(1)}, bf16[1,384,256]{2,1,0:T(8,128)(2,1)S(1)}, u32[]{:S(2)}, u32[]{:S(2)}) collective-permute-start(bf16[1,384,256]{2,1,0:T(8,128)(2,1)S(1)} %get-tuple-element.183), channel_id=1, source_target_pairs={{0,16},{8,24},{16,0},{24,8},{1,17},{9,25},{17,1},{25,9},{2,18},{10... | collective-permute-start | bytes 589832 | tf_op jit(solution)/shard_map/ppermute | solution.py:42
  314.9 13.6 %collective-permute-start.44 = (f32[28,128]{1,0:T(8,128)S(1)}, f32[28,128]{1,0:T(8,128)S(1)}, u32[]{:S(2)}, u32[]{:S(2)}) collective-permute-start(f32[28,128]{1,0:T(8,128)S(1)} %add.239), channel_id=1, source_target_pairs={{0,4},{1,5},{2,6},{3,7},{4,0},{5,1},{6,2},{7,3},{8,12},{9,13},{10,... | collective-permute-start | bytes 43016 | tf_op jit(solution)/shard_map/ppermute | solution.py:42
  321.0 12.0 %collective-permute-start.46 = (bf16[1,384,256]{2,1,0:T(8,128)(2,1)S(1)}, bf16[1,384,256]{2,1,0:T(8,128)(2,1)S(1)}, u32[]{:S(2)}, u32[]{:S(2)}) collective-permute-start(bf16[1,384,256]{2,1,0:T(8,128)(2,1)S(1)} %get-tuple-element.298), channel_id=1, source_target_pairs={{0,16},{8,24},{16,0},{24,8},{1,17},{9,25},{17,1},{25,9},{2,18},{10... | collective-permute-start | bytes 589832 | tf_op jit(solution)/shard_map/ppermute | solution.py:42
  329.5 4.9 %collective-permute-start.49 = (bf16[192,256]{1,0:T(8,128)(2,1)S(1)}, bf16[192,256]{1,0:T(8,128)(2,1)S(1)}, u32[]{:S(2)}, u32[]{:S(2)}) collective-permute-start(bf16[192,256]{1,0:T(8,128)(2,1)S(1)} %get-tuple-element.185), channel_id=1, source_target_pairs={{0,1},{1,0},{2,3},{3,2},{4,5},{5,4},{6,7},{7,6},{8,9},{9,8},{10,11... | collective-permute-start | bytes 294920 | tf_op jit(solution)/shard_map/ppermute | solution.py:42
  333.0 2.2 collective-permute-start.47
  (76 other events, 324.5 us)
